TPU v7x, 32 devices: a whole 2x2x4 slice. The times are simulated.
32 devices in a mesh: dp: 4 (over z), loop: 8 (over y, x, core).
Axes of the slice: x: 2, y: 2, z: 4, core: 2. Of those that a mesh axis runs over, the one named last changes fastest.
Arguments:
- tokens: bfloat16 [8192, 2048], P('loop', 'dp'), may hold values from -6 to 6
- cotangent: bfloat16 [8192, 2048], P('loop', 'dp'), may hold values from -6 to 6
- up_first: bfloat16 [128, 16, 128], P('loop'), may hold values from -0.5 to 0.5
- up_second: bfloat16 [16, 128, 128], P('loop'), may hold values from -0.5 to 0.5
- down_first: bfloat16 [16, 128, 128], P('loop'), may hold values from -0.5 to 0.5
- down_second: bfloat16 [128, 16, 128], P('loop'), may hold values from -1 to 1
- perm_up: int32 [128], replicated, may hold values from 0 to 127, each once
- perm_down: int32 [128], replicated, may hold values from 0 to 127, each once
Outputs:
- mixed: bfloat16 [8192, 2048], P('loop', 'dp')
- grad_tokens: bfloat16 [8192, 2048], P('loop', 'dp')
- grad_up_first: float32 [128, 16, 128], P('loop')
- grad_up_second: float32 [16, 128, 128], P('loop')
- grad_down_first: float32 [16, 128, 128], P('loop')
- grad_down_second: float32 [128, 16, 128], P('loop')
Inputs may be any that keep to these rules, and one draw needn't show every extreme that they name: perm_up holds each of 0 to 127 once. perm_down holds each of 0 to 127 once.
All inputs are finite; a program needn't handle non-finite values.
Results may differ from a plain program's by a relative error of at most 0.01.
Values may be sent and summed in bfloat16 or wider, within the bound.
No kernel may reach another device: no remote copies, remote signals or barrier semaphores. Data moves between devices by JAX's collectives and lax.ppermute only.
A program may use at most 64 MiB of HBM per device.

v0:
```python
import math

import jax
import jax.numpy as jnp
from jax import lax
from jax.sharding import PartitionSpec as P


def from_partner(value, axis, apart):
    mask = 2**apart
    pairs = [(source, source ^ mask) for source in range(lax.axis_size(axis))]
    return lax.ppermute(value, axis, pairs)


def gelu_parts(pre_act):
    cumul = 0.5 * (1.0 + jax.scipy.special.erf(pre_act * (1.0 / math.sqrt(2.0))))
    slope = cumul + pre_act * jnp.exp(-0.5 * pre_act * pre_act) * (1.0 / math.sqrt(2.0 * math.pi))
    return (pre_act * cumul, slope)


def inverse_of(permute):
    return (
        jnp.zeros(permute.shape, jnp.int32)
        .at[permute]
        .set(jnp.arange(permute.shape[0], dtype=jnp.int32))
    )


def pair_total(contrib, half_width, parity):
    pair_blocks = contrib.shape[0]
    tok_count = contrib.shape[2]
    leaving = lax.dynamic_slice_in_dim(contrib, (1 - parity) * half_width, half_width, 1)
    other = from_partner(leaving.astype(jnp.bfloat16), "loop", 0).astype(leaving.dtype)
    mine = lax.dynamic_slice_in_dim(contrib, parity * half_width, half_width, 1) + other
    return mine.reshape(pair_blocks * half_width, tok_count)


def shards(tokens, cotangent, up_first, up_second, down_first, down_second, perm_up, perm_down):
    wide = jnp.float32
    narrow = jnp.bfloat16
    feature_rows = tokens.shape[0]
    tok_count = tokens.shape[1]
    local_rows = up_first.shape[0]
    block = up_first.shape[2]
    half_width = block // 2
    pair_blocks = 2 * feature_rows // block
    group = 2 * local_rows // pair_blocks
    parity = lax.axis_index("loop") % 2
    other_x, other_d = from_partner((tokens, cotangent), "loop", 0)
    low_x = jnp.where(parity == 0, tokens, other_x)
    high_x = jnp.where(parity == 0, other_x, tokens)
    low_d = jnp.where(parity == 0, cotangent, other_d)
    high_d = jnp.where(parity == 0, other_d, cotangent)
    x_blocks = jnp.concatenate(
        [
            low_x.reshape(pair_blocks, half_width, tok_count),
            high_x.reshape(pair_blocks, half_width, tok_count),
        ],
        1,
    )
    d_blocks = jnp.concatenate(
        [
            low_d.reshape(pair_blocks, half_width, tok_count),
            high_d.reshape(pair_blocks, half_width, tok_count),
        ],
        1,
    )
    row_block = (parity * local_rows + jnp.arange(local_rows, dtype=jnp.int32)) // group
    picker = row_block[:, None] == jnp.arange(pair_blocks, dtype=jnp.int32)[None, :]
    picker_narrow = picker.astype(narrow)
    picker_wide = picker.astype(wide)
    x_rows = jnp.einsum("am,mit->ait", picker_narrow, x_blocks, preferred_element_type=wide).astype(
        narrow
    )
    d_rows = jnp.einsum("am,mit->ait", picker_narrow, d_blocks, preferred_element_type=wide).astype(
        narrow
    )
    inverse_up = inverse_of(perm_up)
    inverse_down = inverse_of(perm_down)
    hidden_one = jnp.einsum("abi,ait->abt", up_first, x_rows, preferred_element_type=wide).astype(
        narrow
    )
    permuted = jnp.take(
        lax.all_to_all(hidden_one, "loop", split_axis=1, concat_axis=0, tiled=True), perm_up, axis=0
    )
    pre_act = jnp.einsum("boa,abt->bot", up_second, permuted, preferred_element_type=wide)
    gelu_val, slope = gelu_parts(pre_act)
    activated = gelu_val.astype(narrow)
    mixed_cols = jnp.einsum(
        "bpo,bot->pbt", down_first, activated, preferred_element_type=wide
    ).astype(narrow)
    leaving = jnp.take(mixed_cols, perm_down, axis=0)
    back_rows = lax.all_to_all(leaving, "loop", split_axis=0, concat_axis=1, tiled=True)
    back_rows, permuted, activated, slope = (back_rows, permuted, activated, slope)
    out_rows = jnp.einsum("abo,abt->aot", down_second, back_rows, preferred_element_type=wide)
    out_contrib = jnp.einsum("am,aot->mot", picker_wide, out_rows, precision=lax.Precision.HIGHEST)
    branch_out = pair_total(out_contrib, half_width, parity)
    mixed = (tokens.astype(wide) + branch_out).astype(narrow)
    scale = 1.0 / math.sqrt(lax.axis_size("dp") * tok_count)
    grad_rows = jnp.einsum("abo,aot->abt", down_second, d_rows, preferred_element_type=wide).astype(
        narrow
    )
    g_down_second = jnp.einsum("abt,aot->abo", back_rows, d_rows, preferred_element_type=wide)
    grad_cols = lax.all_to_all(grad_rows, "loop", split_axis=1, concat_axis=0, tiled=True)
    grad_mixed = jnp.take(grad_cols, inverse_down, axis=0)
    grad_act = jnp.einsum("bpo,pbt->bot", down_first, grad_mixed, preferred_element_type=wide)
    g_down_first = jnp.einsum("pbt,bot->bpo", grad_mixed, activated, preferred_element_type=wide)
    grad_pre = (grad_act * slope).astype(narrow)
    g_up_second = jnp.einsum("bot,abt->boa", grad_pre, permuted, preferred_element_type=wide)
    grad_perm = jnp.einsum("boa,bot->abt", up_second, grad_pre, preferred_element_type=wide).astype(
        narrow
    )
    grad_recv = jnp.take(grad_perm, inverse_up, axis=0)
    grad_hidden = lax.all_to_all(grad_recv, "loop", split_axis=0, concat_axis=1, tiled=True)
    g_up_first = jnp.einsum("abt,ait->abi", grad_hidden, x_rows, preferred_element_type=wide)
    g_up_first, g_up_second, g_down_first, g_down_second = (
        lax.psum(g_up_first.astype(jnp.bfloat16), "dp").astype(jnp.float32),
        lax.psum(g_up_second.astype(jnp.bfloat16), "dp").astype(jnp.float32),
        lax.psum(g_down_first.astype(jnp.bfloat16), "dp").astype(jnp.float32),
        lax.psum(g_down_second.astype(jnp.bfloat16), "dp").astype(jnp.float32),
    )
    grad_rows_in = jnp.einsum("abi,abt->ait", up_first, grad_hidden, preferred_element_type=wide)
    grad_contrib = jnp.einsum(
        "am,ait->mit", picker_wide, grad_rows_in, precision=lax.Precision.HIGHEST
    )
    grad_branch = pair_total(grad_contrib, half_width, parity)
    grad_tokens = (cotangent.astype(wide) + grad_branch).astype(narrow)
    return (
        mixed,
        grad_tokens,
        g_up_first * scale,
        g_up_second * scale,
        g_down_first * scale,
        g_down_second * scale,
    )


def solution(mesh):
    in_specs = (
        P("loop", "dp"),
        P("loop", "dp"),
        P("loop", None, None),
        P("loop", None, None),
        P("loop", None, None),
        P("loop", None, None),
        P(),
        P(),
    )
    out_specs = (
        P("loop", "dp"),
        P("loop", "dp"),
        P("loop", None, None),
        P("loop", None, None),
        P("loop", None, None),
        P("loop", None, None),
    )
    return jax.shard_map(shards, mesh=mesh, in_specs=in_specs, out_specs=out_specs, check_vma=False)
```

profile of v0, /device:TPU:0, one launch (start us, length us, event | category | flops | bytes accessed | tf_op | source)
XLA Modules:
  0.0 175.8 jit_solution(6444043014345857143)
XLA Ops:
  15.6 2.3 %fusion.37 = bf16[16,16,512]{2,1,0:T(8,128)(2,1)S(1)} fusion(bf16[16,16,128]{2,1,0:T(8,128)(2,1)S(1)} %copy-done, bf16[16,128,512]{2,0,1:T(8,128)(2,1)S(1)} %fusion.13), kind=kOutput, calls=%fused_computation.45 | convolution fusion | flops 33685504 | bytes 2424832 | tf_op jit(solution)/shard_map/abi,ait->abt/dot_general | solution.py:80
  18.7 5.1 %all-to-all-start = ((bf16[16,16,512]{2,0,1:T(8,128)(2,1)}), bf16[16,16,512]{2,0,1:T(8,128)(2,1)S(1)}, u32[]{:S(2)}, u32[]{:S(2)}) async-start(bf16[16,16,512]{2,0,1:T(8,128)(2,1)} %copy.88), calls=%async_computation | async-start | bytes 524288 | tf_op jit(solution)/shard_map/all_to_all | solution.py:84
  28.5 2.3 %fusion.34 = bf16[16,16,512]{2,1,0:T(8,128)(2,1)S(1)} fusion(bf16[16,16,128]{2,1,0:T(8,128)(2,1)S(1)} %copy-done.8, bf16[16,128,512]{2,0,1:T(8,128)(2,1)S(1)} %fusion.10), kind=kOutput, calls=%fused_computation.44 | convolution fusion | flops 33685504 | bytes 2424832 | tf_op jit(solution)/shard_map/abo,aot->abt/dot_general | solution.py:100
  31.7 4.2 %all-to-all-start.2 = ((bf16[16,16,512]{2,0,1:T(8,128)(2,1)}), bf16[16,16,512]{2,0,1:T(8,128)(2,1)}, u32[]{:S(2)}, u32[]{:S(2)}) async-start(bf16[16,16,512]{2,0,1:T(8,128)(2,1)} %copy.101), calls=%async_computation.2 | async-start | bytes 524288 | tf_op jit(solution)/shard_map/all_to_all | solution.py:104
  38.7 4.3 %all-to-all-done.2 = bf16[16,16,512]{2,0,1:T(8,128)(2,1)} async-done(((bf16[16,16,512]{2,0,1:T(8,128)(2,1)}), bf16[16,16,512]{2,0,1:T(8,128)(2,1)}, u32[]{:S(2)}, u32[]{:S(2)}) %all-to-all-start.2) | async-done | bytes 262176 | tf_op jit(solution)/shard_map/all_to_all | solution.py:104
  48.0 1.9 %multiply_convert_fusion = (bf16[2,128,512]{1,2,0:T(8,128)(2,1)S(1)}, f32[2,128,512]{1,2,0:T(8,128)}) fusion(bf16[2,128,128]{2,1,0:T(8,128)(2,1)} %param.13, bf16[128,2,512]{2,1,0:T(2,128)(2,1)S(1)} %broadcast_select_fusion.7), kind=kOutput, calls=%fused_computation.59 | convolution fusion | flops 34209792 | bytes 1114112 | tf_op jit(solution)/shard_map/boa,abt->bot/dot_general | solution.py:86
  52.3 2.9 %gather_fusion.2 = bf16[128,2,512]{2,1,0:T(2,128)(2,1)} fusion(bf16[128,2,512]{2,1,0:T(2,128)(2,1)} %copy.103, s32[1024]{0:T(1024)} %pad_clamp_fusion.1), kind=kCustom, calls=%fused_computation.2.clone | custom fusion | bytes 524800 | tf_op jit(solution)/shard_map/jit(_take)/gather | solution.py:105
  63.6 2.1 %gather_fusion.3 = bf16[128,2,512]{2,1,0:T(2,128)(2,1)S(1)} fusion(bf16[128,2,512]{2,1,0:T(2,128)(2,1)} %copy.105, s32[1024]{0:T(1024)S(1)} %pad_clamp_fusion), kind=kCustom, calls=%fused_computation.3.clone | custom fusion | bytes 524800 | tf_op jit(solution)/shard_map/jit(_take)/gather | solution.py:113
  66.8 4.0 %all-to-all-start.3 = ((bf16[128,2,512]{2,1,0:T(2,128)(2,1)}), bf16[128,2,512]{2,1,0:T(2,128)(2,1)}, u32[]{:S(2)}, u32[]{:S(2)}) async-start(bf16[128,2,512]{2,1,0:T(2,128)(2,1)} %broadcast_select_fusion.4), calls=%async_computation.3 | async-start | bytes 524288 | tf_op jit(solution)/shard_map/all_to_all | solution.py:114
  70.8 2.1 %gather_fusion.1 = bf16[128,2,512]{2,1,0:T(2,128)(2,1)S(1)} fusion(bf16[128,2,512]{2,1,0:T(2,128)(2,1)} %copy.92, s32[1024]{0:T(1024)S(1)} %pad_clamp_fusion.2), kind=kCustom, calls=%fused_computation.1.clone | custom fusion | bytes 524800 | tf_op jit(solution)/shard_map/jit(_take)/gather | solution.py:92
  74.6 3.2 %all-to-all-done.3 = bf16[128,2,512]{2,1,0:T(2,128)(2,1)} async-done(((bf16[128,2,512]{2,1,0:T(2,128)(2,1)}), bf16[128,2,512]{2,1,0:T(2,128)(2,1)}, u32[]{:S(2)}, u32[]{:S(2)}) %all-to-all-start.3) | async-done | bytes 262176 | tf_op jit(solution)/shard_map/all_to_all | solution.py:114
  77.8 4.0 %all-to-all-start.1 = ((bf16[128,2,512]{2,1,0:T(2,128)(2,1)}), bf16[128,2,512]{2,1,0:T(2,128)(2,1)}, u32[]{:S(2)}, u32[]{:S(2)}) async-start(bf16[128,2,512]{2,1,0:T(2,128)(2,1)} %broadcast_select_fusion.6), calls=%async_computation.1 | async-start | bytes 524288 | tf_op jit(solution)/shard_map/all_to_all | solution.py:93
  84.9 2.7 %convolution_bitcast_fusion = f32[16,128,512]{1,2,0:T(8,128)} fusion(bf16[16,16,512]{2,1,0:T(8,128)(2,1)S(1)} %all_to_all.67, bf16[16,16,128]{2,1,0:T(8,128)(2,1)S(1)} %copy-done), kind=kOutput, calls=%fused_computation.6 | convolution fusion | flops 33554432 | bytes 4521984 | tf_op jit(solution)/shard_map/abi,abt->ait/dot_general | solution.py:122
  87.6 1.9 %fusion.40 = bf16[16,16,128]{2,1,0:T(8,128)(2,1)} fusion(bf16[16,16,512]{2,1,0:T(8,128)(2,1)S(1)} %all_to_all.67, bf16[16,128,512]{2,0,1:T(8,128)(2,1)S(1)} %fusion.13), kind=kOutput, calls=%fused_computation.46 | convolution fusion | flops 33587200 | bytes 2424832 | tf_op jit(solution)/shard_map/abt,ait->abi/dot_general | solution.py:115
  90.9 3.5 %fusion.43 = bf16[16,16,128]{2,1,0:T(8,128)(2,1)} fusion(bf16[16,16,512]{2,1,0:T(8,128)(2,1)S(1)} %all_to_all.59, bf16[16,128,512]{2,0,1:T(8,128)(2,1)} %copy-done.1), kind=kOutput, calls=%fused_computation.47 | convolution fusion | flops 33587200 | bytes 2424832 | tf_op jit(solution)/shard_map/abt,aot->abo/dot_general | solution.py:103
  94.3 2.8 %convolution_bitcast_fusion.1 = f32[16,128,512]{1,2,0:T(8,128)} fusion(bf16[16,16,512]{2,1,0:T(8,128)(2,1)S(1)} %all_to_all.59, bf16[16,16,128]{2,1,0:T(8,128)(2,1)S(1)} %copy-done.8), kind=kOutput, calls=%fused_computation.7 | convolution fusion | flops 33554432 | bytes 4521984 | tf_op jit(solution)/shard_map/abo,abt->aot/dot_general | solution.py:95
  97.1 5.5 %copy.108 = f32[16,128,512]{2,0,1:T(8,128)} copy(f32[16,128,512]{1,2,0:T(8,128)} %convolution_bitcast_fusion) | data formatting | bytes 8388608 | tf_op jit(solution)/shard_map/abi,abt->ait/dot_general | solution.py:122
  102.6 4.4 %fusion.57 = f32[16,128,512]{2,0,1:T(8,128)S(1)} fusion(f32[16,128,512]{2,0,1:T(8,128)} %copy.108, s32[16]{0:T(128)S(1)} %and_select_fusion), kind=kOutput, calls=%fused_computation.75 | convolution fusion | flops 201326848 | bytes 8388672 | tf_op jit(solution)/shard_map/am,ait->mit/dot_general | solution.py:123
  107.0 1.9 %copy-done.2 = f32[16,128,512]{2,0,1:T(8,128)} copy-done((f32[16,128,512]{2,0,1:T(8,128)}, f32[16,128,512]{2,0,1:T(8,128)S(1)}, u32[]{:S(2)}) %copy-start.2) | copy-done | bytes 4194328
  109.5 5.5 %copy.95 = f32[16,128,512]{2,0,1:T(8,128)} copy(f32[16,128,512]{1,2,0:T(8,128)} %convolution_bitcast_fusion.1) | data formatting | bytes 8388608 | tf_op jit(solution)/shard_map/abo,abt->aot/dot_general | solution.py:95
  115.0 4.4 %fusion.59 = f32[16,128,512]{2,0,1:T(8,128)S(1)} fusion(f32[16,128,512]{2,0,1:T(8,128)} %copy.95, s32[16]{0:T(128)S(1)} %and_select_fusion), kind=kOutput, calls=%fused_computation.76 | convolution fusion | flops 201326848 | bytes 8388672 | tf_op jit(solution)/shard_map/am,aot->mot/dot_general | solution.py:96
  119.4 2.0 %copy-done.3 = f32[16,128,512]{2,0,1:T(8,128)} copy-done((f32[16,128,512]{2,0,1:T(8,128)}, f32[16,128,512]{2,0,1:T(8,128)S(1)}, u32[]{:S(2)}) %copy-start.3) | copy-done | bytes 4194328
  121.8 30.8 %all-reduce.3.cloned.1.call-done = (bf16[16,16,128]{2,1,0:T(8,128)(2,1)}, bf16[2,128,128]{2,1,0:T(8,128)(2,1)}, bf16[2,128,128]{2,1,0:T(8,128)(2,1)}, bf16[16,16,128]{2,1,0:T(8,128)(2,1)}) async-done(((bf16[16,16,128]{2,1,0:T(8,128)(2,1)}, bf16[2,128,128]{2,1,0:T(8,128)(2,1)}, bf16[2,128,128]{2,1,0:T(8,128)(2,1)}, bf16[16,16,128]{2,1,0:T(8,128)(2,1)}), (bf16[16,16,128]{2,1,0:T(8,128)(2,1)}, ...) | async-done | bytes 262160 | tf_op jit(solution)/shard_map/psum | solution.py:117
  158.6 2.3 %convert_add_fusion = f32[16,64,512]{2,0,1:T(8,128)S(1)} fusion(bf16[16,64,512]{2,0,1:T(8,128)(2,1)} %collective-permute-done.3, f32[16,128,512]{2,0,1:T(8,128)} %copy-done.2, s32[]{:T(128)S(6)} %select_n.62), kind=kLoop, calls=%fused_computation.20 | loop fusion | flops 1048576 | bytes 5242884 | tf_op jit(solution)/shard_map/add | solution.py:34
  (89 shorter events, 55.4 us)
Async XLA Ops:
  7.2 8.4 %copy-start = (bf16[16,16,128]{2,1,0:T(8,128)(2,1)S(1)}, bf16[16,16,128]{2,1,0:T(8,128)(2,1)}, u32[]{:S(2)}) copy-start(bf16[16,16,128]{2,1,0:T(8,128)(2,1)} %param.12) | copy-start | bytes 196612
  7.2 5.0 %collective-permute-start = (bf16[1024,512]{1,0:T(8,128)(2,1)}, bf16[1024,512]{1,0:T(8,128)(2,1)S(1)}, u32[]{:S(2)}, u32[]{:S(2)}) collective-permute-start(bf16[1024,512]{1,0:T(8,128)(2,1)} %param.10), channel_id=1, source_target_pairs={{0,1},{1,0},{2,3},{3,2},{4,5},{5,4},{6,7},{7,6},{8,9},{9,8},{10,11... | collective-permute-start | bytes 3145736 | tf_op jit(solution)/shard_map/ppermute | solution.py:12
  7.7 16.2 %collective-permute-start.2 = (bf16[1024,512]{1,0:T(8,128)(2,1)}, bf16[1024,512]{1,0:T(8,128)(2,1)}, u32[]{:S(2)}, u32[]{:S(2)}) collective-permute-start(bf16[1024,512]{1,0:T(8,128)(2,1)} %param.11), channel_id=1, source_target_pairs={{0,1},{1,0},{2,3},{3,2},{4,5},{5,4},{6,7},{7,6},{8,9},{9,8},{10,11... | collective-permute-start | bytes 3145736 | tf_op jit(solution)/shard_map/ppermute | solution.py:12
  15.5 8.3 %copy-start.5 = (bf16[1024,512]{1,0:T(8,128)(2,1)S(1)}, bf16[1024,512]{1,0:T(8,128)(2,1)}, u32[]{:S(2)}) copy-start(bf16[1024,512]{1,0:T(8,128)(2,1)} %param.11) | copy-start | bytes 3145732
  18.7 13.0 %all-to-all-start = ((bf16[16,16,512]{2,0,1:T(8,128)(2,1)}), bf16[16,16,512]{2,0,1:T(8,128)(2,1)S(1)}, u32[]{:S(2)}, u32[]{:S(2)}) async-start(bf16[16,16,512]{2,0,1:T(8,128)(2,1)} %copy.88), calls=%async_computation | async-start | bytes 524288 | tf_op jit(solution)/shard_map/all_to_all | solution.py:84
  26.4 2.1 %copy-start.8 = (bf16[16,16,128]{2,1,0:T(8,128)(2,1)S(1)}, bf16[16,16,128]{2,1,0:T(8,128)(2,1)}, u32[]{:S(2)}) copy-start(bf16[16,16,128]{2,1,0:T(8,128)(2,1)} %param.15) | copy-start | bytes 196612
  27.2 1.4 copy-start.1
  31.7 11.2 %all-to-all-start.2 = ((bf16[16,16,512]{2,0,1:T(8,128)(2,1)}), bf16[16,16,512]{2,0,1:T(8,128)(2,1)}, u32[]{:S(2)}, u32[]{:S(2)}) async-start(bf16[16,16,512]{2,0,1:T(8,128)(2,1)} %copy.101), calls=%async_computation.2 | async-start | bytes 524288 | tf_op jit(solution)/shard_map/all_to_all | solution.py:104
  49.9 0.7 copy-start.7
  55.2 5.5 %copy-start.9 = (bf16[2,128,128]{2,1,0:T(8,128)(2,1)S(1)}, bf16[2,128,128]{2,1,0:T(8,128)(2,1)}, u32[]{:S(2)}) copy-start(bf16[2,128,128]{2,1,0:T(8,128)(2,1)} %param.13) | copy-start | bytes 196612
  58.4 7.4 %copy-start.10 = (pred[128]{0:T(512)(128)(4,1)S(1)}, pred[128]{0:T(512)(128)(4,1)}, u32[]{:S(2)}) copy-start(pred[128]{0:T(512)(128)(4,1)} %get-tuple-element.19) | copy-start | bytes 388
  66.8 11.0 %all-to-all-start.3 = ((bf16[128,2,512]{2,1,0:T(2,128)(2,1)}), bf16[128,2,512]{2,1,0:T(2,128)(2,1)}, u32[]{:S(2)}, u32[]{:S(2)}) async-start(bf16[128,2,512]{2,1,0:T(2,128)(2,1)} %broadcast_select_fusion.4), calls=%async_computation.3 | async-start | bytes 524288 | tf_op jit(solution)/shard_map/all_to_all | solution.py:114
  77.8 11.7 %all-to-all-start.1 = ((bf16[128,2,512]{2,1,0:T(2,128)(2,1)}), bf16[128,2,512]{2,1,0:T(2,128)(2,1)}, u32[]{:S(2)}, u32[]{:S(2)}) async-start(bf16[128,2,512]{2,1,0:T(2,128)(2,1)} %broadcast_select_fusion.6), calls=%async_computation.1 | async-start | bytes 524288 | tf_op jit(solution)/shard_map/all_to_all | solution.py:93
  81.8 70.8 %all-reduce.3.cloned.1.call-start = ((), (), s32[]{:S(2)}) async-start(), calls=%async_computation.4 | async-start | bytes 524288 | tf_op jit(solution)/shard_map/psum | solution.py:117
  107.0 2.0 %copy-start.2 = (f32[16,128,512]{2,0,1:T(8,128)}, f32[16,128,512]{2,0,1:T(8,128)S(1)}, u32[]{:S(2)}) copy-start(f32[16,128,512]{2,0,1:T(8,128)S(1)} %fusion.57) | copy-start | bytes 12582916
  109.1 49.5 %collective-permute-start.3 = (bf16[16,64,512]{2,0,1:T(8,128)(2,1)S(1)}, bf16[16,64,512]{2,0,1:T(8,128)(2,1)}, u32[]{:S(2)}, u32[]{:S(2)}) collective-permute-start(bf16[16,64,512]{2,0,1:T(8,128)(2,1)S(1)} %dynamic-slice_convert_fusion), channel_id=1, source_target_pairs={{0,1},{1,0},{2,3},{3,2},{4,5},{5,4},{6,7},{7,6},{8,9},{9,8},{10,11... | collective-permute-start | bytes 3145736 | tf_op jit(solution)/shard_map/ppermute | solution.py:12
  119.4 2.0 %copy-start.3 = (f32[16,128,512]{2,0,1:T(8,128)}, f32[16,128,512]{2,0,1:T(8,128)S(1)}, u32[]{:S(2)}) copy-start(f32[16,128,512]{2,0,1:T(8,128)S(1)} %fusion.59) | copy-start | bytes 12582916
  121.6 41.9 %collective-permute-start.1 = (bf16[16,64,512]{2,0,1:T(8,128)(2,1)S(1)}, bf16[16,64,512]{2,0,1:T(8,128)(2,1)}, u32[]{:S(2)}, u32[]{:S(2)}) collective-permute-start(bf16[16,64,512]{2,0,1:T(8,128)(2,1)S(1)} %dynamic-slice_convert_fusion.1), channel_id=1, source_target_pairs={{0,1},{1,0},{2,3},{3,2},{4,5},{5,4},{6,7},{7,6},{8,9},{9,8},{10,11... | collective-permute-start | bytes 3145736 | tf_op jit(solution)/shard_map/ppermute | solution.py:12
  162.1 2.6 %copy-start.4 = (f32[16,128,512]{2,0,1:T(8,128)S(1)}, f32[16,128,512]{2,0,1:T(8,128)}, u32[]{:S(2)}) copy-start(f32[16,128,512]{2,0,1:T(8,128)} %copy-done.3) | copy-start | bytes 12582916
  166.4 1.2 copy-start.6
Sparse Core Ops, SparseCore 0:
  115.1 37.4 all-reduce.2
where the time goes:
time: 177 us; the launch traced here: 176 us
  local copies, waits for them, and re-layouts  45.1 us (25%)
  waiting for transfers between devices  38.2 us (22%)
  matrix products  33.8 us (19%)
  other arithmetic  25.6 us (14%)
  starting transfers between devices  18.7 us (11%)
  between operations  14.4 us (8%)
    psum x1, waiting for transfers between devices, shards(): lax.psum(g_up_first.astype(jnp.bfloat16), 'dp').astype(jnp.float32)  30.8 us
    unnamed x22, local copies, waits for them, and re-layouts  7.26 us
    dot_general x1, local copies, waits for them, and re-layouts, shards(): jnp.einsum('abi,abt->ait', up_first, grad_hidden, preferred_element_type=...  5.49 us
    dot_general x1, local copies, waits for them, and re-layouts, shards(): jnp.einsum('abo,abt->aot', down_second, back_rows, preferred_element_type...  5.49 us
    all_to_all x1, starting transfers between devices, shards(): lax.all_to_all(hidden_one, 'loop', split_axis=1, concat_axis=0, tiled=True)  5.15 us
    dot_general x1, matrix products, shards(): jnp.einsum('am,aot->mot', picker_wide, out_rows, precision=lax.Precision....  4.39 us
    dot_general x1, matrix products, shards(): jnp.einsum('am,ait->mit', picker_wide, grad_rows_in, precision=lax.Precis...  4.39 us
    all_to_all x1, waiting for transfers between devices, shards(): lax.all_to_all(grad_rows, 'loop', split_axis=1, concat_axis=0, tiled=True)  4.26 us
  transfers between devices with their start and end apart: 9, of which 3 were waited for; matrix products, arithmetic and copies ran while one was open for 29% of the time, Pallas kernels for 0%

commit v1 on v0

--- a/solution.py
+++ b/solution.py
@@ -3,6 +3,8 @@
 import jax
 import jax.numpy as jnp
 from jax import lax
+from jax.experimental import pallas as pl
+from jax.experimental.pallas import tpu as pltpu
 from jax.sharding import PartitionSpec as P
 
 
@@ -35,7 +37,7 @@
     return mine.reshape(pair_blocks * half_width, tok_count)
 
 
-def shards(tokens, cotangent, up_first, up_second, down_first, down_second, perm_up, perm_down):
+def plain_shards(tokens, cotangent, up_first, up_second, down_first, down_second, perm_up, perm_down):
     wide = jnp.float32
     narrow = jnp.bfloat16
     feature_rows = tokens.shape[0]
@@ -135,6 +137,305 @@
     )
 
 
+VMEM_LIMIT = 48 * 2**20
+
+
+def dot(left, right, left_dim=1, right_dim=0):
+    return lax.dot_general(
+        left, right, (((left_dim,), (right_dim,)), ((), ())), preferred_element_type=jnp.float32
+    )
+
+
+def call(body, outs, *args):
+    whole = pl.BlockSpec(memory_space=pltpu.VMEM)
+    return pl.pallas_call(
+        body,
+        out_shape=outs,
+        in_specs=[whole] * len(args),
+        out_specs=jax.tree.map(lambda _: whole, outs),
+        compiler_params=pltpu.CompilerParams(vmem_limit_bytes=VMEM_LIMIT),
+    )(*args)
+
+
+def own_first(weights, parity):
+    wide = weights.astype(jnp.float32)
+    half = wide.shape[1] // 2
+    turned = pltpu.roll(wide, half, 1)
+    return jnp.where(parity == 0, wide, turned)
+
+
+def block_rows(own_ref, other_ref, block, half, parity, count):
+    start = pl.multiple_of(parity * (count * half) + block * half, half)
+    return jnp.concatenate(
+        [own_ref[pl.ds(start, half), :], other_ref[block * half : (block + 1) * half, :]], 0
+    )
+
+
+def grid_order(me, loops, rows, cols, sent_dim):
+    size = loops * rows * cols
+    sent = lax.broadcasted_iota(jnp.int32, (size, size), sent_dim)
+    kept = lax.broadcasted_iota(jnp.int32, (size, size), 1 - sent_dim)
+    device = (sent // (rows * cols)) ^ me
+    col = device * cols + (sent // rows) % cols
+    return (kept == (sent % rows) * (loops * cols) + col).astype(jnp.bfloat16)
+
+
+def first_rows(loops, rows, cols, half):
+    narrow = jnp.bfloat16
+
+    def body(tok_ref, x_ref, cot_ref, d_ref, up_ref, down_ref, *rest):
+        outs, (hid_ref, grad_ref) = rest[:loops], rest[loops:]
+        me = lax.axis_index("loop")
+        parity = me % 2
+        count = x_ref.shape[0] // half
+        high = up_ref.shape[0] // count
+        up = own_first(up_ref[...], parity).astype(narrow)
+        down = own_first(down_ref[...], parity).astype(narrow)
+        for e in range(count):
+            part = slice(e * high, (e + 1) * high)
+            x_rows = block_rows(tok_ref, x_ref, e, half, parity, count)
+            d_rows = block_rows(cot_ref, d_ref, e, half, parity, count)
+            hid_ref[part, :] = dot(up[part], x_rows).astype(narrow)
+            grad_ref[part, :] = dot(down[part], d_rows).astype(narrow)
+        order = grid_order(me, loops, rows, cols, 0)
+        unit = rows * cols
+        for q, ref in enumerate((hid_ref, grad_ref)):
+            sent = dot(order, ref[...]).astype(narrow)
+            for k in range(loops):
+                outs[k][q * unit : (q + 1) * unit, :] = sent[k * unit : (k + 1) * unit]
+
+    return body
+
+
+def columns(loops, rows, cols):
+    narrow = jnp.bfloat16
+
+    def body(*refs):
+        bufs, rest = refs[:loops], refs[loops:]
+        up_ref, down_ref, perm_up_ref, perm_down_ref = rest[:4]
+        outs, grads_ref = rest[4 : 4 + loops], rest[4 + loops]
+        me = lax.axis_index("loop")
+        size = loops * rows
+        unit = rows * cols
+        lead = lax.broadcasted_iota(jnp.int32, (size, size), 0)
+        lane = lax.broadcasted_iota(jnp.int32, (size, size), 1)
+        row = ((lead // rows) ^ me) * rows + lead % rows
+        take_up = (perm_up_ref[...] == row).astype(narrow)
+        take_down = dot(
+            (lane == row).astype(narrow), (perm_down_ref[...] == lead).astype(narrow), 1, 1
+        ).astype(narrow)
+        for b in range(cols):
+            span = slice(b * size, (b + 1) * size)
+            hid = jnp.concatenate([r[b * rows : (b + 1) * rows, :] for r in bufs], 0)
+            grad = jnp.concatenate([r[unit + b * rows : unit + (b + 1) * rows, :] for r in bufs], 0)
+            up = dot(up_ref[span, :], take_up, 1, 1).astype(narrow)
+            down = dot(take_down, down_ref[span, :]).astype(narrow)
+            gelu_val, slope = gelu_parts(dot(up, hid))
+            activated = gelu_val.astype(narrow)
+            back = dot(down, activated).astype(narrow)
+            grad_pre = (dot(down, grad, 0, 0) * slope).astype(narrow)
+            grad_back = dot(up, grad_pre, 0, 0).astype(narrow)
+            for k in range(loops):
+                part = slice(k * rows, (k + 1) * rows)
+                outs[k][b * rows : (b + 1) * rows, :] = back[part]
+                outs[k][unit + b * rows : unit + (b + 1) * rows, :] = grad_back[part]
+            g_up = dot(grad_pre, hid, 1, 1).astype(narrow)
+            g_down = dot(grad, activated, 1, 1).astype(narrow)
+            grads_ref[span, :] = dot(g_up, take_up).astype(narrow)
+            grads_ref[cols * size + b * size : cols * size + (b + 1) * size, :] = dot(
+                take_down, g_down, 0, 0
+            ).astype(narrow)
+
+    return body
+
+
+def row_grads(loops, rows, cols, half):
+    narrow = jnp.bfloat16
+
+    def body(*refs):
+        bufs, rest = refs[:loops], refs[loops:]
+        tok_ref, x_ref, cot_ref, d_ref, grads_ref, back_ref, grad_ref = rest
+        me = lax.axis_index("loop")
+        parity = me % 2
+        unit = rows * cols
+        count = x_ref.shape[0] // half
+        size = loops * unit
+        high = size // count
+        order = grid_order(me, loops, rows, cols, 1)
+        for q, ref in enumerate((back_ref, grad_ref)):
+            sent = jnp.concatenate([r[q * unit : (q + 1) * unit, :] for r in bufs], 0)
+            ref[...] = dot(order, sent).astype(narrow)
+        g_up, g_down = [], []
+        for e in range(count):
+            part = slice(e * high, (e + 1) * high)
+            x_rows = block_rows(tok_ref, x_ref, e, half, parity, count)
+            d_rows = block_rows(cot_ref, d_ref, e, half, parity, count)
+            g_up.append(dot(grad_ref[part, :], x_rows, 1, 1))
+            g_down.append(dot(back_ref[part, :], d_rows, 1, 1))
+        grads_ref[:size, :] = own_first(jnp.concatenate(g_up, 0), parity).astype(narrow)
+        grads_ref[size:, :] = own_first(jnp.concatenate(g_down, 0), parity).astype(narrow)
+
+    return body
+
+
+def row_outputs(half):
+    narrow = jnp.bfloat16
+
+    def body(back_ref, grad_ref, tok_ref, x_ref, cot_ref, d_ref, up_ref, down_ref, *outs):
+        mixed_ref, mixed_send_ref, grads_ref, grads_send_ref = outs
+        parity = lax.axis_index("loop") % 2
+        count = x_ref.shape[0] // half
+        high = up_ref.shape[0] // count
+        up = own_first(up_ref[...], parity).astype(narrow)
+        down = own_first(down_ref[...], parity).astype(narrow)
+        jobs = (
+            (down, back_ref, tok_ref, x_ref, mixed_ref, mixed_send_ref),
+            (up, grad_ref, cot_ref, d_ref, grads_ref, grads_send_ref),
+        )
+        for weights, rows_ref, own_ref, other_ref, kept_ref, sent_ref in jobs:
+            for e in range(count):
+                part = slice(e * high, (e + 1) * high)
+                start = pl.multiple_of(parity * (count * half) + e * half, half)
+                near = slice(e * half, (e + 1) * half)
+                branch = dot(weights[part], rows_ref[part, :], 0, 0)
+                own = own_ref[pl.ds(start, half), :].astype(jnp.float32)
+                kept_ref[pl.ds(start, half), :] = (own + branch[:half]).astype(narrow)
+                other = other_ref[near, :].astype(jnp.float32)
+                sent_ref[near, :] = (other + branch[half:]).astype(narrow)
+
+    return body
+
+
+def add_shards(scale):
+    def body(*refs):
+        parts, outs = refs[:-2], refs[-2:]
+        size = outs[0].shape[0]
+        for at, out in enumerate(outs):
+            span = slice(at * size, (at + 1) * size)
+            total = parts[0][span, :].astype(jnp.float32)
+            for part in parts[1:]:
+                total = total + part[span, :].astype(jnp.float32)
+            out[...] = total * scale
+
+    return body
+
+
+def exchange(bufs, axis):
+    count = len(bufs)
+    got = {
+        k: lax.ppermute(bufs[k], axis, [(s, s ^ k) for s in range(count)])
+        for k in range(count - 1, 0, -1)
+    }
+    return [bufs[0]] + [got[k] for k in range(1, count)]
+
+
+def shards(tokens, cotangent, up_first, up_second, down_first, down_second, perm_up, perm_down):
+    narrow = jnp.bfloat16
+    loops, dps = lax.axis_size("loop"), lax.axis_size("dp")
+    feature_rows, toks = tokens.shape
+    rows, all_cols, block = up_first.shape
+    cols = up_second.shape[0]
+    half = block // 2
+    group = 2 * rows // (2 * feature_rows // block)
+    if loops > 8 or rows % 16 or rows % group or dps & (dps - 1):
+        return plain_shards(
+            tokens, cotangent, up_first, up_second, down_first, down_second, perm_up, perm_down
+        )
+    parity = lax.axis_index("loop") % 2
+    kept = feature_rows // 2
+
+    def partner_half(value):
+        leaving = lax.dynamic_slice_in_dim(value, (1 - parity) * kept, kept, 0)
+        return from_partner(leaving, "loop", 0)
+
+    other_x, other_d = partner_half(tokens), partner_half(cotangent)
+    up_rows = up_first.reshape(rows * all_cols, block)
+    down_rows = down_second.reshape(rows * all_cols, block)
+    buf = jax.ShapeDtypeStruct((2 * rows * cols, toks), narrow)
+    whole = jax.ShapeDtypeStruct((rows * all_cols, toks), narrow)
+    grads = jax.ShapeDtypeStruct((2 * rows * all_cols, block), narrow)
+    unit = rows * cols
+
+    def rows_call(body, outs, args, scratch):
+        spec = pl.BlockSpec(memory_space=pltpu.VMEM)
+        return pl.pallas_call(
+            body,
+            out_shape=outs,
+            in_specs=[spec] * len(args),
+            out_specs=[spec] * len(outs),
+            scratch_shapes=scratch,
+            compiler_params=pltpu.CompilerParams(vmem_limit_bytes=VMEM_LIMIT),
+        )(*args)
+
+    sent = rows_call(
+        first_rows(loops, rows, cols, half),
+        [buf] * loops,
+        (tokens, other_x, cotangent, other_d, up_rows, down_rows),
+        [pltpu.VMEM(whole.shape, narrow)] * 2,
+    )
+    got = exchange(sent, "loop")
+    size = up_second.shape[1]
+    *sent, col_grads = call(
+        columns(loops, rows, cols),
+        [buf] * loops + [jax.ShapeDtypeStruct((2 * cols * size, size), narrow)],
+        *got,
+        up_second.reshape(cols * size, size),
+        down_first.reshape(cols * size, size),
+        perm_up.reshape(1, size),
+        perm_down.reshape(1, size),
+    )
+    got = exchange(sent, "loop")
+    row_sums, back, grad = call(
+        row_grads(loops, rows, cols, half),
+        [grads, whole, whole],
+        *got,
+        tokens,
+        other_x,
+        cotangent,
+        other_d,
+    )
+    scale = 1.0 / math.sqrt(dps * toks)
+
+    def dp_total(value):
+        parts = [value] + [
+            lax.ppermute(value, "dp", [(s, s ^ k) for s in range(dps)])
+            for k in range(dps - 1, 0, -1)
+        ]
+        out = jax.ShapeDtypeStruct((value.shape[0] // 2, value.shape[1]), jnp.float32)
+        return call(add_shards(scale), [out, out], *parts)
+
+    g_up_second, g_down_first = dp_total(col_grads)
+    g_up_first, g_down_second = dp_total(row_sums)
+    full = jax.ShapeDtypeStruct(tokens.shape, narrow)
+    part = jax.ShapeDtypeStruct((kept, toks), narrow)
+    mixed, mixed_send, grad_tokens, grad_send = call(
+        row_outputs(half),
+        [full, part, full, part],
+        back,
+        grad,
+        tokens,
+        other_x,
+        cotangent,
+        other_d,
+        up_rows,
+        down_rows,
+    )
+
+    def place(value, leaving):
+        return lax.dynamic_update_slice_in_dim(
+            value, from_partner(leaving, "loop", 0), (1 - parity) * kept, 0
+        )
+
+    return (
+        place(mixed, mixed_send),
+        place(grad_tokens, grad_send),
+        g_up_first.reshape(up_first.shape),
+        g_up_second.reshape(up_second.shape),
+        g_down_first.reshape(down_first.shape),
+        g_down_second.reshape(down_second.shape),
+    )
+
+
 def solution(mesh):
     in_specs = (
         P("loop", "dp"),

time: 177 us -> 65 us (0.37)
  local copies, waits for them, and re-layouts: 45.1 us -> 4.95 us
  matrix products: 33.8 us -> 0 us
  other arithmetic: 25.6 us -> 0 us
  between operations: 14.4 us -> 0.79 us
  waiting for transfers between devices: 38.2 us -> 27.3 us
  Pallas kernels: 0 us -> 6.88 us
  starting transfers between devices: 18.7 us -> 24.8 us
    dot_general x16 -> x0, matrix products: 33.8 us -> none  [the longest x1 4.39 us: shards(): jnp.einsum('am,aot->mot', picker_wide, out_rows, precision=lax.Precision....]
    psum x1 -> x0, waiting for transfers between devices: 30.8 us -> none  [shards(): lax.psum(g_up_first.astype(jnp.bfloat16), 'dp').astype(jnp.float32)]
    ppermute x0 -> x20, waiting for transfers between devices: none -> 25.2 us  [the longest x6 16.3 us: dp_total(): lax.ppermute(value, 'dp', [(s, s ^ k) for s in range(dps)])]
    ppermute x0 -> x20, starting transfers between devices: none -> 23.6 us  [the longest x14 13.9 us: exchange(): lax.ppermute(bufs[k], axis, [(s, s ^ k) for s in range(count)])]
    all_to_all x4 -> x0, starting transfers between devices: 17.5 us -> none  [the longest x1 5.15 us: shards(): lax.all_to_all(hidden_one, 'loop', split_axis=1, concat_axis=0, tiled=True)]
    dot_general x2 -> x0, local copies, waits for them, and re-layouts: 11 us -> none  [the longest x1 5.49 us: shards(): jnp.einsum('abi,abt->ait', up_first, grad_hidden, preferred_element_type=...]
    select_n x10 -> x0, other arithmetic: 9.89 us -> none  [the longest x2 2.35 us: shards(): leaving = jnp.take(mixed_cols, perm_down, axis=0)]
    gather x4 -> x0, local copies, waits for them, and re-layouts: 8.87 us -> none  [the longest x1 2.89 us: shards(): grad_mixed = jnp.take(grad_cols, inverse_down, axis=0)]
  transfers between devices with their start and end apart: 9 -> 24, of which waited for: 3 -> 12; matrix products, arithmetic and copies ran while one was open for 29% -> 0% of each run, Pallas kernels for 0% -> 2%
where the time goes in v1:
time: 65 us; the launch traced here: 64.7 us
  waiting for transfers between devices  27.3 us (42%)
  starting transfers between devices  24.8 us (38%)
  Pallas kernels  6.88 us (11%)
  local copies, waits for them, and re-layouts  4.95 us (8%)
  between operations  0.79 us (1%)
    ppermute x6, waiting for transfers between devices, dp_total(): lax.ppermute(value, 'dp', [(s, s ^ k) for s in range(dps)])  16.3 us
    ppermute x14, starting transfers between devices, exchange(): lax.ppermute(bufs[k], axis, [(s, s ^ k) for s in range(count)])  13.9 us
    ppermute x6, starting transfers between devices, dp_total(): lax.ppermute(value, 'dp', [(s, s ^ k) for s in range(dps)])  9.69 us
    ppermute x14, waiting for transfers between devices, exchange(): lax.ppermute(bufs[k], axis, [(s, s ^ k) for s in range(count)])  8.9 us
    pallas_call x5, Pallas kernels, call(): pl.pallas_call(body, out_shape=outs, in_specs=[whole] * len(args), out_sp...  6.16 us
    unnamed x28, local copies, waits for them, and re-layouts  3.61 us
    ppermute x4, waiting for transfers between devices, from_partner(): return lax.ppermute(value, axis, pairs)  2.13 us
  transfers between devices with their start and end apart: 24, of which 12 were waited for; matrix products, arithmetic and copies ran while one was open for 0% of the time, Pallas kernels for 2%

profile of v1, /device:TPU:0, one launch (start us, length us, event | category | flops | bytes accessed | tf_op | source)
XLA Modules:
  0.0 64.7 jit_solution(11657444986916280910)
XLA Ops:
  0.7 1.2 %constant_dynamic-slice_fusion.1 = bf16[512,512]{1,0:T(8,128)(2,1)S(1)} fusion(bf16[1024,512]{1,0:T(8,128)(2,1)} %tok_ref.3, s32[]{:T(128)S(6)} %select_n.14), kind=kLoop, calls=%fused_computation.3 | loop fusion | bytes 1048580 | tf_op jit(solution)/shard_map/dynamic_slice | solution.py:348
  2.6 1.4 %collective-permute-done.x_ref.refs_9_ = bf16[512,512]{1,0:T(8,128)(2,1)S(1)} collective-permute-done((bf16[512,512]{1,0:T(8,128)(2,1)S(1)}, bf16[512,512]{1,0:T(8,128)(2,1)S(1)}, u32[]{:S(2)}, u32[]{:S(2)}) %collective-permute-start) | collective-permute-done | bytes 524320 | tf_op jit(solution)/shard_map/ppermute | solution.py:14
  4.7 0.8 %copy-done.2 = bf16[16,16,128]{2,1,0:T(8,128)(2,1)S(1)} copy-done((bf16[16,16,128]{2,1,0:T(8,128)(2,1)S(1)}, bf16[16,16,128]{2,1,0:T(8,128)(2,1)}, u32[]{:S(2)}) %copy-start.2) | copy-done | bytes 65560
  7.5 2.7 %collective-permute-start.3 = (bf16[64,512]{1,0:T(8,128)(2,1)S(1)}, bf16[64,512]{1,0:T(8,128)(2,1)S(1)}, u32[]{:S(2)}, u32[]{:S(2)}) collective-permute-start(bf16[64,512]{1,0:T(8,128)(2,1)S(1)} %get-tuple-element.36), channel_id=1, source_target_pairs={{0,2},{1,3},{2,0},{3,1},{4,6},{5,7},{6,4},{7,5},{8,10},{9,11},{10,... | collective-permute-start | bytes 196616 | tf_op jit(solution)/shard_map/ppermute | solution.py:326
  10.2 1.7 %collective-permute-start.5 = (bf16[64,512]{1,0:T(8,128)(2,1)S(1)}, bf16[64,512]{1,0:T(8,128)(2,1)S(1)}, u32[]{:S(2)}, u32[]{:S(2)}) collective-permute-start(bf16[64,512]{1,0:T(8,128)(2,1)S(1)} %get-tuple-element.38), channel_id=1, source_target_pairs={{0,4},{1,5},{2,6},{3,7},{4,0},{5,1},{6,2},{7,3},{8,12},{9,13},{10,... | collective-permute-start | bytes 196616 | tf_op jit(solution)/shard_map/ppermute | solution.py:326
  12.0 2.7 %collective-permute-start.7 = (bf16[64,512]{1,0:T(8,128)(2,1)S(1)}, bf16[64,512]{1,0:T(8,128)(2,1)S(1)}, u32[]{:S(2)}, u32[]{:S(2)}) collective-permute-start(bf16[64,512]{1,0:T(8,128)(2,1)S(1)} %get-tuple-element.40), channel_id=1, source_target_pairs={{0,6},{1,7},{2,4},{3,5},{4,2},{5,3},{6,0},{7,1},{8,14},{9,15},{10,... | collective-permute-start | bytes 196616 | tf_op jit(solution)/shard_map/ppermute | solution.py:326
  14.7 2.8 %collective-permute-done.6.refs_5_ = bf16[64,512]{1,0:T(8,128)(2,1)S(1)} collective-permute-done((bf16[64,512]{1,0:T(8,128)(2,1)S(1)}, bf16[64,512]{1,0:T(8,128)(2,1)S(1)}, u32[]{:S(2)}, u32[]{:S(2)}) %collective-permute-start.6) | collective-permute-done | bytes 65568 | tf_op jit(solution)/shard_map/ppermute | solution.py:326
  17.5 2.2 %collective-permute-done.8.refs_7_ = bf16[64,512]{1,0:T(8,128)(2,1)S(1)} collective-permute-done((bf16[64,512]{1,0:T(8,128)(2,1)S(1)}, bf16[64,512]{1,0:T(8,128)(2,1)S(1)}, u32[]{:S(2)}, u32[]{:S(2)}) %collective-permute-start.8) | collective-permute-done | bytes 65568 | tf_op jit(solution)/shard_map/ppermute | solution.py:326
  20.4 1.7 %shard_map.128 = (bf16[64,512]{1,0:T(8,128)(2,1)S(1)}, bf16[64,512]{1,0:T(8,128)(2,1)S(1)}, bf16[64,512]{1,0:T(8,128)(2,1)S(1)}, bf16[64,512]{1,0:T(8,128)(2,1)S...) custom-call(bf16[64,512]{1,0:T(8,128)(2,1)S(1)} %get-tuple-element.3, ...), custom_call_target="tpu_custom_call" | custom-call | tf_op jit(solution)/shard_map/pallas_call | solution.py:151
  22.9 1.1 %collective-permute-start.11 = (bf16[64,512]{1,0:T(8,128)(2,1)S(1)}, bf16[64,512]{1,0:T(8,128)(2,1)S(1)}, u32[]{:S(2)}, u32[]{:S(2)}) collective-permute-start(bf16[64,512]{1,0:T(8,128)(2,1)S(1)} %get-tuple-element.45), channel_id=1, source_target_pairs={{0,3},{1,2},{2,1},{3,0},{4,7},{5,6},{6,5},{7,4},{8,11},{9,10},{10,... | collective-permute-start | bytes 196616 | tf_op jit(solution)/shard_map/ppermute | solution.py:326
  24.6 1.2 %collective-permute-start.13 = (bf16[64,512]{1,0:T(8,128)(2,1)S(1)}, bf16[64,512]{1,0:T(8,128)(2,1)S(1)}, u32[]{:S(2)}, u32[]{:S(2)}) collective-permute-start(bf16[64,512]{1,0:T(8,128)(2,1)S(1)} %get-tuple-element.47), channel_id=1, source_target_pairs={{0,5},{1,4},{2,7},{3,6},{4,1},{5,0},{6,3},{7,2},{8,13},{9,12},{10,... | collective-permute-start | bytes 196616 | tf_op jit(solution)/shard_map/ppermute | solution.py:326
  25.8 1.6 %collective-permute-start.14 = (bf16[64,512]{1,0:T(8,128)(2,1)S(1)}, bf16[64,512]{1,0:T(8,128)(2,1)S(1)}, u32[]{:S(2)}, u32[]{:S(2)}) collective-permute-start(bf16[64,512]{1,0:T(8,128)(2,1)S(1)} %get-tuple-element.48), channel_id=1, source_target_pairs={{0,6},{1,7},{2,4},{3,5},{4,2},{5,3},{6,0},{7,1},{8,14},{9,15},{10,... | collective-permute-start | bytes 196616 | tf_op jit(solution)/shard_map/ppermute | solution.py:326
  27.4 1.1 %collective-permute-start.15 = (bf16[64,512]{1,0:T(8,128)(2,1)S(1)}, bf16[64,512]{1,0:T(8,128)(2,1)S(1)}, u32[]{:S(2)}, u32[]{:S(2)}) collective-permute-start(bf16[64,512]{1,0:T(8,128)(2,1)S(1)} %get-tuple-element.49), channel_id=1, source_target_pairs={{0,7},{1,6},{2,5},{3,4},{4,3},{5,2},{6,1},{7,0},{8,15},{9,14},{10,... | collective-permute-start | bytes 196616 | tf_op jit(solution)/shard_map/ppermute | solution.py:326
  29.2 2.0 %collective-permute-done.14.refs_6_ = bf16[64,512]{1,0:T(8,128)(2,1)S(1)} collective-permute-done((bf16[64,512]{1,0:T(8,128)(2,1)S(1)}, bf16[64,512]{1,0:T(8,128)(2,1)S(1)}, u32[]{:S(2)}, u32[]{:S(2)}) %collective-permute-start.14) | collective-permute-done | bytes 65568 | tf_op jit(solution)/shard_map/ppermute | solution.py:326
  31.2 1.1 %collective-permute-done.15.refs_7_ = bf16[64,512]{1,0:T(8,128)(2,1)S(1)} collective-permute-done((bf16[64,512]{1,0:T(8,128)(2,1)S(1)}, bf16[64,512]{1,0:T(8,128)(2,1)S(1)}, u32[]{:S(2)}, u32[]{:S(2)}) %collective-permute-start.15) | collective-permute-done | bytes 65568 | tf_op jit(solution)/shard_map/ppermute | solution.py:326
  32.3 0.9 %shard_map.129 = (bf16[512,128]{1,0:T(8,128)(2,1)S(1)}, bf16[256,512]{1,0:T(8,128)(2,1)S(1)}, bf16[256,512]{1,0:T(8,128)(2,1)S(1)}) custom-call(bf16[64,512]{1,0:T(8,128)(2,1)S(1)} %get-tuple-element.42.refs_0_, bf16[64,512]{1,0:T(8,128)(2,1)S(1)} %collective-permute-done.9.refs_1_, bf16[64,512]{1,0:T(8,128)(2,1)S(1)} %collective-permute-done.10.refs_2_, ...), custom_call_target="tpu_custom_call" | custom-call | tf_op jit(solution)/shard_map/pallas_call | solution.py:151
  33.3 2.1 %shard_map.130 = (bf16[1024,512]{1,0:T(8,128)(2,1)}, bf16[512,512]{1,0:T(8,128)(2,1)S(1)}, bf16[1024,512]{1,0:T(8,128)(2,1)}, bf16[512,512]{1,0:T(8,128)(2,1)S(1)}) custom-call(bf16[256,512]{1,0:T(8,128)(2,1)S(1)} %get-tuple-element.50.back_ref, bf16[256,512]{1,0:T(8,128)(2,1)S(1)} %get-tuple-element.51.grad_ref, bf16[1024,512]{1,0:T(8,128)(2,1)S(1)} %copy-done, ...), custom_call_target="tpu_custom_call" | custom-call | tf_op jit(solution)/shard_map/pallas_call | solution.py:151
  35.9 3.6 %collective-permute-start.21 = (bf16[512,128]{1,0:T(8,128)(2,1)S(1)}, bf16[512,128]{1,0:T(8,128)(2,1)S(1)}, u32[]{:S(2)}, u32[]{:S(2)}) collective-permute-start(bf16[512,128]{1,0:T(8,128)(2,1)S(1)} %get-tuple-element.58.refs_0_), channel_id=1, source_target_pairs={{0,24},{8,16},{16,8},{24,0},{1,25},{9,17},{17,9},{25,1},{2,26},{10... | collective-permute-start | bytes 393224 | tf_op jit(solution)/shard_map/ppermute | solution.py:401
  40.3 3.8 %collective-permute-done.21.refs_1_ = bf16[512,128]{1,0:T(8,128)(2,1)S(1)} collective-permute-done((bf16[512,128]{1,0:T(8,128)(2,1)S(1)}, bf16[512,128]{1,0:T(8,128)(2,1)S(1)}, u32[]{:S(2)}, u32[]{:S(2)}) %collective-permute-start.21) | collective-permute-done | bytes 131104 | tf_op jit(solution)/shard_map/ppermute | solution.py:401
  44.1 3.7 %collective-permute-start.18 = (bf16[512,128]{1,0:T(8,128)(2,1)S(1)}, bf16[512,128]{1,0:T(8,128)(2,1)S(1)}, u32[]{:S(2)}, u32[]{:S(2)}) collective-permute-start(bf16[512,128]{1,0:T(8,128)(2,1)S(1)} %get-tuple-element.56.refs_0_), channel_id=1, source_target_pairs={{0,24},{8,16},{16,8},{24,0},{1,25},{9,17},{17,9},{25,1},{2,26},{10... | collective-permute-start | bytes 393224 | tf_op jit(solution)/shard_map/ppermute | solution.py:401
  47.8 8.1 %collective-permute-done.22.refs_2_ = bf16[512,128]{1,0:T(8,128)(2,1)S(1)} collective-permute-done((bf16[512,128]{1,0:T(8,128)(2,1)S(1)}, bf16[512,128]{1,0:T(8,128)(2,1)S(1)}, u32[]{:S(2)}, u32[]{:S(2)}) %collective-permute-start.22) | collective-permute-done | bytes 131104 | tf_op jit(solution)/shard_map/ppermute | solution.py:401
  55.9 1.6 %collective-permute-start.20 = (bf16[512,128]{1,0:T(8,128)(2,1)S(1)}, bf16[512,128]{1,0:T(8,128)(2,1)S(1)}, u32[]{:S(2)}, u32[]{:S(2)}) collective-permute-start(bf16[512,128]{1,0:T(8,128)(2,1)S(1)} %get-tuple-element.56.refs_0_), channel_id=1, source_target_pairs={{0,8},{8,0},{16,24},{24,16},{1,9},{9,1},{17,25},{25,17},{2,10},{10... | collective-permute-start | bytes 393224 | tf_op jit(solution)/shard_map/ppermute | solution.py:401
  58.3 4.0 %collective-permute-done.19.refs_2_ = bf16[512,128]{1,0:T(8,128)(2,1)S(1)} collective-permute-done((bf16[512,128]{1,0:T(8,128)(2,1)S(1)}, bf16[512,128]{1,0:T(8,128)(2,1)S(1)}, u32[]{:S(2)}, u32[]{:S(2)}) %collective-permute-start.19) | collective-permute-done | bytes 131104 | tf_op jit(solution)/shard_map/ppermute | solution.py:401
  63.5 0.9 %copy-done.13 = bf16[1024,512]{1,0:T(8,128)(2,1)} copy-done((bf16[1024,512]{1,0:T(8,128)(2,1)}, bf16[1024,512]{1,0:T(8,128)(2,1)S(1)}, u32[]{:S(2)}) %copy-start.13) | copy-done | bytes 1048600
  (62 shorter events, 10.0 us)
Async XLA Ops:
  1.9 2.1 %collective-permute-start = (bf16[512,512]{1,0:T(8,128)(2,1)S(1)}, bf16[512,512]{1,0:T(8,128)(2,1)S(1)}, u32[]{:S(2)}, u32[]{:S(2)}) collective-permute-start(bf16[512,512]{1,0:T(8,128)(2,1)S(1)} %constant_dynamic-slice_fusion.1), channel_id=1, source_target_pairs={{0,1},{1,0},{2,3},{3,2},{4,5},{5,4},{6,7},{7,6},{8,9},{9,8},{10,11... | collective-permute-start | bytes 1572872 | tf_op jit(solution)/shard_map/ppermute | solution.py:14
  2.5 2.2 %collective-permute-start.1 = (bf16[512,512]{1,0:T(8,128)(2,1)S(1)}, bf16[512,512]{1,0:T(8,128)(2,1)S(1)}, u32[]{:S(2)}, u32[]{:S(2)}) collective-permute-start(bf16[512,512]{1,0:T(8,128)(2,1)S(1)} %constant_dynamic-slice_fusion), channel_id=1, source_target_pairs={{0,1},{1,0},{2,3},{3,2},{4,5},{5,4},{6,7},{7,6},{8,9},{9,8},{10,11... | collective-permute-start | bytes 1572872 | tf_op jit(solution)/shard_map/ppermute | solution.py:14
  7.1 4.9 %collective-permute-start.2 = (bf16[64,512]{1,0:T(8,128)(2,1)S(1)}, bf16[64,512]{1,0:T(8,128)(2,1)S(1)}, u32[]{:S(2)}, u32[]{:S(2)}) collective-permute-start(bf16[64,512]{1,0:T(8,128)(2,1)S(1)} %get-tuple-element.35), channel_id=1, source_target_pairs={{0,1},{1,0},{2,3},{3,2},{4,5},{5,4},{6,7},{7,6},{8,9},{9,8},{10,11... | collective-permute-start | bytes 196616 | tf_op jit(solution)/shard_map/ppermute | solution.py:326
  7.5 7.1 %collective-permute-start.3 = (bf16[64,512]{1,0:T(8,128)(2,1)S(1)}, bf16[64,512]{1,0:T(8,128)(2,1)S(1)}, u32[]{:S(2)}, u32[]{:S(2)}) collective-permute-start(bf16[64,512]{1,0:T(8,128)(2,1)S(1)} %get-tuple-element.36), channel_id=1, source_target_pairs={{0,2},{1,3},{2,0},{3,1},{4,6},{5,7},{6,4},{7,5},{8,10},{9,11},{10,... | collective-permute-start | bytes 196616 | tf_op jit(solution)/shard_map/ppermute | solution.py:326
  10.2 4.5 %collective-permute-start.4 = (bf16[64,512]{1,0:T(8,128)(2,1)S(1)}, bf16[64,512]{1,0:T(8,128)(2,1)S(1)}, u32[]{:S(2)}, u32[]{:S(2)}) collective-permute-start(bf16[64,512]{1,0:T(8,128)(2,1)S(1)} %get-tuple-element.37), channel_id=1, source_target_pairs={{0,3},{1,2},{2,1},{3,0},{4,7},{5,6},{6,5},{7,4},{8,11},{9,10},{10,... | collective-permute-start | bytes 196616 | tf_op jit(solution)/shard_map/ppermute | solution.py:326
  10.2 4.5 %collective-permute-start.5 = (bf16[64,512]{1,0:T(8,128)(2,1)S(1)}, bf16[64,512]{1,0:T(8,128)(2,1)S(1)}, u32[]{:S(2)}, u32[]{:S(2)}) collective-permute-start(bf16[64,512]{1,0:T(8,128)(2,1)S(1)} %get-tuple-element.38), channel_id=1, source_target_pairs={{0,4},{1,5},{2,6},{3,7},{4,0},{5,1},{6,2},{7,3},{8,12},{9,13},{10,... | collective-permute-start | bytes 196616 | tf_op jit(solution)/shard_map/ppermute | solution.py:326
  11.9 5.5 %collective-permute-start.6 = (bf16[64,512]{1,0:T(8,128)(2,1)S(1)}, bf16[64,512]{1,0:T(8,128)(2,1)S(1)}, u32[]{:S(2)}, u32[]{:S(2)}) collective-permute-start(bf16[64,512]{1,0:T(8,128)(2,1)S(1)} %get-tuple-element.39), channel_id=1, source_target_pairs={{0,5},{1,4},{2,7},{3,6},{4,1},{5,0},{6,3},{7,2},{8,13},{9,12},{10,... | collective-permute-start | bytes 196616 | tf_op jit(solution)/shard_map/ppermute | solution.py:326
  12.0 5.5 %collective-permute-start.7 = (bf16[64,512]{1,0:T(8,128)(2,1)S(1)}, bf16[64,512]{1,0:T(8,128)(2,1)S(1)}, u32[]{:S(2)}, u32[]{:S(2)}) collective-permute-start(bf16[64,512]{1,0:T(8,128)(2,1)S(1)} %get-tuple-element.40), channel_id=1, source_target_pairs={{0,6},{1,7},{2,4},{3,5},{4,2},{5,3},{6,0},{7,1},{8,14},{9,15},{10,... | collective-permute-start | bytes 196616 | tf_op jit(solution)/shard_map/ppermute | solution.py:326
  14.7 5.0 %collective-permute-start.8 = (bf16[64,512]{1,0:T(8,128)(2,1)S(1)}, bf16[64,512]{1,0:T(8,128)(2,1)S(1)}, u32[]{:S(2)}, u32[]{:S(2)}) collective-permute-start(bf16[64,512]{1,0:T(8,128)(2,1)S(1)} %get-tuple-element.41), channel_id=1, source_target_pairs={{0,7},{1,6},{2,5},{3,4},{4,3},{5,2},{6,1},{7,0},{8,15},{9,14},{10,... | collective-permute-start | bytes 196616 | tf_op jit(solution)/shard_map/ppermute | solution.py:326
  22.1 3.7 %collective-permute-start.9 = (bf16[64,512]{1,0:T(8,128)(2,1)S(1)}, bf16[64,512]{1,0:T(8,128)(2,1)S(1)}, u32[]{:S(2)}, u32[]{:S(2)}) collective-permute-start(bf16[64,512]{1,0:T(8,128)(2,1)S(1)} %get-tuple-element.43), channel_id=1, source_target_pairs={{0,1},{1,0},{2,3},{3,2},{4,5},{5,4},{6,7},{7,6},{8,9},{9,8},{10,11... | collective-permute-start | bytes 196616 | tf_op jit(solution)/shard_map/ppermute | solution.py:326
  22.3 5.1 %collective-permute-start.10 = (bf16[64,512]{1,0:T(8,128)(2,1)S(1)}, bf16[64,512]{1,0:T(8,128)(2,1)S(1)}, u32[]{:S(2)}, u32[]{:S(2)}) collective-permute-start(bf16[64,512]{1,0:T(8,128)(2,1)S(1)} %get-tuple-element.44), channel_id=1, source_target_pairs={{0,2},{1,3},{2,0},{3,1},{4,6},{5,7},{6,4},{7,5},{8,10},{9,11},{10,... | collective-permute-start | bytes 196616 | tf_op jit(solution)/shard_map/ppermute | solution.py:326
  22.9 5.6 %collective-permute-start.11 = (bf16[64,512]{1,0:T(8,128)(2,1)S(1)}, bf16[64,512]{1,0:T(8,128)(2,1)S(1)}, u32[]{:S(2)}, u32[]{:S(2)}) collective-permute-start(bf16[64,512]{1,0:T(8,128)(2,1)S(1)} %get-tuple-element.45), channel_id=1, source_target_pairs={{0,3},{1,2},{2,1},{3,0},{4,7},{5,6},{6,5},{7,4},{8,11},{9,10},{10,... | collective-permute-start | bytes 196616 | tf_op jit(solution)/shard_map/ppermute | solution.py:326
  24.0 4.9 %collective-permute-start.12 = (bf16[64,512]{1,0:T(8,128)(2,1)S(1)}, bf16[64,512]{1,0:T(8,128)(2,1)S(1)}, u32[]{:S(2)}, u32[]{:S(2)}) collective-permute-start(bf16[64,512]{1,0:T(8,128)(2,1)S(1)} %get-tuple-element.46), channel_id=1, source_target_pairs={{0,4},{1,5},{2,6},{3,7},{4,0},{5,1},{6,2},{7,3},{8,12},{9,13},{10,... | collective-permute-start | bytes 196616 | tf_op jit(solution)/shard_map/ppermute | solution.py:326
  24.6 4.7 %collective-permute-start.13 = (bf16[64,512]{1,0:T(8,128)(2,1)S(1)}, bf16[64,512]{1,0:T(8,128)(2,1)S(1)}, u32[]{:S(2)}, u32[]{:S(2)}) collective-permute-start(bf16[64,512]{1,0:T(8,128)(2,1)S(1)} %get-tuple-element.47), channel_id=1, source_target_pairs={{0,5},{1,4},{2,7},{3,6},{4,1},{5,0},{6,3},{7,2},{8,13},{9,12},{10,... | collective-permute-start | bytes 196616 | tf_op jit(solution)/shard_map/ppermute | solution.py:326
  25.8 5.4 %collective-permute-start.14 = (bf16[64,512]{1,0:T(8,128)(2,1)S(1)}, bf16[64,512]{1,0:T(8,128)(2,1)S(1)}, u32[]{:S(2)}, u32[]{:S(2)}) collective-permute-start(bf16[64,512]{1,0:T(8,128)(2,1)S(1)} %get-tuple-element.48), channel_id=1, source_target_pairs={{0,6},{1,7},{2,4},{3,5},{4,2},{5,3},{6,0},{7,1},{8,14},{9,15},{10,... | collective-permute-start | bytes 196616 | tf_op jit(solution)/shard_map/ppermute | solution.py:326
  27.4 4.9 %collective-permute-start.15 = (bf16[64,512]{1,0:T(8,128)(2,1)S(1)}, bf16[64,512]{1,0:T(8,128)(2,1)S(1)}, u32[]{:S(2)}, u32[]{:S(2)}) collective-permute-start(bf16[64,512]{1,0:T(8,128)(2,1)S(1)} %get-tuple-element.49), channel_id=1, source_target_pairs={{0,7},{1,6},{2,5},{3,4},{4,3},{5,2},{6,1},{7,0},{8,15},{9,14},{10,... | collective-permute-start | bytes 196616 | tf_op jit(solution)/shard_map/ppermute | solution.py:326
  35.4 28.0 %collective-permute-start.16 = (bf16[512,512]{1,0:T(8,128)(2,1)S(1)}, bf16[512,512]{1,0:T(8,128)(2,1)S(1)}, u32[]{:S(2)}, u32[]{:S(2)}) collective-permute-start(bf16[512,512]{1,0:T(8,128)(2,1)S(1)} %get-tuple-element.53), channel_id=1, source_target_pairs={{0,1},{1,0},{2,3},{3,2},{4,5},{5,4},{6,7},{7,6},{8,9},{9,8},{10,11... | collective-permute-start | bytes 1572872 | tf_op jit(solution)/shard_map/ppermute | solution.py:14
  35.5 27.9 %collective-permute-start.17 = (bf16[512,512]{1,0:T(8,128)(2,1)S(1)}, bf16[512,512]{1,0:T(8,128)(2,1)S(1)}, u32[]{:S(2)}, u32[]{:S(2)}) collective-permute-start(bf16[512,512]{1,0:T(8,128)(2,1)S(1)} %get-tuple-element.55), channel_id=1, source_target_pairs={{0,1},{1,0},{2,3},{3,2},{4,5},{5,4},{6,7},{7,6},{8,9},{9,8},{10,11... | collective-permute-start | bytes 1572872 | tf_op jit(solution)/shard_map/ppermute | solution.py:14
  35.9 8.2 %collective-permute-start.21 = (bf16[512,128]{1,0:T(8,128)(2,1)S(1)}, bf16[512,128]{1,0:T(8,128)(2,1)S(1)}, u32[]{:S(2)}, u32[]{:S(2)}) collective-permute-start(bf16[512,128]{1,0:T(8,128)(2,1)S(1)} %get-tuple-element.58.refs_0_), channel_id=1, source_target_pairs={{0,24},{8,16},{16,8},{24,0},{1,25},{9,17},{17,9},{25,1},{2,26},{10... | collective-permute-start | bytes 393224 | tf_op jit(solution)/shard_map/ppermute | solution.py:401
  39.5 16.4 %collective-permute-start.22 = (bf16[512,128]{1,0:T(8,128)(2,1)S(1)}, bf16[512,128]{1,0:T(8,128)(2,1)S(1)}, u32[]{:S(2)}, u32[]{:S(2)}) collective-permute-start(bf16[512,128]{1,0:T(8,128)(2,1)S(1)} %get-tuple-element.58.refs_0_), channel_id=1, source_target_pairs={{0,16},{8,24},{16,0},{24,8},{1,17},{9,25},{17,1},{25,9},{2,18},{10... | collective-permute-start | bytes 393224 | tf_op jit(solution)/shard_map/ppermute | solution.py:401
  39.5 16.4 %collective-permute-start.23 = (bf16[512,128]{1,0:T(8,128)(2,1)S(1)}, bf16[512,128]{1,0:T(8,128)(2,1)S(1)}, u32[]{:S(2)}, u32[]{:S(2)}) collective-permute-start(bf16[512,128]{1,0:T(8,128)(2,1)S(1)} %get-tuple-element.58.refs_0_), channel_id=1, source_target_pairs={{0,8},{8,0},{16,24},{24,16},{1,9},{9,1},{17,25},{25,17},{2,10},{10... | collective-permute-start | bytes 393224 | tf_op jit(solution)/shard_map/ppermute | solution.py:401
  44.1 14.1 %collective-permute-start.18 = (bf16[512,128]{1,0:T(8,128)(2,1)S(1)}, bf16[512,128]{1,0:T(8,128)(2,1)S(1)}, u32[]{:S(2)}, u32[]{:S(2)}) collective-permute-start(bf16[512,128]{1,0:T(8,128)(2,1)S(1)} %get-tuple-element.56.refs_0_), channel_id=1, source_target_pairs={{0,24},{8,16},{16,8},{24,0},{1,25},{9,17},{17,9},{25,1},{2,26},{10... | collective-permute-start | bytes 393224 | tf_op jit(solution)/shard_map/ppermute | solution.py:401
  55.9 6.4 %collective-permute-start.19 = (bf16[512,128]{1,0:T(8,128)(2,1)S(1)}, bf16[512,128]{1,0:T(8,128)(2,1)S(1)}, u32[]{:S(2)}, u32[]{:S(2)}) collective-permute-start(bf16[512,128]{1,0:T(8,128)(2,1)S(1)} %get-tuple-element.56.refs_0_), channel_id=1, source_target_pairs={{0,16},{8,24},{16,0},{24,8},{1,17},{9,25},{17,1},{25,9},{2,18},{10... | collective-permute-start | bytes 393224 | tf_op jit(solution)/shard_map/ppermute | solution.py:401
  55.9 6.7 %collective-permute-start.20 = (bf16[512,128]{1,0:T(8,128)(2,1)S(1)}, bf16[512,128]{1,0:T(8,128)(2,1)S(1)}, u32[]{:S(2)}, u32[]{:S(2)}) collective-permute-start(bf16[512,128]{1,0:T(8,128)(2,1)S(1)} %get-tuple-element.56.refs_0_), channel_id=1, source_target_pairs={{0,8},{8,0},{16,24},{24,16},{1,9},{9,1},{17,25},{25,17},{2,10},{10... | collective-permute-start | bytes 393224 | tf_op jit(solution)/shard_map/ppermute | solution.py:401
  (14 other events, 86.9 us)

commit v2 on v0

--- a/solution.py
+++ b/solution.py
@@ -3,6 +3,8 @@
 import jax
 import jax.numpy as jnp
 from jax import lax
+from jax.experimental import pallas as pl
+from jax.experimental.pallas import tpu as pltpu
 from jax.sharding import PartitionSpec as P
 
 
@@ -35,7 +37,7 @@
     return mine.reshape(pair_blocks * half_width, tok_count)
 
 
-def shards(tokens, cotangent, up_first, up_second, down_first, down_second, perm_up, perm_down):
+def plain_shards(tokens, cotangent, up_first, up_second, down_first, down_second, perm_up, perm_down):
     wide = jnp.float32
     narrow = jnp.bfloat16
     feature_rows = tokens.shape[0]
@@ -135,6 +137,408 @@
     )
 
 
+VMEM_LIMIT = 16 * 2**20
+
+
+def dot(left, right, left_dim=1, right_dim=0):
+    return lax.dot_general(
+        left, right, (((left_dim,), (right_dim,)), ((), ())), preferred_element_type=jnp.float32
+    )
+
+
+def call(body, outs, *args, scratch=(), micros=0.01, to_hbm=False, aliases=()):
+    whole = pl.BlockSpec(memory_space=pltpu.VMEM)
+    return pl.pallas_call(
+        body,
+        out_shape=outs,
+        in_specs=[whole] * len(args),
+        out_specs=[pl.BlockSpec() if to_hbm else whole] * len(outs),
+        scratch_shapes=list(scratch),
+        input_output_aliases=dict(aliases),
+        compiler_params=pltpu.CompilerParams(vmem_limit_bytes=VMEM_LIMIT),
+        cost_estimate=pl.CostEstimate(
+            flops=int(micros * 1e9), bytes_accessed=int(micros * 3e6), transcendentals=0
+        ),
+    )(*args)
+
+
+def own_first(weights, parity):
+    half = weights.shape[1] // 2
+    return jnp.where(parity == 0, weights, pltpu.roll(weights, half, 1))
+
+
+def one_hot(rows, cols, at):
+    lead = lax.broadcasted_iota(jnp.int32, (rows, cols), 0)
+    lane = lax.broadcasted_iota(jnp.int32, (rows, cols), 1)
+    return at(lead, lane).astype(jnp.bfloat16)
+
+
+def pair_cols(me, chips, rows, cols, turn):
+    mine = chips * cols
+    every = 2 * mine
+
+    def at(lead, lane):
+        chip = (me // 2) ^ ((lane // cols) % chips)
+        col = (2 * chip + ((me % 2) ^ turn)) * cols + lane % cols
+        return lead == (lane // mine) * every + col
+
+    return one_hot(rows * every, rows * mine, at)
+
+
+def sent_order(chips, rows, cols, sent_dim):
+    def at(lead, lane):
+        sent, kept = (lead, lane) if sent_dim == 0 else (lane, lead)
+        q, rest = sent // (cols * 2 * rows), sent % (cols * 2 * rows)
+        b, row = rest // (2 * rows), rest % (2 * rows)
+        return kept == row * (chips * cols) + q * cols + b
+
+    size = 2 * rows * chips * cols
+    return one_hot(size, size, at)
+
+
+def block_rows(own_ref, other_ref, start, half):
+    span = pl.ds(pl.multiple_of(start, half), half)
+    return jnp.concatenate([own_ref[span, :], other_ref[span, :]], 0)
+
+
+def pair_blocks_of(parity, pair_blocks):
+    local = pair_blocks // 2
+    return [(parity if at < local else 1 - parity) * local + at % local for at in range(pair_blocks)]
+
+
+def tables(chips, rows, cols):
+    def body(take_ref, order_ref, back_ref):
+        take_ref[...] = pair_cols(lax.axis_index("loop"), chips, rows, cols, 0)
+        order_ref[...] = sent_order(chips, rows, cols, 0)
+        back_ref[...] = sent_order(chips, rows, cols, 1)
+
+    return body
+
+
+def first_rows(chips, rows, cols, half):
+    narrow = jnp.bfloat16
+
+    def body(*refs):
+        x_refs, d_refs, (take_ref, order_ref), rest = refs[:4], refs[4:8], refs[8:10], refs[10:]
+        outs, (up_out, down_out, hid_ref, grad_ref) = rest[:chips], rest[chips:]
+        parity = lax.axis_index("loop") % 2
+        take, order = take_ref[...], order_ref[...]
+        unit = 2 * rows * cols
+        jobs = ((x_refs, up_out, hid_ref), (d_refs, down_out, grad_ref))
+        for job, ((own_ref, other_ref, *weights), taken_ref, grid_ref) in enumerate(jobs):
+            pair_blocks = own_ref.shape[0] // half
+            taken = [own_first(dot(take, ref[...], 0, 0), parity) for ref in weights]
+            taken_ref[...] = jnp.concatenate(taken, 0).astype(narrow)
+            high = taken_ref.shape[0] // pair_blocks
+            for at, block in enumerate(pair_blocks_of(parity, pair_blocks)):
+                part = slice(at * high, (at + 1) * high)
+                features = block_rows(own_ref, other_ref, block * half, half)
+                grid_ref[part, :] = dot(taken_ref[part, :], features).astype(narrow)
+            sent = dot(order, grid_ref[...]).astype(narrow)
+            for q in range(chips):
+                outs[q][job * unit : (job + 1) * unit, :] = sent[q * unit : (q + 1) * unit]
+
+    return body
+
+
+def one_col(bufs, at, deep):
+    return jnp.concatenate([r[at * deep : (at + 1) * deep, :] for r in bufs], 0)
+
+
+def spread(outs, at, deep, value):
+    for q, out in enumerate(outs):
+        out[at * deep : (at + 1) * deep, :] = value[q * deep : (q + 1) * deep]
+
+
+def columns(chips, rows, cols):
+    narrow = jnp.bfloat16
+    deep = 2 * rows
+
+    def body(*refs):
+        bufs, rest = refs[:chips], refs[chips:]
+        up_ref, down_ref, perm_up_ref, perm_down_ref = rest[:4]
+        outs, rest = rest[4 : 4 + chips], rest[4 + chips :]
+        activated_ref, grad_pre_ref, take_up_ref, take_down_ref = rest
+        me = lax.axis_index("loop")
+        size = chips * deep
+        lead = lax.broadcasted_iota(jnp.int32, (size, size), 0)
+        lane = lax.broadcasted_iota(jnp.int32, (size, size), 1)
+        row = ((lead // rows) ^ me) * rows + lead % rows
+        take_up_ref[...] = (perm_up_ref[...] == row).astype(narrow)
+        take_down_ref[...] = dot(
+            (lane == row).astype(narrow), (perm_down_ref[...] == lead).astype(narrow), 1, 1
+        ).astype(narrow)
+        for b in range(cols):
+            span = slice(b * size, (b + 1) * size)
+            up = dot(up_ref[span, :], take_up_ref[...], 1, 1).astype(narrow)
+            down = dot(take_down_ref[...], down_ref[span, :]).astype(narrow)
+            gelu_val, slope = gelu_parts(dot(up, one_col(bufs, b, deep)))
+            activated = gelu_val.astype(narrow)
+            activated_ref[span, :] = activated
+            spread(outs, b, deep, dot(down, activated).astype(narrow))
+            grad_act = dot(down, one_col(bufs, cols + b, deep), 0, 0)
+            grad_pre = (grad_act * slope).astype(narrow)
+            grad_pre_ref[span, :] = grad_pre
+            spread(outs, cols + b, deep, dot(up, grad_pre, 0, 0).astype(narrow))
+
+    return body
+
+
+def column_grads(chips, rows, cols):
+    narrow = jnp.bfloat16
+    deep = 2 * rows
+
+    def body(*refs):
+        bufs = refs[:chips]
+        activated_ref, grad_pre_ref, take_up_ref, take_down_ref, out_ref = refs[chips:]
+        size = chips * deep
+        for b in range(cols):
+            span = slice(b * size, (b + 1) * size)
+            hid = one_col(bufs, b, deep)
+            grad = one_col(bufs, cols + b, deep)
+            g_up = dot(grad_pre_ref[span, :], hid, 1, 1).astype(narrow)
+            g_down = dot(grad, activated_ref[span, :], 1, 1).astype(narrow)
+            out_ref[span, :] = dot(g_up, take_up_ref[...]).astype(narrow)
+            out_ref[cols * size + b * size : cols * size + (b + 1) * size, :] = dot(
+                take_down_ref[...], g_down, 0, 0
+            ).astype(narrow)
+
+    return body
+
+
+def row_grads(chips, rows, cols, half):
+    narrow = jnp.bfloat16
+
+    def body(*refs):
+        bufs, (tok_ref, x_ref, cot_ref, d_ref, order_ref) = refs[:chips], refs[chips : chips + 5]
+        kept_ref, leave_ref, back_ref, grad_ref = refs[-4:]
+        parity = lax.axis_index("loop") % 2
+        pair_blocks = tok_ref.shape[0] // half
+        unit = 2 * rows * cols
+        jobs = ((1, grad_ref, tok_ref, x_ref), (0, back_ref, cot_ref, d_ref))
+        for at, (job, grid_ref, own_ref, other_ref) in enumerate(jobs):
+            sent = one_col(bufs, job, unit)
+            grid_ref[...] = dot(order_ref[...], sent).astype(narrow)
+            high = grid_ref.shape[0] // pair_blocks
+            grads = []
+            for place, block in enumerate(pair_blocks_of(parity, pair_blocks)):
+                part = slice(place * high, (place + 1) * high)
+                features = block_rows(own_ref, other_ref, block * half, half)
+                grads.append(dot(grid_ref[part, :], features, 1, 1))
+            both = own_first(jnp.concatenate(grads, 0), parity).astype(narrow)
+            size = both.shape[0] // 2
+            kept_ref[at * size : (at + 1) * size, :] = both[:size]
+            leave_ref[at * size : (at + 1) * size, :] = both[size:]
+
+    return body
+
+
+def join(kept_ref, came_ref, left_ref, right_ref, *rest):
+    out_ref, with_ref = rest[-4:-2]
+    size = kept_ref.shape[0] // 2
+    for at in range(2):
+        span = slice(at * size, (at + 1) * size)
+        for off, ref in enumerate((kept_ref, came_ref)):
+            to = slice((2 * at + off) * size, (2 * at + off + 1) * size)
+            out_ref[to, :] = ref[span, :]
+            with_ref[to, :] = ref[span, :]
+    total = left_ref[...].astype(jnp.float32) + right_ref[...].astype(jnp.float32)
+    with_ref[4 * size :, :] = total.astype(with_ref.dtype)
+
+
+def row_outputs(half):
+    def body(*refs):
+        jobs, outs = (refs[:3], refs[3:6]), refs[6:]
+        parity = lax.axis_index("loop") % 2
+        for at, (grid_ref, own_ref, weights_ref) in enumerate(jobs):
+            kept_ref, sent_ref = outs[2 * at : 2 * at + 2]
+            pair_blocks = own_ref.shape[0] // half
+            high = weights_ref.shape[0] // pair_blocks
+            for place, block in enumerate(pair_blocks_of(parity, pair_blocks)):
+                part = slice(place * high, (place + 1) * high)
+                span = pl.ds(pl.multiple_of(block * half, half), half)
+                branch = dot(weights_ref[part, :], grid_ref[part, :], 0, 0)
+                kept_ref[span, :] = own_ref[span, :].astype(jnp.float32) + branch[:half]
+                sent_ref[span, :] = branch[half:].astype(jnp.bfloat16)
+
+    return body
+
+
+def add_partner(*refs):
+    jobs, done_ref = ((refs[0], refs[1], refs[4]), (refs[2], refs[3], refs[5])), refs[6]
+    for kept, got, out in jobs:
+        out[...] = (kept[...] + got[...].astype(jnp.float32)).astype(out.dtype)
+    done_ref[...] = jnp.zeros_like(done_ref)
+
+
+def total_grads(chips, rows, cols, dps, scale):
+    def body(*refs):
+        parts, outs = refs[:dps], refs[-4:]
+        both_ref, got_ref = refs[0], refs[dps - 1]
+        me = lax.axis_index("loop")
+        place = jnp.concatenate([pair_cols(me, chips, rows, cols, turn) for turn in (0, 1)], 1)
+        place = jnp.concatenate([place] * dps, 1)
+        size = outs[0].shape[0]
+        for at, out in enumerate(outs[:2]):
+            span = slice(at * size, (at + 1) * size)
+            out[...] = dot(place, jnp.concatenate([r[span, :] for r in parts], 0)) * scale
+        size = outs[2].shape[0]
+        for at, out in enumerate(outs[2:]):
+            span = slice(2 * outs[0].shape[0] + at * size, 2 * outs[0].shape[0] + (at + 1) * size)
+            both = both_ref[span, :].astype(jnp.float32) + got_ref[span, :].astype(jnp.float32)
+            out[...] = both * scale
+
+    return body
+
+
+def exchange(bufs, axis):
+    count = 2 * len(bufs)
+    got = {
+        q: lax.ppermute(bufs[q], axis, [(s, s ^ (2 * q)) for s in range(count)])
+        for q in range(len(bufs) - 1, 0, -1)
+    }
+    return [bufs[0]] + [got[q] for q in range(1, len(bufs))]
+
+
+def shards(tokens, cotangent, up_first, up_second, down_first, down_second, perm_up, perm_down):
+    narrow = jnp.bfloat16
+    wide = jnp.float32
+    loops, dps = lax.axis_size("loop"), lax.axis_size("dp")
+    feature_rows, toks = tokens.shape
+    rows, all_cols, block = up_first.shape
+    cols, size = up_second.shape[:2]
+    half = block // 2
+    pair_blocks = feature_rows // half
+    if loops != 8 or dps != 4 or rows % 16 or pair_blocks % 2 or 2 * rows * cols * loops // 2 % (16 * pair_blocks):
+        return plain_shards(
+            tokens, cotangent, up_first, up_second, down_first, down_second, perm_up, perm_down
+        )
+    chips = loops // 2
+
+    def struct(lead, width, dtype=narrow):
+        return jax.ShapeDtypeStruct((lead, width), dtype)
+
+    up_rows = up_first.reshape(rows * all_cols, block)
+    down_rows = down_second.reshape(rows * all_cols, block)
+    other_x = from_partner(tokens, "loop", 0)
+    other_up = from_partner(up_rows, "loop", 0)
+    other_d = from_partner(cotangent, "loop", 0)
+    other_down = from_partner(down_rows, "loop", 0)
+    grid_rows = 2 * rows * chips * cols
+    buf = struct(4 * rows * cols, toks)
+    grid = struct(grid_rows, toks)
+    taken = struct(grid_rows, block)
+    take, order, order_back = call(
+        tables(chips, rows, cols),
+        [struct(rows * all_cols, rows * chips * cols)] + [struct(grid_rows, grid_rows)] * 2,
+        micros=4,
+    )
+    *sent, up_taken, down_taken = call(
+        first_rows(chips, rows, cols, half),
+        [buf] * chips + [taken] * 2,
+        tokens,
+        other_x,
+        up_rows,
+        other_up,
+        cotangent,
+        other_d,
+        down_rows,
+        other_down,
+        take,
+        order,
+        scratch=[pltpu.VMEM(grid.shape, narrow)] * 2,
+    )
+    cells = exchange(sent, "loop")
+    square = struct(cols * size, size)
+    *sent, activated, grad_pre, take_up, take_down = call(
+        columns(chips, rows, cols),
+        [buf] * chips + [grid] * 2 + [struct(size, size)] * 2,
+        *cells,
+        up_second.reshape(square.shape),
+        down_first.reshape(square.shape),
+        perm_up.reshape(1, size),
+        perm_down.reshape(1, size),
+    )
+    back = exchange(sent, "loop")
+    (col_grads,) = call(
+        column_grads(chips, rows, cols),
+        [struct(2 * cols * size, size)],
+        *cells,
+        activated,
+        grad_pre,
+        take_up,
+        take_down,
+    )
+
+    def over_dp(value, apart):
+        return lax.ppermute(value, "dp", [(s, s ^ apart) for s in range(dps)])
+
+    col_got = over_dp(col_grads, dps - 1)
+    kept, leaving, back_rows, grad_rows = call(
+        row_grads(chips, rows, cols, half),
+        [taken] * 2 + [grid] * 2,
+        *back,
+        tokens,
+        other_x,
+        cotangent,
+        other_d,
+        order_back,
+        col_grads,
+    )
+    came = from_partner(leaving, "loop", 0)
+    partial = struct(feature_rows, toks, wide)
+    full = struct(feature_rows, toks)
+    mixed, mixed_send, grad_tokens, grad_send = call(
+        row_outputs(half),
+        [partial, full] * 2,
+        back_rows,
+        tokens,
+        down_taken,
+        grad_rows,
+        cotangent,
+        up_taken,
+    )
+    sums, sums_more, mixed_send, grad_send = call(
+        join,
+        [struct(2 * grid_rows, block), struct(2 * grid_rows + 2 * cols * size, block), full, full],
+        kept,
+        came,
+        col_grads,
+        col_got,
+        mixed_send,
+        grad_send,
+        aliases=((4, 2), (5, 3)),
+    )
+    parts = [sums_more] + [
+        over_dp(sums if apart > 1 else sums_more, apart) for apart in range(dps - 1, 0, -1)
+    ]
+    mixed, grad_tokens, done = call(
+        add_partner,
+        [full] * 2 + [struct(8, 128, wide)],
+        mixed,
+        from_partner(mixed_send, "loop", 0),
+        grad_tokens,
+        from_partner(grad_send, "loop", 0),
+        to_hbm=True,
+    )
+    scale = 1.0 / math.sqrt(dps * toks)
+    g_up_first, g_down_second, g_up_second, g_down_first = call(
+        total_grads(chips, rows, cols, dps, scale),
+        [struct(rows * all_cols, block, wide)] * 2 + [struct(*square.shape, wide)] * 2,
+        *parts,
+        done,
+        to_hbm=True,
+    )
+    return (
+        mixed,
+        grad_tokens,
+        g_up_first.reshape(up_first.shape),
+        g_up_second.reshape(up_second.shape),
+        g_down_first.reshape(down_first.shape),
+        g_down_second.reshape(down_second.shape),
+    )
+
+
 def solution(mesh):
     in_specs = (
         P("loop", "dp"),

time: 177 us -> 49.2 us (0.28)
  local copies, waits for them, and re-layouts: 45.1 us -> 0.04 us
  matrix products: 33.8 us -> 0 us
  other arithmetic: 25.6 us -> 0 us
  waiting for transfers between devices: 38.2 us -> 21.3 us
  between operations: 14.4 us -> 0.79 us
  Pallas kernels: 0 us -> 9.26 us
    dot_general x16 -> x0, matrix products: 33.8 us -> none  [the longest x1 4.39 us: shards(): jnp.einsum('am,aot->mot', picker_wide, out_rows, precision=lax.Precision....]
    psum x1 -> x0, waiting for transfers between devices: 30.8 us -> none  [shards(): lax.psum(g_up_first.astype(jnp.bfloat16), 'dp').astype(jnp.float32)]
    ppermute x0 -> x10, waiting for transfers between devices: none -> 17.8 us  [the longest x4 10.6 us: over_dp(): return lax.ppermute(value, 'dp', [(s, s ^ apart) for s in range(dps)])]
    all_to_all x4 -> x0, starting transfers between devices: 17.5 us -> none  [the longest x1 5.15 us: shards(): lax.all_to_all(hidden_one, 'loop', split_axis=1, concat_axis=0, tiled=True)]
    ppermute x0 -> x10, starting transfers between devices: none -> 15.8 us  [the longest x6 8.02 us: exchange(): lax.ppermute(bufs[q], axis, [(s, s ^ 2 * q) for s in range(count)])]
    dot_general x2 -> x0, local copies, waits for them, and re-layouts: 11 us -> none  [the longest x1 5.49 us: shards(): jnp.einsum('abi,abt->ait', up_first, grad_hidden, preferred_element_type=...]
    select_n x10 -> x0, other arithmetic: 9.89 us -> none  [the longest x2 2.35 us: shards(): leaving = jnp.take(mixed_cols, perm_down, axis=0)]
    pallas_call x0 -> x9, Pallas kernels: none -> 9.26 us  [call(): pl.pallas_call(body, out_shape=outs, in_specs=[whole] * len(args), out_sp...]
  transfers between devices with their start and end apart: 9 -> 17, of which waited for: 3 -> 7; matrix products, arithmetic and copies ran while one was open for 29% -> 0% of each run, Pallas kernels for 0% -> 11%
where the time goes in v2:
time: 49.2 us; the launch traced here: 49 us
  waiting for transfers between devices  21.3 us (43%)
  starting transfers between devices  17.7 us (36%)
  Pallas kernels  9.26 us (19%)
  between operations  0.79 us (2%)
    ppermute x4, waiting for transfers between devices, over_dp(): return lax.ppermute(value, 'dp', [(s, s ^ apart) for s in range(dps)])  10.6 us
    pallas_call x9, Pallas kernels, call(): pl.pallas_call(body, out_shape=outs, in_specs=[whole] * len(args), out_sp...  9.26 us
    ppermute x6, starting transfers between devices, exchange(): lax.ppermute(bufs[q], axis, [(s, s ^ 2 * q) for s in range(count)])  8.02 us
    ppermute x4, starting transfers between devices, over_dp(): return lax.ppermute(value, 'dp', [(s, s ^ apart) for s in range(dps)])  7.81 us
    ppermute x6, waiting for transfers between devices, exchange(): lax.ppermute(bufs[q], axis, [(s, s ^ 2 * q) for s in range(count)])  7.25 us
    ppermute x7, waiting for transfers between devices, from_partner(): return lax.ppermute(value, axis, pairs)  3.42 us
    ppermute x7, starting transfers between devices, from_partner(): return lax.ppermute(value, axis, pairs)  1.84 us
  transfers between devices with their start and end apart: 17, of which 7 were waited for; matrix products, arithmetic and copies ran while one was open for 0% of the time, Pallas kernels for 11%

profile of v2, /device:TPU:0, one launch (start us, length us, event | category | flops | bytes accessed | tf_op | source)
XLA Modules:
  0.0 49.0 jit_solution(13123925486896936659)
XLA Ops:
  0.6 0.5 %collective-permute-start = (bf16[1024,512]{1,0:T(8,128)(2,1)}, bf16[1024,512]{1,0:T(8,128)(2,1)S(1)}, u32[]{:S(2)}, u32[]{:S(2)}) collective-permute-start(bf16[1024,512]{1,0:T(8,128)(2,1)} %refs_1_.1), channel_id=1, source_target_pairs={{0,1},{1,0},{2,3},{3,2},{4,5},{5,4},{6,7},{7,6},{8,9},{9,8},{10,11... | collective-permute-start | bytes 3145736 | tf_op jit(solution)/shard_map/ppermute | solution.py:14
  1.2 0.4 collective-permute-start.1
  1.9 3.3 %collective-permute-done.1.refs_3_ = bf16[256,128]{1,0:T(8,128)(2,1)S(1)} collective-permute-done((bf16[256,128]{1,0:T(8,128)(2,1)}, bf16[256,128]{1,0:T(8,128)(2,1)S(1)}, u32[]{:S(2)}, u32[]{:S(2)}) %collective-permute-start.1) | collective-permute-done | bytes 65568 | tf_op jit(solution)/shard_map/ppermute | solution.py:14
  5.4 1.5 %shard_map.128 = (bf16[128,512]{1,0:T(8,128)(2,1)S(1)}, bf16[128,512]{1,0:T(8,128)(2,1)S(1)}, bf16[128,512]{1,0:T(8,128)(2,1)S(1)}, bf16[128,512]{1,0:T(8,128)(2...) custom-call(bf16[1024,512]{1,0:T(8,128)(2,1)S(1)} %copy-done, ...), custom_call_target="tpu_custom_call" | custom-call | flops 10000000 | bytes 30000 | tf_op jit(solution)/shard_map/pallas_call | solution.py:151
  6.9 2.9 %collective-permute-start.4 = (bf16[128,512]{1,0:T(8,128)(2,1)S(1)}, bf16[128,512]{1,0:T(8,128)(2,1)S(1)}, u32[]{:S(2)}, u32[]{:S(2)}) collective-permute-start(bf16[128,512]{1,0:T(8,128)(2,1)S(1)} %get-tuple-element.45), channel_id=1, source_target_pairs={{0,2},{1,3},{2,0},{3,1},{4,6},{5,7},{6,4},{7,5},{8,10},{9,11},{10,... | collective-permute-start | bytes 393224 | tf_op jit(solution)/shard_map/ppermute | solution.py:397
  9.8 1.5 %collective-permute-start.5 = (bf16[128,512]{1,0:T(8,128)(2,1)S(1)}, bf16[128,512]{1,0:T(8,128)(2,1)S(1)}, u32[]{:S(2)}, u32[]{:S(2)}) collective-permute-start(bf16[128,512]{1,0:T(8,128)(2,1)S(1)} %get-tuple-element.46), channel_id=1, source_target_pairs={{0,4},{1,5},{2,6},{3,7},{4,0},{5,1},{6,2},{7,3},{8,12},{9,13},{10,... | collective-permute-start | bytes 393224 | tf_op jit(solution)/shard_map/ppermute | solution.py:397
  11.4 2.4 %collective-permute-done.4.refs_1_ = bf16[128,512]{1,0:T(8,128)(2,1)S(1)} collective-permute-done((bf16[128,512]{1,0:T(8,128)(2,1)S(1)}, bf16[128,512]{1,0:T(8,128)(2,1)S(1)}, u32[]{:S(2)}, u32[]{:S(2)}) %collective-permute-start.4) | collective-permute-done | bytes 131104 | tf_op jit(solution)/shard_map/ppermute | solution.py:397
  13.7 4.2 %collective-permute-done.5.refs_2_ = bf16[128,512]{1,0:T(8,128)(2,1)S(1)} collective-permute-done((bf16[128,512]{1,0:T(8,128)(2,1)S(1)}, bf16[128,512]{1,0:T(8,128)(2,1)S(1)}, u32[]{:S(2)}, u32[]{:S(2)}) %collective-permute-start.5) | collective-permute-done | bytes 131104 | tf_op jit(solution)/shard_map/ppermute | solution.py:397
  17.9 1.3 %shard_map.129 = (bf16[128,512]{1,0:T(8,128)(2,1)S(1)}, bf16[128,512]{1,0:T(8,128)(2,1)S(1)}, bf16[128,512]{1,0:T(8,128)(2,1)S(1)}, bf16[128,512]{1,0:T(8,128)(2...) custom-call(bf16[128,512]{1,0:T(8,128)(2,1)S(1)} %get-tuple-element., ...), custom_call_target="tpu_custom_call" | custom-call | flops 10000000 | bytes 30000 | tf_op jit(solution)/shard_map/pallas_call | solution.py:151
  19.3 1.3 %collective-permute-start.7 = (bf16[128,512]{1,0:T(8,128)(2,1)S(1)}, bf16[128,512]{1,0:T(8,128)(2,1)S(1)}, u32[]{:S(2)}, u32[]{:S(2)}) collective-permute-start(bf16[128,512]{1,0:T(8,128)(2,1)S(1)} %get-tuple-element.49), channel_id=1, source_target_pairs={{0,2},{1,3},{2,0},{3,1},{4,6},{5,7},{6,4},{7,5},{8,10},{9,11},{10,... | collective-permute-start | bytes 393224 | tf_op jit(solution)/shard_map/ppermute | solution.py:397
  20.6 0.8 %collective-permute-start.8 = (bf16[128,512]{1,0:T(8,128)(2,1)S(1)}, bf16[128,512]{1,0:T(8,128)(2,1)S(1)}, u32[]{:S(2)}, u32[]{:S(2)}) collective-permute-start(bf16[128,512]{1,0:T(8,128)(2,1)S(1)} %get-tuple-element.50), channel_id=1, source_target_pairs={{0,4},{1,5},{2,6},{3,7},{4,0},{5,1},{6,2},{7,3},{8,12},{9,13},{10,... | collective-permute-start | bytes 393224 | tf_op jit(solution)/shard_map/ppermute | solution.py:397
  21.4 1.4 %collective-permute-start.9 = (bf16[128,512]{1,0:T(8,128)(2,1)S(1)}, bf16[128,512]{1,0:T(8,128)(2,1)S(1)}, u32[]{:S(2)}, u32[]{:S(2)}) collective-permute-start(bf16[128,512]{1,0:T(8,128)(2,1)S(1)} %get-tuple-element.51), channel_id=1, source_target_pairs={{0,6},{1,7},{2,4},{3,5},{4,2},{5,3},{6,0},{7,1},{8,14},{9,15},{10,... | collective-permute-start | bytes 393224 | tf_op jit(solution)/shard_map/ppermute | solution.py:397
  22.8 0.6 %shard_map.130.refs_9_.left_ref = bf16[512,128]{1,0:T(8,128)(2,1)S(1)} custom-call(bf16[128,512]{1,0:T(8,128)(2,1)S(1)} %get-tuple-element.44.refs_0_, bf16[128,512]{1,0:T(8,128)(2,1)S(1)} %collective-permute-done.4.refs_1_, bf16[128,512]{1,0:T(8,128)(2,1)S(1)} %collective-permute-done.5.refs_2_, bf16[128,512]{1,0:T(8,128)(2,1)S(1)} %collective-permute-done.6.refs_3_, ...), custom_call_target="tpu_custom_call" | custom-call | flops 10000000 | bytes 30000 | tf_op jit(solution)/shard_map/pallas_call | solution.py:151
  23.4 3.7 %collective-permute-start.11 = (bf16[512,128]{1,0:T(8,128)(2,1)S(1)}, bf16[512,128]{1,0:T(8,128)(2,1)S(1)}, u32[]{:S(2)}, u32[]{:S(2)}) collective-permute-start(bf16[512,128]{1,0:T(8,128)(2,1)S(1)} %shard_map.130.refs_9_.left_ref), channel_id=1, source_target_pairs={{0,24},{8,16},{16,8},{24,0},{1,25},{9,17},{17,9},{25,1},{2,26},{10... | collective-permute-start | bytes 393224 | tf_op jit(solution)/shard_map/ppermute | solution.py:474
  27.1 0.7 %collective-permute-done.8.refs_2_ = bf16[128,512]{1,0:T(8,128)(2,1)S(1)} collective-permute-done((bf16[128,512]{1,0:T(8,128)(2,1)S(1)}, bf16[128,512]{1,0:T(8,128)(2,1)S(1)}, u32[]{:S(2)}, u32[]{:S(2)}) %collective-permute-start.8) | collective-permute-done | bytes 131104 | tf_op jit(solution)/shard_map/ppermute | solution.py:397
  27.8 1.5 %shard_map.131 = (bf16[256,128]{1,0:T(8,128)(2,1)S(1)}, bf16[256,128]{1,0:T(8,128)(2,1)S(1)}, bf16[256,512]{1,0:T(8,128)(2,1)S(1)}, bf16[256,512]{1,0:T(8,128)(2,1)S(1)}) custom-call(bf16[128,512]{1,0:T(8,128)(2,1)S(1)} %get-tuple-element.48.refs_0_, bf16[128,512]{1,0:T(8,128)(2,1)S(1)} %collective-permute-done.7.refs_1_, ...), custom_call_target="tpu_custom_call" | custom-call | flops 10000000 | bytes 30000 | tf_op jit(solution)/shard_map/pallas_call | solution.py:151
  29.4 1.3 %shard_map.132 = (f32[1024,512]{1,0:T(8,128)S(1)}, bf16[1024,512]{1,0:T(8,128)(2,1)S(1)}, f32[1024,512]{1,0:T(8,128)S(1)}, bf16[1024,512]{1,0:T(8,128)(2,1)S(1)}) custom-call(bf16[256,512]{1,0:T(8,128)(2,1)S(1)} %get-tuple-element.57.refs_0_, bf16[1024,512]{1,0:T(8,128)(2,1)S(1)} %copy-done, bf16[256,128]{1,0:T(8,128)(2,1)S(1)} %get-tuple-element.58.refs_2_, ...), custom_call_target="tpu_custom_call" | custom-call | flops 10000000 | bytes 30000 | tf_op jit(solution)/shard_map/pallas_call | solution.py:151
  30.8 0.6 %collective-permute-start.12 = (bf16[1024,512]{1,0:T(8,128)(2,1)S(1)}, bf16[1024,512]{1,0:T(8,128)(2,1)S(1)}, u32[]{:S(2)}, u32[]{:S(2)}) collective-permute-start(bf16[1024,512]{1,0:T(8,128)(2,1)S(1)} %get-tuple-element.66), channel_id=1, source_target_pairs={{0,1},{1,0},{2,3},{3,2},{4,5},{5,4},{6,7},{7,6},{8,9},{9,8},{10,11... | collective-permute-start | bytes 3145736 | tf_op jit(solution)/shard_map/ppermute | solution.py:14
  31.4 1.6 %collective-permute-start.16 = (bf16[1024,128]{1,0:T(8,128)(2,1)S(1)}, bf16[1024,128]{1,0:T(8,128)(2,1)S(1)}, u32[]{:S(2)}, u32[]{:S(2)}) collective-permute-start(bf16[1024,128]{1,0:T(8,128)(2,1)S(1)} %get-tuple-element.71.refs_0_), channel_id=1, source_target_pairs={{0,8},{8,0},{16,24},{24,16},{1,9},{9,1},{17,25},{25,17},{2,10},{10... | collective-permute-start | bytes 786440 | tf_op jit(solution)/shard_map/ppermute | solution.py:474
  33.0 2.5 %collective-permute-start.14 = (bf16[512,128]{1,0:T(8,128)(2,1)S(1)}, bf16[512,128]{1,0:T(8,128)(2,1)S(1)}, u32[]{:S(2)}, u32[]{:S(2)}) collective-permute-start(bf16[512,128]{1,0:T(8,128)(2,1)S(1)} %get-tuple-element.72), channel_id=1, source_target_pairs={{0,24},{8,16},{16,8},{24,0},{1,25},{9,17},{17,9},{25,1},{2,26},{10... | collective-permute-start | bytes 393224 | tf_op jit(solution)/shard_map/ppermute | solution.py:474
  35.6 1.7 %shard_map.134 = (bf16[1024,512]{1,0:T(8,128)(2,1)}, bf16[1024,512]{1,0:T(8,128)(2,1)}, f32[8,128]{1,0:T(8,128)S(1)}) custom-call(f32[1024,512]{1,0:T(8,128)S(1)} %get-tuple-element.61.refs_0_, bf16[1024,512]{1,0:T(8,128)(2,1)S(1)} %collective-permute-done.12.refs_1_, f32[1024,512]{1,0:T(8,128)S(1)} %get-tuple-element.67.refs_2_, ...), custom_call_target="tpu_custom_call" | custom-call | flops 10000000 | bytes 30000 | tf_op jit(solution)/shard_map/pallas_call | solution.py:151
  37.3 8.2 %collective-permute-done.14.refs_1_ = bf16[512,128]{1,0:T(8,128)(2,1)S(1)} collective-permute-done((bf16[512,128]{1,0:T(8,128)(2,1)S(1)}, bf16[512,128]{1,0:T(8,128)(2,1)S(1)}, u32[]{:S(2)}, u32[]{:S(2)}) %collective-permute-start.14) | collective-permute-done | bytes 131104 | tf_op jit(solution)/shard_map/ppermute | solution.py:474
  45.4 2.4 %collective-permute-done.15.refs_2_ = bf16[512,128]{1,0:T(8,128)(2,1)S(1)} collective-permute-done((bf16[512,128]{1,0:T(8,128)(2,1)S(1)}, bf16[512,128]{1,0:T(8,128)(2,1)S(1)}, u32[]{:S(2)}, u32[]{:S(2)}) %collective-permute-start.15) | collective-permute-done | bytes 131104 | tf_op jit(solution)/shard_map/ppermute | solution.py:474
  47.8 1.2 %shard_map.135 = (f32[256,128]{1,0:T(8,128)}, f32[256,128]{1,0:T(8,128)}, f32[256,128]{1,0:T(8,128)}, f32[256,128]{1,0:T(8,128)}) custom-call(bf16[1024,128]{1,0:T(8,128)(2,1)S(1)} %get-tuple-element.71.refs_0_, bf16[512,128]{1,0:T(8,128)(2,1)S(1)} %collective-permute-done.14.refs_1_, bf16[512,128]{1,0:T(8,128)(2,1)S(1)} %collective-permute-done.15.refs_2_, ...), custom_call_target="tpu_custom_call" | custom-call | flops 10000000 | bytes 30000 | tf_op jit(solution)/shard_map/pallas_call | solution.py:151
  (35 shorter events, 0.8 us)
Async XLA Ops:
  0.6 4.7 %collective-permute-start = (bf16[1024,512]{1,0:T(8,128)(2,1)}, bf16[1024,512]{1,0:T(8,128)(2,1)S(1)}, u32[]{:S(2)}, u32[]{:S(2)}) collective-permute-start(bf16[1024,512]{1,0:T(8,128)(2,1)} %refs_1_.1), channel_id=1, source_target_pairs={{0,1},{1,0},{2,3},{3,2},{4,5},{5,4},{6,7},{7,6},{8,9},{9,8},{10,11... | collective-permute-start | bytes 3145736 | tf_op jit(solution)/shard_map/ppermute | solution.py:14
  1.2 4.2 %collective-permute-start.2 = (bf16[1024,512]{1,0:T(8,128)(2,1)}, bf16[1024,512]{1,0:T(8,128)(2,1)S(1)}, u32[]{:S(2)}, u32[]{:S(2)}) collective-permute-start(bf16[1024,512]{1,0:T(8,128)(2,1)} %refs_4_.5), channel_id=1, source_target_pairs={{0,1},{1,0},{2,3},{3,2},{4,5},{5,4},{6,7},{7,6},{8,9},{9,8},{10,11... | collective-permute-start | bytes 3145736 | tf_op jit(solution)/shard_map/ppermute | solution.py:14
  1.2 4.0 %collective-permute-start.1 = (bf16[256,128]{1,0:T(8,128)(2,1)}, bf16[256,128]{1,0:T(8,128)(2,1)S(1)}, u32[]{:S(2)}, u32[]{:S(2)}) collective-permute-start(bf16[256,128]{1,0:T(8,128)(2,1)} %bitcast.10), channel_id=1, source_target_pairs={{0,1},{1,0},{2,3},{3,2},{4,5},{5,4},{6,7},{7,6},{8,9},{9,8},{10,11... | collective-permute-start | bytes 196616 | tf_op jit(solution)/shard_map/ppermute | solution.py:14
  1.7 3.7 %copy-start.1 = (bf16[1024,512]{1,0:T(8,128)(2,1)S(1)}, bf16[1024,512]{1,0:T(8,128)(2,1)}, u32[]{:S(2)}) copy-start(bf16[1024,512]{1,0:T(8,128)(2,1)} %refs_4_.5) | copy-start | bytes 3145732
  1.7 3.7 %copy-start.2 = (bf16[16,16,128]{2,1,0:T(8,128)(2,1)S(1)}, bf16[16,16,128]{2,1,0:T(8,128)(2,1)}, u32[]{:S(2)}) copy-start(bf16[16,16,128]{2,1,0:T(8,128)(2,1)} %param.10) | copy-start | bytes 196612
  1.7 3.7 %copy-start.3 = (bf16[16,16,128]{2,1,0:T(8,128)(2,1)S(1)}, bf16[16,16,128]{2,1,0:T(8,128)(2,1)}, u32[]{:S(2)}) copy-start(bf16[16,16,128]{2,1,0:T(8,128)(2,1)} %param.13) | copy-start | bytes 196612
  1.7 3.7 %collective-permute-start.3 = (bf16[256,128]{1,0:T(8,128)(2,1)}, bf16[256,128]{1,0:T(8,128)(2,1)S(1)}, u32[]{:S(2)}, u32[]{:S(2)}) collective-permute-start(bf16[256,128]{1,0:T(8,128)(2,1)} %bitcast.12), channel_id=1, source_target_pairs={{0,1},{1,0},{2,3},{3,2},{4,5},{5,4},{6,7},{7,6},{8,9},{9,8},{10,11... | collective-permute-start | bytes 196616 | tf_op jit(solution)/shard_map/ppermute | solution.py:14
  5.4 12.5 %copy-start.4 = (bf16[2,128,128]{2,1,0:T(8,128)(2,1)S(1)}, bf16[2,128,128]{2,1,0:T(8,128)(2,1)}, u32[]{:S(2)}) copy-start(bf16[2,128,128]{2,1,0:T(8,128)(2,1)} %param.11) | copy-start | bytes 196612
  5.4 12.5 %copy-start.5 = (bf16[2,128,128]{2,1,0:T(8,128)(2,1)S(1)}, bf16[2,128,128]{2,1,0:T(8,128)(2,1)}, u32[]{:S(2)}) copy-start(bf16[2,128,128]{2,1,0:T(8,128)(2,1)} %param.12) | copy-start | bytes 196612
  5.4 12.5 %copy-start.6 = (s32[128]{0:T(128)S(1)}, s32[128]{0:T(128)}, u32[]{:S(2)}) copy-start(s32[128]{0:T(128)} %param.14) | copy-start | bytes 1540
  5.4 12.5 %copy-start.7 = (s32[128]{0:T(128)S(1)}, s32[128]{0:T(128)}, u32[]{:S(2)}) copy-start(s32[128]{0:T(128)} %param.15) | copy-start | bytes 1540
  6.9 6.8 %collective-permute-start.4 = (bf16[128,512]{1,0:T(8,128)(2,1)S(1)}, bf16[128,512]{1,0:T(8,128)(2,1)S(1)}, u32[]{:S(2)}, u32[]{:S(2)}) collective-permute-start(bf16[128,512]{1,0:T(8,128)(2,1)S(1)} %get-tuple-element.45), channel_id=1, source_target_pairs={{0,2},{1,3},{2,0},{3,1},{4,6},{5,7},{6,4},{7,5},{8,10},{9,11},{10,... | collective-permute-start | bytes 393224 | tf_op jit(solution)/shard_map/ppermute | solution.py:397
  9.8 8.1 %collective-permute-start.5 = (bf16[128,512]{1,0:T(8,128)(2,1)S(1)}, bf16[128,512]{1,0:T(8,128)(2,1)S(1)}, u32[]{:S(2)}, u32[]{:S(2)}) collective-permute-start(bf16[128,512]{1,0:T(8,128)(2,1)S(1)} %get-tuple-element.46), channel_id=1, source_target_pairs={{0,4},{1,5},{2,6},{3,7},{4,0},{5,1},{6,2},{7,3},{8,12},{9,13},{10,... | collective-permute-start | bytes 393224 | tf_op jit(solution)/shard_map/ppermute | solution.py:397
  11.4 6.6 %collective-permute-start.6 = (bf16[128,512]{1,0:T(8,128)(2,1)S(1)}, bf16[128,512]{1,0:T(8,128)(2,1)S(1)}, u32[]{:S(2)}, u32[]{:S(2)}) collective-permute-start(bf16[128,512]{1,0:T(8,128)(2,1)S(1)} %get-tuple-element.47), channel_id=1, source_target_pairs={{0,6},{1,7},{2,4},{3,5},{4,2},{5,3},{6,0},{7,1},{8,14},{9,15},{10,... | collective-permute-start | bytes 393224 | tf_op jit(solution)/shard_map/ppermute | solution.py:397
  19.3 7.8 %collective-permute-start.7 = (bf16[128,512]{1,0:T(8,128)(2,1)S(1)}, bf16[128,512]{1,0:T(8,128)(2,1)S(1)}, u32[]{:S(2)}, u32[]{:S(2)}) collective-permute-start(bf16[128,512]{1,0:T(8,128)(2,1)S(1)} %get-tuple-element.49), channel_id=1, source_target_pairs={{0,2},{1,3},{2,0},{3,1},{4,6},{5,7},{6,4},{7,5},{8,10},{9,11},{10,... | collective-permute-start | bytes 393224 | tf_op jit(solution)/shard_map/ppermute | solution.py:397
  20.6 7.2 %collective-permute-start.8 = (bf16[128,512]{1,0:T(8,128)(2,1)S(1)}, bf16[128,512]{1,0:T(8,128)(2,1)S(1)}, u32[]{:S(2)}, u32[]{:S(2)}) collective-permute-start(bf16[128,512]{1,0:T(8,128)(2,1)S(1)} %get-tuple-element.50), channel_id=1, source_target_pairs={{0,4},{1,5},{2,6},{3,7},{4,0},{5,1},{6,2},{7,3},{8,12},{9,13},{10,... | collective-permute-start | bytes 393224 | tf_op jit(solution)/shard_map/ppermute | solution.py:397
  21.4 6.4 %collective-permute-start.9 = (bf16[128,512]{1,0:T(8,128)(2,1)S(1)}, bf16[128,512]{1,0:T(8,128)(2,1)S(1)}, u32[]{:S(2)}, u32[]{:S(2)}) collective-permute-start(bf16[128,512]{1,0:T(8,128)(2,1)S(1)} %get-tuple-element.51), channel_id=1, source_target_pairs={{0,6},{1,7},{2,4},{3,5},{4,2},{5,3},{6,0},{7,1},{8,14},{9,15},{10,... | collective-permute-start | bytes 393224 | tf_op jit(solution)/shard_map/ppermute | solution.py:397
  23.4 7.2 %collective-permute-start.11 = (bf16[512,128]{1,0:T(8,128)(2,1)S(1)}, bf16[512,128]{1,0:T(8,128)(2,1)S(1)}, u32[]{:S(2)}, u32[]{:S(2)}) collective-permute-start(bf16[512,128]{1,0:T(8,128)(2,1)S(1)} %shard_map.130.refs_9_.left_ref), channel_id=1, source_target_pairs={{0,24},{8,16},{16,8},{24,0},{1,25},{9,17},{17,9},{25,1},{2,26},{10... | collective-permute-start | bytes 393224 | tf_op jit(solution)/shard_map/ppermute | solution.py:474
  29.3 1.3 %collective-permute-start.10 = (bf16[256,128]{1,0:T(8,128)(2,1)S(1)}, bf16[256,128]{1,0:T(8,128)(2,1)S(1)}, u32[]{:S(2)}, u32[]{:S(2)}) collective-permute-start(bf16[256,128]{1,0:T(8,128)(2,1)S(1)} %get-tuple-element.63), channel_id=1, source_target_pairs={{0,1},{1,0},{2,3},{3,2},{4,5},{5,4},{6,7},{7,6},{8,9},{9,8},{10,11... | collective-permute-start | bytes 196616 | tf_op jit(solution)/shard_map/ppermute | solution.py:14
  30.8 4.8 %collective-permute-start.12 = (bf16[1024,512]{1,0:T(8,128)(2,1)S(1)}, bf16[1024,512]{1,0:T(8,128)(2,1)S(1)}, u32[]{:S(2)}, u32[]{:S(2)}) collective-permute-start(bf16[1024,512]{1,0:T(8,128)(2,1)S(1)} %get-tuple-element.66), channel_id=1, source_target_pairs={{0,1},{1,0},{2,3},{3,2},{4,5},{5,4},{6,7},{7,6},{8,9},{9,8},{10,11... | collective-permute-start | bytes 3145736 | tf_op jit(solution)/shard_map/ppermute | solution.py:14
  31.3 4.2 %collective-permute-start.13 = (bf16[1024,512]{1,0:T(8,128)(2,1)S(1)}, bf16[1024,512]{1,0:T(8,128)(2,1)S(1)}, u32[]{:S(2)}, u32[]{:S(2)}) collective-permute-start(bf16[1024,512]{1,0:T(8,128)(2,1)S(1)} %get-tuple-element.68), channel_id=1, source_target_pairs={{0,1},{1,0},{2,3},{3,2},{4,5},{5,4},{6,7},{7,6},{8,9},{9,8},{10,11... | collective-permute-start | bytes 3145736 | tf_op jit(solution)/shard_map/ppermute | solution.py:14
  31.4 16.4 %collective-permute-start.16 = (bf16[1024,128]{1,0:T(8,128)(2,1)S(1)}, bf16[1024,128]{1,0:T(8,128)(2,1)S(1)}, u32[]{:S(2)}, u32[]{:S(2)}) collective-permute-start(bf16[1024,128]{1,0:T(8,128)(2,1)S(1)} %get-tuple-element.71.refs_0_), channel_id=1, source_target_pairs={{0,8},{8,0},{16,24},{24,16},{1,9},{9,1},{17,25},{25,17},{2,10},{10... | collective-permute-start | bytes 786440 | tf_op jit(solution)/shard_map/ppermute | solution.py:474
  33.0 12.5 %collective-permute-start.14 = (bf16[512,128]{1,0:T(8,128)(2,1)S(1)}, bf16[512,128]{1,0:T(8,128)(2,1)S(1)}, u32[]{:S(2)}, u32[]{:S(2)}) collective-permute-start(bf16[512,128]{1,0:T(8,128)(2,1)S(1)} %get-tuple-element.72), channel_id=1, source_target_pairs={{0,24},{8,16},{16,8},{24,0},{1,25},{9,17},{17,9},{25,1},{2,26},{10... | collective-permute-start | bytes 393224 | tf_op jit(solution)/shard_map/ppermute | solution.py:474
  35.5 12.4 %collective-permute-start.15 = (bf16[512,128]{1,0:T(8,128)(2,1)S(1)}, bf16[512,128]{1,0:T(8,128)(2,1)S(1)}, u32[]{:S(2)}, u32[]{:S(2)}) collective-permute-start(bf16[512,128]{1,0:T(8,128)(2,1)S(1)} %get-tuple-element.72), channel_id=1, source_target_pairs={{0,16},{8,24},{16,0},{24,8},{1,17},{9,25},{17,1},{25,9},{2,18},{10... | collective-permute-start | bytes 393224 | tf_op jit(solution)/shard_map/ppermute | solution.py:474
  (1 other events, 3.7 us)

commit v3 on v2

--- a/solution.py
+++ b/solution.py
@@ -138,6 +138,7 @@
 
 
 VMEM_LIMIT = 16 * 2**20
+COL_MICROS = 0.5
 
 
 def dot(left, right, left_dim=1, right_dim=0):
@@ -146,13 +147,13 @@
     )
 
 
-def call(body, outs, *args, scratch=(), micros=0.01, to_hbm=False, aliases=()):
+def call(body, outs, *args, scratch=(), micros=0.01, to_hbm=0, aliases=()):
     whole = pl.BlockSpec(memory_space=pltpu.VMEM)
     return pl.pallas_call(
         body,
         out_shape=outs,
         in_specs=[whole] * len(args),
-        out_specs=[pl.BlockSpec() if to_hbm else whole] * len(outs),
+        out_specs=[pl.BlockSpec()] * to_hbm + [whole] * (len(outs) - to_hbm),
         scratch_shapes=list(scratch),
         input_output_aliases=dict(aliases),
         compiler_params=pltpu.CompilerParams(vmem_limit_bytes=VMEM_LIMIT),
@@ -207,10 +208,13 @@
 
 
 def tables(chips, rows, cols):
-    def body(take_ref, order_ref, back_ref):
-        take_ref[...] = pair_cols(lax.axis_index("loop"), chips, rows, cols, 0)
+    def body(take_ref, order_ref, back_ref, place_ref):
+        me = lax.axis_index("loop")
+        places = [pair_cols(me, chips, rows, cols, turn) for turn in (0, 1)]
+        take_ref[...] = places[0]
         order_ref[...] = sent_order(chips, rows, cols, 0)
         back_ref[...] = sent_order(chips, rows, cols, 1)
+        place_ref[...] = jnp.concatenate(places, 1)
 
     return body
 
@@ -219,26 +223,29 @@
     narrow = jnp.bfloat16
 
     def body(*refs):
-        x_refs, d_refs, (take_ref, order_ref), rest = refs[:4], refs[4:8], refs[8:10], refs[10:]
-        outs, (up_out, down_out, hid_ref, grad_ref) = rest[:chips], rest[chips:]
+        (own_ref, other_ref, *weights, take_ref, order_ref) = refs[:6]
+        earlier, outs, (taken_ref, grid_ref) = refs[6 : -chips - 2], refs[-chips - 2 : -2], refs[-2:]
         parity = lax.axis_index("loop") % 2
-        take, order = take_ref[...], order_ref[...]
+        pair_blocks = own_ref.shape[0] // half
+        taken = [own_first(dot(take_ref[...], ref[...], 0, 0), parity) for ref in weights]
+        taken_ref[...] = jnp.concatenate(taken, 0).astype(narrow)
+        high = taken_ref.shape[0] // pair_blocks
+        for at, block in enumerate(pair_blocks_of(parity, pair_blocks)):
+            part = slice(at * high, (at + 1) * high)
+            features = block_rows(own_ref, other_ref, block * half, half)
+            grid_ref[part, :] = dot(taken_ref[part, :], features).astype(narrow)
+        sent = dot(order_ref[...], grid_ref[...]).astype(narrow)
         unit = 2 * rows * cols
-        jobs = ((x_refs, up_out, hid_ref), (d_refs, down_out, grad_ref))
-        for job, ((own_ref, other_ref, *weights), taken_ref, grid_ref) in enumerate(jobs):
-            pair_blocks = own_ref.shape[0] // half
-            taken = [own_first(dot(take, ref[...], 0, 0), parity) for ref in weights]
-            taken_ref[...] = jnp.concatenate(taken, 0).astype(narrow)
-            high = taken_ref.shape[0] // pair_blocks
-            for at, block in enumerate(pair_blocks_of(parity, pair_blocks)):
-                part = slice(at * high, (at + 1) * high)
-                features = block_rows(own_ref, other_ref, block * half, half)
-                grid_ref[part, :] = dot(taken_ref[part, :], features).astype(narrow)
-            sent = dot(order, grid_ref[...]).astype(narrow)
-            for q in range(chips):
-                outs[q][job * unit : (job + 1) * unit, :] = sent[q * unit : (q + 1) * unit]
-
-    return body
+        for q, out in enumerate(outs):
+            if earlier:
+                out[:unit, :] = earlier[q][...]
+            out[out.shape[0] - unit :, :] = sent[q * unit : (q + 1) * unit]
+
+    return body
+
+
+def by_distance(bufs):
+    return [bufs[0], *bufs[:0:-1]]
 
 
 def one_col(bufs, at, deep):
@@ -255,7 +262,7 @@
     deep = 2 * rows
 
     def body(*refs):
-        bufs, rest = refs[:chips], refs[chips:]
+        bufs, rest = by_distance(refs[:chips]), refs[chips:]
         up_ref, down_ref, perm_up_ref, perm_down_ref = rest[:4]
         outs, rest = rest[4 : 4 + chips], rest[4 + chips :]
         activated_ref, grad_pre_ref, take_up_ref, take_down_ref = rest
@@ -289,7 +296,7 @@
     deep = 2 * rows
 
     def body(*refs):
-        bufs = refs[:chips]
+        bufs = by_distance(refs[:chips])
         activated_ref, grad_pre_ref, take_up_ref, take_down_ref, out_ref = refs[chips:]
         size = chips * deep
         for b in range(cols):
@@ -334,24 +341,22 @@
 
 
 def join(kept_ref, came_ref, left_ref, right_ref, *rest):
-    out_ref, with_ref = rest[-4:-2]
+    out_ref, sum_ref = rest[-3:-1]
     size = kept_ref.shape[0] // 2
     for at in range(2):
         span = slice(at * size, (at + 1) * size)
         for off, ref in enumerate((kept_ref, came_ref)):
-            to = slice((2 * at + off) * size, (2 * at + off + 1) * size)
-            out_ref[to, :] = ref[span, :]
-            with_ref[to, :] = ref[span, :]
+            out_ref[(2 * at + off) * size : (2 * at + off + 1) * size, :] = ref[span, :]
     total = left_ref[...].astype(jnp.float32) + right_ref[...].astype(jnp.float32)
-    with_ref[4 * size :, :] = total.astype(with_ref.dtype)
+    sum_ref[...] = total.astype(sum_ref.dtype)
 
 
 def row_outputs(half):
     def body(*refs):
-        jobs, outs = (refs[:3], refs[3:6]), refs[6:]
+        jobs, (*kept_refs, sent_ref) = (refs[:3], refs[3:6]), refs[6:]
         parity = lax.axis_index("loop") % 2
         for at, (grid_ref, own_ref, weights_ref) in enumerate(jobs):
-            kept_ref, sent_ref = outs[2 * at : 2 * at + 2]
+            kept_ref, features = kept_refs[at], own_ref.shape[0]
             pair_blocks = own_ref.shape[0] // half
             high = weights_ref.shape[0] // pair_blocks
             for place, block in enumerate(pair_blocks_of(parity, pair_blocks)):
@@ -359,45 +364,55 @@
                 span = pl.ds(pl.multiple_of(block * half, half), half)
                 branch = dot(weights_ref[part, :], grid_ref[part, :], 0, 0)
                 kept_ref[span, :] = own_ref[span, :].astype(jnp.float32) + branch[:half]
+                span = pl.ds(pl.multiple_of(at * features + block * half, half), half)
                 sent_ref[span, :] = branch[half:].astype(jnp.bfloat16)
 
     return body
 
 
-def add_partner(*refs):
-    jobs, done_ref = ((refs[0], refs[1], refs[4]), (refs[2], refs[3], refs[5])), refs[6]
-    for kept, got, out in jobs:
-        out[...] = (kept[...] + got[...].astype(jnp.float32)).astype(out.dtype)
+def add_partner(mixed_ref, grad_ref, got_ref, _, mixed_out, grad_out, done_ref):
+    size = mixed_ref.shape[0]
+    for at, (kept, out) in enumerate(((mixed_ref, mixed_out), (grad_ref, grad_out))):
+        got = got_ref[at * size : (at + 1) * size, :].astype(jnp.float32)
+        out[...] = (kept[...] + got).astype(out.dtype)
     done_ref[...] = jnp.zeros_like(done_ref)
 
 
-def total_grads(chips, rows, cols, dps, scale):
+def add(*refs):
+    left_ref, right_ref, out_ref = refs[-3:]
+    total = left_ref[...].astype(jnp.float32) + right_ref[...].astype(jnp.float32)
+    out_ref[...] = total.astype(out_ref.dtype)
+
+
+def total_grads(scale):
     def body(*refs):
-        parts, outs = refs[:dps], refs[-4:]
-        both_ref, got_ref = refs[0], refs[dps - 1]
-        me = lax.axis_index("loop")
-        place = jnp.concatenate([pair_cols(me, chips, rows, cols, turn) for turn in (0, 1)], 1)
-        place = jnp.concatenate([place] * dps, 1)
+        pair, place_ref, outs = refs[:2], refs[2], refs[-2:]
+        place = jnp.concatenate([place_ref[...]] * 2, 1)
         size = outs[0].shape[0]
-        for at, out in enumerate(outs[:2]):
+        for at, out in enumerate(outs):
             span = slice(at * size, (at + 1) * size)
-            out[...] = dot(place, jnp.concatenate([r[span, :] for r in parts], 0)) * scale
-        size = outs[2].shape[0]
-        for at, out in enumerate(outs[2:]):
-            span = slice(2 * outs[0].shape[0] + at * size, 2 * outs[0].shape[0] + (at + 1) * size)
-            both = both_ref[span, :].astype(jnp.float32) + got_ref[span, :].astype(jnp.float32)
+            out[...] = dot(place, jnp.concatenate([r[span, :] for r in pair], 0)) * scale
+
+    return body
+
+
+def total_col_grads(scale):
+    def body(sum_ref, got_ref, up_ref, down_ref, done_ref):
+        done_ref[...] = jnp.zeros_like(done_ref)
+        size = up_ref.shape[0]
+        for at, out in enumerate((up_ref, down_ref)):
+            span = slice(at * size, (at + 1) * size)
+            both = sum_ref[span, :].astype(jnp.float32) + got_ref[span, :].astype(jnp.float32)
             out[...] = both * scale
 
     return body
 
 
-def exchange(bufs, axis):
-    count = 2 * len(bufs)
-    got = {
-        q: lax.ppermute(bufs[q], axis, [(s, s ^ (2 * q)) for s in range(count)])
-        for q in range(len(bufs) - 1, 0, -1)
-    }
-    return [bufs[0]] + [got[q] for q in range(1, len(bufs))]
+def exchange(bufs, axis, far_first):
+    count = len(bufs)
+    order = range(count - 1, 0, -1) if far_first else range(1, count)
+    pairs = {q: [(s, s ^ (2 * q)) for s in range(2 * count)] for q in order}
+    return [bufs[0]] + [lax.ppermute(bufs[q], axis, pairs[q]) for q in order]
 
 
 def shards(tokens, cotangent, up_first, up_second, down_first, down_second, perm_up, perm_down):
@@ -420,35 +435,37 @@
 
     up_rows = up_first.reshape(rows * all_cols, block)
     down_rows = down_second.reshape(rows * all_cols, block)
+    grid_rows = 2 * rows * chips * cols
+    half_buf = struct(2 * rows * cols, toks)
+    buf = struct(4 * rows * cols, toks)
+    grid = struct(grid_rows, toks)
+    half_grid = struct(grid_rows // 2, toks)
+    taken = struct(grid_rows, block)
+    full = struct(feature_rows, toks)
+    take, order, order_back, place = call(
+        tables(chips, rows, cols),
+        [struct(rows * all_cols, rows * chips * cols)] + [struct(grid_rows, grid_rows)] * 3,
+        micros=4,
+    )
     other_x = from_partner(tokens, "loop", 0)
     other_up = from_partner(up_rows, "loop", 0)
-    other_d = from_partner(cotangent, "loop", 0)
     other_down = from_partner(down_rows, "loop", 0)
-    grid_rows = 2 * rows * chips * cols
-    buf = struct(4 * rows * cols, toks)
-    grid = struct(grid_rows, toks)
-    taken = struct(grid_rows, block)
-    take, order, order_back = call(
-        tables(chips, rows, cols),
-        [struct(rows * all_cols, rows * chips * cols)] + [struct(grid_rows, grid_rows)] * 2,
-        micros=4,
-    )
-    *sent, up_taken, down_taken = call(
-        first_rows(chips, rows, cols, half),
-        [buf] * chips + [taken] * 2,
-        tokens,
-        other_x,
-        up_rows,
-        other_up,
-        cotangent,
-        other_d,
-        down_rows,
-        other_down,
-        take,
-        order,
-        scratch=[pltpu.VMEM(grid.shape, narrow)] * 2,
-    )
-    cells = exchange(sent, "loop")
+    leaving, other_up, other_down = lax.optimization_barrier((cotangent, other_up, other_down))
+    other_d = from_partner(leaving, "loop", 0)
+
+    def rows_out(out, *args):
+        return call(
+            first_rows(chips, rows, cols, half),
+            [out] * chips + [taken],
+            *args,
+            scratch=[pltpu.VMEM(grid.shape, narrow)],
+        )
+
+    *sent, up_taken = rows_out(half_buf, tokens, other_x, up_rows, other_up, take, order)
+    *sent, down_taken = rows_out(
+        buf, cotangent, other_d, down_rows, other_down, take, order, *sent
+    )
+    cells = exchange(sent, "loop", True)
     square = struct(cols * size, size)
     *sent, activated, grad_pre, take_up, take_down = call(
         columns(chips, rows, cols),
@@ -459,7 +476,7 @@
         perm_up.reshape(1, size),
         perm_down.reshape(1, size),
     )
-    back = exchange(sent, "loop")
+    back = exchange(sent, "loop", False)
     (col_grads,) = call(
         column_grads(chips, rows, cols),
         [struct(2 * cols * size, size)],
@@ -473,7 +490,6 @@
     def over_dp(value, apart):
         return lax.ppermute(value, "dp", [(s, s ^ apart) for s in range(dps)])
 
-    col_got = over_dp(col_grads, dps - 1)
     kept, leaving, back_rows, grad_rows = call(
         row_grads(chips, rows, cols, half),
         [taken] * 2 + [grid] * 2,
@@ -485,12 +501,11 @@
         order_back,
         col_grads,
     )
-    came = from_partner(leaving, "loop", 0)
     partial = struct(feature_rows, toks, wide)
-    full = struct(feature_rows, toks)
-    mixed, mixed_send, grad_tokens, grad_send = call(
+    both = struct(2 * feature_rows, toks)
+    mixed, grad_tokens, branches = call(
         row_outputs(half),
-        [partial, full] * 2,
+        [partial, partial, both],
         back_rows,
         tokens,
         down_taken,
@@ -498,36 +513,44 @@
         cotangent,
         up_taken,
     )
-    sums, sums_more, mixed_send, grad_send = call(
+    sums, col_sum, branches = call(
         join,
-        [struct(2 * grid_rows, block), struct(2 * grid_rows + 2 * cols * size, block), full, full],
+        [struct(2 * grid_rows, block), struct(*col_grads.shape), both],
         kept,
-        came,
+        from_partner(leaving, "loop", 0),
         col_grads,
-        col_got,
-        mixed_send,
-        grad_send,
-        aliases=((4, 2), (5, 3)),
-    )
-    parts = [sums_more] + [
-        over_dp(sums if apart > 1 else sums_more, apart) for apart in range(dps - 1, 0, -1)
-    ]
+        over_dp(col_grads, dps - 1),
+        branches,
+        aliases=((4, 2),),
+    )
+    (sums,) = call(add, [struct(*sums.shape)], sums, over_dp(sums, dps - 1))
+    scale = 1.0 / math.sqrt(dps * toks)
+    token = struct(8, 128, wide)
+    g_up_second, g_down_first, done = call(
+        total_col_grads(scale),
+        [struct(*square.shape, wide)] * 2 + [token],
+        col_sum,
+        over_dp(col_sum, 1),
+        to_hbm=2,
+        micros=COL_MICROS,
+    )
     mixed, grad_tokens, done = call(
         add_partner,
-        [full] * 2 + [struct(8, 128, wide)],
+        [full] * 2 + [token],
         mixed,
-        from_partner(mixed_send, "loop", 0),
         grad_tokens,
-        from_partner(grad_send, "loop", 0),
-        to_hbm=True,
-    )
-    scale = 1.0 / math.sqrt(dps * toks)
-    g_up_first, g_down_second, g_up_second, g_down_first = call(
-        total_grads(chips, rows, cols, dps, scale),
-        [struct(rows * all_cols, block, wide)] * 2 + [struct(*square.shape, wide)] * 2,
-        *parts,
+        from_partner(branches, "loop", 0),
         done,
-        to_hbm=True,
+        to_hbm=2,
+    )
+    g_up_first, g_down_second = call(
+        total_grads(scale),
+        [struct(rows * all_cols, block, wide)] * 2,
+        sums,
+        over_dp(sums, 1),
+        place,
+        done,
+        to_hbm=2,
     )
     return (
         mixed,

time: 49.2 us -> 45.9 us (0.933)
  waiting for transfers between devices: 21.3 us -> 16.2 us
  starting transfers between devices: 17.7 us -> 18.9 us
  Pallas kernels: 9.26 us -> 9.84 us
    ppermute x4, waiting for transfers between devices: 10.6 us -> 5.55 us  [over_dp(): return lax.ppermute(value, 'dp', [(s, s ^ apart) for s in range(dps)])]
    ppermute x4, starting transfers between devices: 7.81 us -> 9.03 us  [over_dp(): return lax.ppermute(value, 'dp', [(s, s ^ apart) for s in range(dps)])]
    ppermute x7 -> x6, waiting for transfers between devices: 3.42 us -> 2.8 us  [from_partner(): return lax.ppermute(value, axis, pairs)]
    ppermute x6, waiting for transfers between devices: 7.25 us -> 7.86 us  [exchange(): return [bufs[0]] + [lax.ppermute(bufs[q], axis, pairs[q]) for q in order]]
    pallas_call x9 -> x12, Pallas kernels: 9.26 us -> 9.84 us  [call(): pl.pallas_call(body, out_shape=outs, in_specs=[whole] * len(args), out_sp...]
    ppermute x7 -> x6, starting transfers between devices: 1.84 us -> 1.77 us  [from_partner(): return lax.ppermute(value, axis, pairs)]
  transfers between devices with their start and end apart: 17 -> 16, of which waited for: 7 -> 11; matrix products, arithmetic and copies ran while one was open for 0% -> 0% of each run, Pallas kernels for 11% -> 15%
where the time goes in v3:
time: 45.9 us; the launch traced here: 45.7 us
  starting transfers between devices  18.9 us (41%)
  waiting for transfers between devices  16.2 us (35%)
  Pallas kernels  9.84 us (21%)
  between operations  0.77 us (2%)
    pallas_call x12, Pallas kernels, call(): pl.pallas_call(body, out_shape=outs, in_specs=[whole] * len(args), out_sp...  9.84 us
    ppermute x4, starting transfers between devices, over_dp(): return lax.ppermute(value, 'dp', [(s, s ^ apart) for s in range(dps)])  9.03 us
    ppermute x6, starting transfers between devices, exchange(): return [bufs[0]] + [lax.ppermute(bufs[q], axis, pairs[q]) for q in order]  8.07 us
    ppermute x6, waiting for transfers between devices, exchange(): return [bufs[0]] + [lax.ppermute(bufs[q], axis, pairs[q]) for q in order]  7.86 us
    ppermute x4, waiting for transfers between devices, over_dp(): return lax.ppermute(value, 'dp', [(s, s ^ apart) for s in range(dps)])  5.55 us
    ppermute x6, waiting for transfers between devices, from_partner(): return lax.ppermute(value, axis, pairs)  2.8 us
    ppermute x6, starting transfers between devices, from_partner(): return lax.ppermute(value, axis, pairs)  1.77 us
  transfers between devices with their start and end apart: 16, of which 11 were waited for; matrix products, arithmetic and copies ran while one was open for 0% of the time, Pallas kernels for 15%

profile of v3, /device:TPU:0, one launch (start us, length us, event | category | flops | bytes accessed | tf_op | source)
XLA Modules:
  0.0 45.7 jit_solution(16099104820499178866)
XLA Ops:
  1.7 0.6 %collective-permute-done.refs_3_ = bf16[256,128]{1,0:T(8,128)(2,1)S(1)} collective-permute-done((bf16[256,128]{1,0:T(8,128)(2,1)}, bf16[256,128]{1,0:T(8,128)(2,1)S(1)}, u32[]{:S(2)}, u32[]{:S(2)}) %collective-permute-start) | collective-permute-done | bytes 65568 | tf_op jit(solution)/shard_map/ppermute | solution.py:14
  2.9 1.2 %collective-permute-done.3.refs_1_.refs_5_ = bf16[1024,512]{1,0:T(8,128)(2,1)S(1)} collective-permute-done((bf16[1024,512]{1,0:T(8,128)(2,1)}, bf16[1024,512]{1,0:T(8,128)(2,1)S(1)}, u32[]{:S(2)}, u32[]{:S(2)}) %collective-permute-start.3) | collective-permute-done | bytes 1048608 | tf_op jit(solution)/shard_map/ppermute | solution.py:14
  4.2 0.8 %shard_map.128 = (bf16[64,512]{1,0:T(8,128)(2,1)S(1)}, bf16[64,512]{1,0:T(8,128)(2,1)S(1)}, bf16[64,512]{1,0:T(8,128)(2,1)S(1)}, bf16[64,512]{1,0:T(8,128)(2,1)S(1)}, bf16[256,128]{1,0:T(8,128)(2,1)S(1)}) custom-call(bf16[1024,512]{1,0:T(8,128)(2,1)S(1)} %copy-done, bf16[1024,512]{1,0:T(8,128)(2,1)S(1)} %collective-permute-done.3.refs_1_.refs_5_, ...), custom_call_target="tpu_custom_call" | custom-call | flops 10000000 | bytes 30000 | tf_op jit(solution)/shard_map/pallas_call | solution.py:152
  5.0 0.6 %collective-permute-done.2.refs_1_.refs_7_ = bf16[1024,512]{1,0:T(8,128)(2,1)S(1)} collective-permute-done((bf16[1024,512]{1,0:T(8,128)(2,1)}, bf16[1024,512]{1,0:T(8,128)(2,1)S(1)}, u32[]{:S(2)}, u32[]{:S(2)}) %collective-permute-start.2) | collective-permute-done | bytes 1048608 | tf_op jit(solution)/shard_map/ppermute | solution.py:14
  5.7 0.8 %shard_map.129 = (bf16[128,512]{1,0:T(8,128)(2,1)S(1)}, bf16[128,512]{1,0:T(8,128)(2,1)S(1)}, bf16[128,512]{1,0:T(8,128)(2,1)S(1)}, bf16[128,512]{1,0:T(8,128)(2,1)S(1)}, bf16[256,128]{1,0:T(8,128)(2,1)S(1)}) custom-call(bf16[1024,512]{1,0:T(8,128)(2,1)S(1)} %copy-done.1, bf16[1024,512]{1,0:T(8,128)(2,1)S(1)} %collective-permute-done.2.refs_1_.refs_7_, ...), custom_call_target="tpu_custom_call" | custom-call | flops 10000000 | bytes 30000 | tf_op jit(solution)/shard_map/pallas_call | solution.py:152
  6.5 3.9 %collective-permute-start.4 = (bf16[128,512]{1,0:T(8,128)(2,1)S(1)}, bf16[128,512]{1,0:T(8,128)(2,1)S(1)}, u32[]{:S(2)}, u32[]{:S(2)}) collective-permute-start(bf16[128,512]{1,0:T(8,128)(2,1)S(1)} %get-tuple-element.59), channel_id=1, source_target_pairs={{0,6},{1,7},{2,4},{3,5},{4,2},{5,3},{6,0},{7,1},{8,14},{9,15},{10,... | collective-permute-start | bytes 393224 | tf_op jit(solution)/shard_map/ppermute | solution.py:415
  11.0 3.3 %collective-permute-done.4.refs_1_ = bf16[128,512]{1,0:T(8,128)(2,1)S(1)} collective-permute-done((bf16[128,512]{1,0:T(8,128)(2,1)S(1)}, bf16[128,512]{1,0:T(8,128)(2,1)S(1)}, u32[]{:S(2)}, u32[]{:S(2)}) %collective-permute-start.4) | collective-permute-done | bytes 131104 | tf_op jit(solution)/shard_map/ppermute | solution.py:415
  14.3 2.7 %collective-permute-done.5.refs_2_ = bf16[128,512]{1,0:T(8,128)(2,1)S(1)} collective-permute-done((bf16[128,512]{1,0:T(8,128)(2,1)S(1)}, bf16[128,512]{1,0:T(8,128)(2,1)S(1)}, u32[]{:S(2)}, u32[]{:S(2)}) %collective-permute-start.5) | collective-permute-done | bytes 131104 | tf_op jit(solution)/shard_map/ppermute | solution.py:415
  17.3 1.3 %shard_map.130 = (bf16[128,512]{1,0:T(8,128)(2,1)S(1)}, bf16[128,512]{1,0:T(8,128)(2,1)S(1)}, bf16[128,512]{1,0:T(8,128)(2,1)S(1)}, bf16[128,512]{1,0:T(8,128)(2...) custom-call(bf16[128,512]{1,0:T(8,128)(2,1)S(1)} %get-tuple-element., ...), custom_call_target="tpu_custom_call" | custom-call | flops 10000000 | bytes 30000 | tf_op jit(solution)/shard_map/pallas_call | solution.py:152
  18.6 1.6 %collective-permute-start.7 = (bf16[128,512]{1,0:T(8,128)(2,1)S(1)}, bf16[128,512]{1,0:T(8,128)(2,1)S(1)}, u32[]{:S(2)}, u32[]{:S(2)}) collective-permute-start(bf16[128,512]{1,0:T(8,128)(2,1)S(1)} %get-tuple-element.63), channel_id=1, source_target_pairs={{0,2},{1,3},{2,0},{3,1},{4,6},{5,7},{6,4},{7,5},{8,10},{9,11},{10,... | collective-permute-start | bytes 393224 | tf_op jit(solution)/shard_map/ppermute | solution.py:415
  20.2 0.6 %collective-permute-start.8 = (bf16[128,512]{1,0:T(8,128)(2,1)S(1)}, bf16[128,512]{1,0:T(8,128)(2,1)S(1)}, u32[]{:S(2)}, u32[]{:S(2)}) collective-permute-start(bf16[128,512]{1,0:T(8,128)(2,1)S(1)} %get-tuple-element.64), channel_id=1, source_target_pairs={{0,4},{1,5},{2,6},{3,7},{4,0},{5,1},{6,2},{7,3},{8,12},{9,13},{10,... | collective-permute-start | bytes 393224 | tf_op jit(solution)/shard_map/ppermute | solution.py:415
  20.8 1.4 %collective-permute-start.9 = (bf16[128,512]{1,0:T(8,128)(2,1)S(1)}, bf16[128,512]{1,0:T(8,128)(2,1)S(1)}, u32[]{:S(2)}, u32[]{:S(2)}) collective-permute-start(bf16[128,512]{1,0:T(8,128)(2,1)S(1)} %get-tuple-element.65), channel_id=1, source_target_pairs={{0,6},{1,7},{2,4},{3,5},{4,2},{5,3},{6,0},{7,1},{8,14},{9,15},{10,... | collective-permute-start | bytes 393224 | tf_op jit(solution)/shard_map/ppermute | solution.py:415
  22.2 0.6 %shard_map.131.refs_9_.left_ref = bf16[512,128]{1,0:T(8,128)(2,1)S(1)} custom-call(bf16[128,512]{1,0:T(8,128)(2,1)S(1)} %get-tuple-element.58.refs_0_, bf16[128,512]{1,0:T(8,128)(2,1)S(1)} %collective-permute-done.4.refs_1_, bf16[128,512]{1,0:T(8,128)(2,1)S(1)} %collective-permute-done.5.refs_2_, bf16[128,512]{1,0:T(8,128)(2,1)S(1)} %collective-permute-done.6.refs_3_, ...), custom_call_target="tpu_custom_call" | custom-call | flops 10000000 | bytes 30000 | tf_op jit(solution)/shard_map/pallas_call | solution.py:152
  22.8 3.7 %collective-permute-start.11 = (bf16[512,128]{1,0:T(8,128)(2,1)S(1)}, bf16[512,128]{1,0:T(8,128)(2,1)S(1)}, u32[]{:S(2)}, u32[]{:S(2)}) collective-permute-start(bf16[512,128]{1,0:T(8,128)(2,1)S(1)} %shard_map.131.refs_9_.left_ref), channel_id=1, source_target_pairs={{0,24},{8,16},{16,8},{24,0},{1,25},{9,17},{17,9},{25,1},{2,26},{10... | collective-permute-start | bytes 393224 | tf_op jit(solution)/shard_map/ppermute | solution.py:491
  26.4 1.6 %collective-permute-done.8.refs_2_ = bf16[128,512]{1,0:T(8,128)(2,1)S(1)} collective-permute-done((bf16[128,512]{1,0:T(8,128)(2,1)S(1)}, bf16[128,512]{1,0:T(8,128)(2,1)S(1)}, u32[]{:S(2)}, u32[]{:S(2)}) %collective-permute-start.8) | collective-permute-done | bytes 131104 | tf_op jit(solution)/shard_map/ppermute | solution.py:415
  28.0 1.5 %shard_map.132 = (bf16[256,128]{1,0:T(8,128)(2,1)S(1)}, bf16[256,128]{1,0:T(8,128)(2,1)S(1)}, bf16[256,512]{1,0:T(8,128)(2,1)S(1)}, bf16[256,512]{1,0:T(8,128)(2,1)S(1)}) custom-call(bf16[128,512]{1,0:T(8,128)(2,1)S(1)} %get-tuple-element.62.refs_0_, bf16[128,512]{1,0:T(8,128)(2,1)S(1)} %collective-permute-done.7.refs_1_, ...), custom_call_target="tpu_custom_call" | custom-call | flops 10000000 | bytes 30000 | tf_op jit(solution)/shard_map/pallas_call | solution.py:152
  29.6 1.3 %shard_map.133 = (f32[1024,512]{1,0:T(8,128)S(1)}, f32[1024,512]{1,0:T(8,128)S(1)}, bf16[2048,512]{1,0:T(8,128)(2,1)S(1)}) custom-call(bf16[256,512]{1,0:T(8,128)(2,1)S(1)} %get-tuple-element.71.refs_0_, bf16[1024,512]{1,0:T(8,128)(2,1)S(1)} %copy-done, bf16[256,128]{1,0:T(8,128)(2,1)S(1)} %get-tuple-element.72.refs_2_, ...), custom_call_target="tpu_custom_call" | custom-call | flops 10000000 | bytes 30000 | tf_op jit(solution)/shard_map/pallas_call | solution.py:152
  31.5 3.6 %collective-permute-start.14 = (bf16[512,128]{1,0:T(8,128)(2,1)S(1)}, bf16[512,128]{1,0:T(8,128)(2,1)S(1)}, u32[]{:S(2)}, u32[]{:S(2)}) collective-permute-start(bf16[512,128]{1,0:T(8,128)(2,1)S(1)} %get-tuple-element.85.refs_0_), channel_id=1, source_target_pairs={{0,24},{8,16},{16,8},{24,0},{1,25},{9,17},{17,9},{25,1},{2,26},{10... | collective-permute-start | bytes 393224 | tf_op jit(solution)/shard_map/ppermute | solution.py:491
  35.1 4.6 %collective-permute-done.14.refs_1_ = bf16[512,128]{1,0:T(8,128)(2,1)S(1)} collective-permute-done((bf16[512,128]{1,0:T(8,128)(2,1)S(1)}, bf16[512,128]{1,0:T(8,128)(2,1)S(1)}, u32[]{:S(2)}, u32[]{:S(2)}) %collective-permute-start.14) | collective-permute-done | bytes 131104 | tf_op jit(solution)/shard_map/ppermute | solution.py:491
  39.8 1.7 %collective-permute-start.15 = (bf16[512,128]{1,0:T(8,128)(2,1)S(1)}, bf16[512,128]{1,0:T(8,128)(2,1)S(1)}, u32[]{:S(2)}, u32[]{:S(2)}) collective-permute-start(bf16[512,128]{1,0:T(8,128)(2,1)S(1)} %shard_map.137.refs_0_), channel_id=1, source_target_pairs={{0,8},{8,0},{16,24},{24,16},{1,9},{9,1},{17,25},{25,17},{2,10},{10... | collective-permute-start | bytes 393224 | tf_op jit(solution)/shard_map/ppermute | solution.py:491
  41.9 0.7 %shard_map.135 = (f32[256,128]{1,0:T(8,128)}, f32[256,128]{1,0:T(8,128)}, f32[8,128]{1,0:T(8,128)S(1)}) custom-call(bf16[512,128]{1,0:T(8,128)(2,1)S(1)} %get-tuple-element.81.sum_ref, bf16[512,128]{1,0:T(8,128)(2,1)S(1)} %collective-permute-done.13.got_ref), custom_call_target="tpu_custom_call" | custom-call | flops 500000000 | bytes 1500000 | tf_op jit(solution)/shard_map/pallas_call | solution.py:152
  42.6 1.6 %shard_map.136 = (bf16[1024,512]{1,0:T(8,128)(2,1)}, bf16[1024,512]{1,0:T(8,128)(2,1)}, f32[8,128]{1,0:T(8,128)S(1)}) custom-call(f32[1024,512]{1,0:T(8,128)S(1)} %get-tuple-element.75.mixed_ref, f32[1024,512]{1,0:T(8,128)S(1)} %get-tuple-element.76.grad_ref, bf16[2048,512]{1,0:T(8,128)(2,1)S(1)} %collective-permute-done.12.got_ref, ...), custom_call_target="tpu_custom_call" | custom-call | flops 10000000 | bytes 30000 | tf_op jit(solution)/shard_map/pallas_call | solution.py:152
  44.2 0.6 %collective-permute-done.15.refs_1_ = bf16[512,128]{1,0:T(8,128)(2,1)S(1)} collective-permute-done((bf16[512,128]{1,0:T(8,128)(2,1)S(1)}, bf16[512,128]{1,0:T(8,128)(2,1)S(1)}, u32[]{:S(2)}, u32[]{:S(2)}) %collective-permute-start.15) | collective-permute-done | bytes 131104 | tf_op jit(solution)/shard_map/ppermute | solution.py:491
  44.8 0.9 %shard_map.138 = (f32[256,128]{1,0:T(8,128)}, f32[256,128]{1,0:T(8,128)}) custom-call(bf16[512,128]{1,0:T(8,128)(2,1)S(1)} %shard_map.137.refs_0_, bf16[512,128]{1,0:T(8,128)(2,1)S(1)} %collective-permute-done.15.refs_1_, bf16[256,256]{1,0:T(8,128)(2,1)S(1)} %get-tuple-element.86.refs_2_, f32[8,128]{1,0:T(8,128)S(1)} %get-tuple-element.87.refs_3_), custom_call_target="tpu_custom_call" | custom-call | flops 10000000 | bytes 30000 | tf_op jit(solution)/shard_map/pallas_call | solution.py:152
  (36 shorter events, 3.7 us)
Async XLA Ops:
  0.6 1.6 %collective-permute-start = (bf16[256,128]{1,0:T(8,128)(2,1)}, bf16[256,128]{1,0:T(8,128)(2,1)S(1)}, u32[]{:S(2)}, u32[]{:S(2)}) collective-permute-start(bf16[256,128]{1,0:T(8,128)(2,1)} %bitcast.10), channel_id=1, source_target_pairs={{0,1},{1,0},{2,3},{3,2},{4,5},{5,4},{6,7},{7,6},{8,9},{9,8},{10,11... | collective-permute-start | bytes 196616 | tf_op jit(solution)/shard_map/ppermute | solution.py:14
  1.1 3.0 %copy-start = (bf16[1024,512]{1,0:T(8,128)(2,1)S(1)}, bf16[1024,512]{1,0:T(8,128)(2,1)}, u32[]{:S(2)}) copy-start(bf16[1024,512]{1,0:T(8,128)(2,1)} %refs_1_.1) | copy-start | bytes 3145732
  1.2 3.0 %copy-start.2 = (bf16[16,16,128]{2,1,0:T(8,128)(2,1)S(1)}, bf16[16,16,128]{2,1,0:T(8,128)(2,1)}, u32[]{:S(2)}) copy-start(bf16[16,16,128]{2,1,0:T(8,128)(2,1)} %param.10) | copy-start | bytes 196612
  1.2 1.5 %collective-permute-start.1 = (bf16[256,128]{1,0:T(8,128)(2,1)}, bf16[256,128]{1,0:T(8,128)(2,1)S(1)}, u32[]{:S(2)}, u32[]{:S(2)}) collective-permute-start(bf16[256,128]{1,0:T(8,128)(2,1)} %bitcast.14), channel_id=1, source_target_pairs={{0,1},{1,0},{2,3},{3,2},{4,5},{5,4},{6,7},{7,6},{8,9},{9,8},{10,11... | collective-permute-start | bytes 196616 | tf_op jit(solution)/shard_map/ppermute | solution.py:14
  1.2 2.9 %collective-permute-start.3 = (bf16[1024,512]{1,0:T(8,128)(2,1)}, bf16[1024,512]{1,0:T(8,128)(2,1)S(1)}, u32[]{:S(2)}, u32[]{:S(2)}) collective-permute-start(bf16[1024,512]{1,0:T(8,128)(2,1)} %refs_1_.1), channel_id=1, source_target_pairs={{0,1},{1,0},{2,3},{3,2},{4,5},{5,4},{6,7},{7,6},{8,9},{9,8},{10,11... | collective-permute-start | bytes 3145736 | tf_op jit(solution)/shard_map/ppermute | solution.py:14
  2.6 3.0 %collective-permute-start.2 = (bf16[1024,512]{1,0:T(8,128)(2,1)}, bf16[1024,512]{1,0:T(8,128)(2,1)S(1)}, u32[]{:S(2)}, u32[]{:S(2)}) collective-permute-start(bf16[1024,512]{1,0:T(8,128)(2,1)} %refs_4_.3), channel_id=1, source_target_pairs={{0,1},{1,0},{2,3},{3,2},{4,5},{5,4},{6,7},{7,6},{8,9},{9,8},{10,11... | collective-permute-start | bytes 3145736 | tf_op jit(solution)/shard_map/ppermute | solution.py:14
  2.9 2.7 %copy-start.1 = (bf16[1024,512]{1,0:T(8,128)(2,1)S(1)}, bf16[1024,512]{1,0:T(8,128)(2,1)}, u32[]{:S(2)}) copy-start(bf16[1024,512]{1,0:T(8,128)(2,1)} %refs_4_.3) | copy-start | bytes 3145732
  2.9 2.7 %copy-start.5 = (bf16[16,16,128]{2,1,0:T(8,128)(2,1)S(1)}, bf16[16,16,128]{2,1,0:T(8,128)(2,1)}, u32[]{:S(2)}) copy-start(bf16[16,16,128]{2,1,0:T(8,128)(2,1)} %param.13) | copy-start | bytes 196612
  4.2 13.1 %copy-start.3 = (bf16[2,128,128]{2,1,0:T(8,128)(2,1)S(1)}, bf16[2,128,128]{2,1,0:T(8,128)(2,1)}, u32[]{:S(2)}) copy-start(bf16[2,128,128]{2,1,0:T(8,128)(2,1)} %param.11) | copy-start | bytes 196612
  4.2 13.1 %copy-start.4 = (bf16[2,128,128]{2,1,0:T(8,128)(2,1)S(1)}, bf16[2,128,128]{2,1,0:T(8,128)(2,1)}, u32[]{:S(2)}) copy-start(bf16[2,128,128]{2,1,0:T(8,128)(2,1)} %param.12) | copy-start | bytes 196612
  4.2 13.1 %copy-start.6 = (s32[128]{0:T(128)S(1)}, s32[128]{0:T(128)}, u32[]{:S(2)}) copy-start(s32[128]{0:T(128)} %param.14) | copy-start | bytes 1540
  4.2 13.1 %copy-start.7 = (s32[128]{0:T(128)S(1)}, s32[128]{0:T(128)}, u32[]{:S(2)}) copy-start(s32[128]{0:T(128)} %param.15) | copy-start | bytes 1540
  6.5 7.8 %collective-permute-start.4 = (bf16[128,512]{1,0:T(8,128)(2,1)S(1)}, bf16[128,512]{1,0:T(8,128)(2,1)S(1)}, u32[]{:S(2)}, u32[]{:S(2)}) collective-permute-start(bf16[128,512]{1,0:T(8,128)(2,1)S(1)} %get-tuple-element.59), channel_id=1, source_target_pairs={{0,6},{1,7},{2,4},{3,5},{4,2},{5,3},{6,0},{7,1},{8,14},{9,15},{10,... | collective-permute-start | bytes 393224 | tf_op jit(solution)/shard_map/ppermute | solution.py:415
  10.4 6.6 %collective-permute-start.5 = (bf16[128,512]{1,0:T(8,128)(2,1)S(1)}, bf16[128,512]{1,0:T(8,128)(2,1)S(1)}, u32[]{:S(2)}, u32[]{:S(2)}) collective-permute-start(bf16[128,512]{1,0:T(8,128)(2,1)S(1)} %get-tuple-element.60), channel_id=1, source_target_pairs={{0,4},{1,5},{2,6},{3,7},{4,0},{5,1},{6,2},{7,3},{8,12},{9,13},{10,... | collective-permute-start | bytes 393224 | tf_op jit(solution)/shard_map/ppermute | solution.py:415
  10.9 6.4 %collective-permute-start.6 = (bf16[128,512]{1,0:T(8,128)(2,1)S(1)}, bf16[128,512]{1,0:T(8,128)(2,1)S(1)}, u32[]{:S(2)}, u32[]{:S(2)}) collective-permute-start(bf16[128,512]{1,0:T(8,128)(2,1)S(1)} %get-tuple-element.61), channel_id=1, source_target_pairs={{0,2},{1,3},{2,0},{3,1},{4,6},{5,7},{6,4},{7,5},{8,10},{9,11},{10,... | collective-permute-start | bytes 393224 | tf_op jit(solution)/shard_map/ppermute | solution.py:415
  18.6 7.8 %collective-permute-start.7 = (bf16[128,512]{1,0:T(8,128)(2,1)S(1)}, bf16[128,512]{1,0:T(8,128)(2,1)S(1)}, u32[]{:S(2)}, u32[]{:S(2)}) collective-permute-start(bf16[128,512]{1,0:T(8,128)(2,1)S(1)} %get-tuple-element.63), channel_id=1, source_target_pairs={{0,2},{1,3},{2,0},{3,1},{4,6},{5,7},{6,4},{7,5},{8,10},{9,11},{10,... | collective-permute-start | bytes 393224 | tf_op jit(solution)/shard_map/ppermute | solution.py:415
  20.2 7.9 %collective-permute-start.8 = (bf16[128,512]{1,0:T(8,128)(2,1)S(1)}, bf16[128,512]{1,0:T(8,128)(2,1)S(1)}, u32[]{:S(2)}, u32[]{:S(2)}) collective-permute-start(bf16[128,512]{1,0:T(8,128)(2,1)S(1)} %get-tuple-element.64), channel_id=1, source_target_pairs={{0,4},{1,5},{2,6},{3,7},{4,0},{5,1},{6,2},{7,3},{8,12},{9,13},{10,... | collective-permute-start | bytes 393224 | tf_op jit(solution)/shard_map/ppermute | solution.py:415
  20.8 7.3 %collective-permute-start.9 = (bf16[128,512]{1,0:T(8,128)(2,1)S(1)}, bf16[128,512]{1,0:T(8,128)(2,1)S(1)}, u32[]{:S(2)}, u32[]{:S(2)}) collective-permute-start(bf16[128,512]{1,0:T(8,128)(2,1)S(1)} %get-tuple-element.65), channel_id=1, source_target_pairs={{0,6},{1,7},{2,4},{3,5},{4,2},{5,3},{6,0},{7,1},{8,14},{9,15},{10,... | collective-permute-start | bytes 393224 | tf_op jit(solution)/shard_map/ppermute | solution.py:415
  22.8 8.1 %collective-permute-start.11 = (bf16[512,128]{1,0:T(8,128)(2,1)S(1)}, bf16[512,128]{1,0:T(8,128)(2,1)S(1)}, u32[]{:S(2)}, u32[]{:S(2)}) collective-permute-start(bf16[512,128]{1,0:T(8,128)(2,1)S(1)} %shard_map.131.refs_9_.left_ref), channel_id=1, source_target_pairs={{0,24},{8,16},{16,8},{24,0},{1,25},{9,17},{17,9},{25,1},{2,26},{10... | collective-permute-start | bytes 393224 | tf_op jit(solution)/shard_map/ppermute | solution.py:491
  29.6 1.3 %collective-permute-start.10 = (bf16[256,128]{1,0:T(8,128)(2,1)S(1)}, bf16[256,128]{1,0:T(8,128)(2,1)S(1)}, u32[]{:S(2)}, u32[]{:S(2)}) collective-permute-start(bf16[256,128]{1,0:T(8,128)(2,1)S(1)} %get-tuple-element.78), channel_id=1, source_target_pairs={{0,1},{1,0},{2,3},{3,2},{4,5},{5,4},{6,7},{7,6},{8,9},{9,8},{10,11... | collective-permute-start | bytes 196616 | tf_op jit(solution)/shard_map/ppermute | solution.py:14
  31.0 11.7 %collective-permute-start.12 = (bf16[2048,512]{1,0:T(8,128)(2,1)S(1)}, bf16[2048,512]{1,0:T(8,128)(2,1)S(1)}, u32[]{:S(2)}, u32[]{:S(2)}) collective-permute-start(bf16[2048,512]{1,0:T(8,128)(2,1)S(1)} %get-tuple-element.80), channel_id=1, source_target_pairs={{0,1},{1,0},{2,3},{3,2},{4,5},{5,4},{6,7},{7,6},{8,9},{9,8},{10,11... | collective-permute-start | bytes 6291464 | tf_op jit(solution)/shard_map/ppermute | solution.py:14
  31.5 8.2 %collective-permute-start.14 = (bf16[512,128]{1,0:T(8,128)(2,1)S(1)}, bf16[512,128]{1,0:T(8,128)(2,1)S(1)}, u32[]{:S(2)}, u32[]{:S(2)}) collective-permute-start(bf16[512,128]{1,0:T(8,128)(2,1)S(1)} %get-tuple-element.85.refs_0_), channel_id=1, source_target_pairs={{0,24},{8,16},{16,8},{24,0},{1,25},{9,17},{17,9},{25,1},{2,26},{10... | collective-permute-start | bytes 393224 | tf_op jit(solution)/shard_map/ppermute | solution.py:491
  35.1 6.8 %collective-permute-start.13 = (bf16[512,128]{1,0:T(8,128)(2,1)S(1)}, bf16[512,128]{1,0:T(8,128)(2,1)S(1)}, u32[]{:S(2)}, u32[]{:S(2)}) collective-permute-start(bf16[512,128]{1,0:T(8,128)(2,1)S(1)} %get-tuple-element.81.sum_ref), channel_id=1, source_target_pairs={{0,8},{8,0},{16,24},{24,16},{1,9},{9,1},{17,25},{25,17},{2,10},{10... | collective-permute-start | bytes 393224 | tf_op jit(solution)/shard_map/ppermute | solution.py:491
  39.8 5.0 %collective-permute-start.15 = (bf16[512,128]{1,0:T(8,128)(2,1)S(1)}, bf16[512,128]{1,0:T(8,128)(2,1)S(1)}, u32[]{:S(2)}, u32[]{:S(2)}) collective-permute-start(bf16[512,128]{1,0:T(8,128)(2,1)S(1)} %shard_map.137.refs_0_), channel_id=1, source_target_pairs={{0,8},{8,0},{16,24},{24,16},{1,9},{9,1},{17,25},{25,17},{2,10},{10... | collective-permute-start | bytes 393224 | tf_op jit(solution)/shard_map/ppermute | solution.py:491

commit v4 on v3

--- a/solution.py
+++ b/solution.py
@@ -138,7 +138,7 @@
 
 
 VMEM_LIMIT = 16 * 2**20
-COL_MICROS = 0.5
+COL_MICROS = 28
 
 
 def dot(left, right, left_dim=1, right_dim=0):
@@ -318,7 +318,7 @@
 
     def body(*refs):
         bufs, (tok_ref, x_ref, cot_ref, d_ref, order_ref) = refs[:chips], refs[chips : chips + 5]
-        kept_ref, leave_ref, back_ref, grad_ref = refs[-4:]
+        grads_ref, back_ref, grad_ref = refs[-3:]
         parity = lax.axis_index("loop") % 2
         pair_blocks = tok_ref.shape[0] // half
         unit = 2 * rows * cols
@@ -334,26 +334,17 @@
                 grads.append(dot(grid_ref[part, :], features, 1, 1))
             both = own_first(jnp.concatenate(grads, 0), parity).astype(narrow)
             size = both.shape[0] // 2
-            kept_ref[at * size : (at + 1) * size, :] = both[:size]
-            leave_ref[at * size : (at + 1) * size, :] = both[size:]
-
-    return body
-
-
-def join(kept_ref, came_ref, left_ref, right_ref, *rest):
-    out_ref, sum_ref = rest[-3:-1]
-    size = kept_ref.shape[0] // 2
-    for at in range(2):
-        span = slice(at * size, (at + 1) * size)
-        for off, ref in enumerate((kept_ref, came_ref)):
-            out_ref[(2 * at + off) * size : (2 * at + off + 1) * size, :] = ref[span, :]
-    total = left_ref[...].astype(jnp.float32) + right_ref[...].astype(jnp.float32)
-    sum_ref[...] = total.astype(sum_ref.dtype)
+            for turn in range(2):
+                start = (2 * turn + at) * size
+                grads_ref[start : start + size, :] = both[turn * size : (turn + 1) * size]
+
+    return body
 
 
 def row_outputs(half):
     def body(*refs):
-        jobs, (*kept_refs, sent_ref) = (refs[:3], refs[3:6]), refs[6:]
+        jobs, col_refs, (*kept_refs, sent_ref, sum_ref) = (refs[:3], refs[3:6]), refs[6:8], refs[8:]
+        add(*col_refs, sum_ref)
         parity = lax.axis_index("loop") % 2
         for at, (grid_ref, own_ref, weights_ref) in enumerate(jobs):
             kept_ref, features = kept_refs[at], own_ref.shape[0]
@@ -378,20 +369,28 @@
     done_ref[...] = jnp.zeros_like(done_ref)
 
 
-def add(*refs):
-    left_ref, right_ref, out_ref = refs[-3:]
+def add(left_ref, right_ref, out_ref):
     total = left_ref[...].astype(jnp.float32) + right_ref[...].astype(jnp.float32)
     out_ref[...] = total.astype(out_ref.dtype)
 
 
+def add_halves(left_ref, right_ref, kept_ref, leave_ref):
+    size = kept_ref.shape[0]
+    for at, out in enumerate((kept_ref, leave_ref)):
+        span = slice(at * size, (at + 1) * size)
+        total = left_ref[span, :].astype(jnp.float32) + right_ref[span, :].astype(jnp.float32)
+        out[...] = total.astype(out.dtype)
+
+
 def total_grads(scale):
     def body(*refs):
-        pair, place_ref, outs = refs[:2], refs[2], refs[-2:]
-        place = jnp.concatenate([place_ref[...]] * 2, 1)
-        size = outs[0].shape[0]
+        parts, place_ref, outs = refs[:4], refs[4], refs[-2:]
+        size = parts[0].shape[0] // 2
+        near, far = place_ref[:, :size], place_ref[:, size:]
+        place = jnp.concatenate([near, near, far, far], 1)
         for at, out in enumerate(outs):
             span = slice(at * size, (at + 1) * size)
-            out[...] = dot(place, jnp.concatenate([r[span, :] for r in pair], 0)) * scale
+            out[...] = dot(place, jnp.concatenate([r[span, :] for r in parts], 0)) * scale
 
     return body
 
@@ -490,9 +489,9 @@
     def over_dp(value, apart):
         return lax.ppermute(value, "dp", [(s, s ^ apart) for s in range(dps)])
 
-    kept, leaving, back_rows, grad_rows = call(
+    sums, back_rows, grad_rows = call(
         row_grads(chips, rows, cols, half),
-        [taken] * 2 + [grid] * 2,
+        [struct(2 * grid_rows, block), grid, grid],
         *back,
         tokens,
         other_x,
@@ -501,29 +500,28 @@
         order_back,
         col_grads,
     )
+    sums_got = over_dp(sums, dps - 1)
     partial = struct(feature_rows, toks, wide)
     both = struct(2 * feature_rows, toks)
-    mixed, grad_tokens, branches = call(
+    mixed, grad_tokens, branches, col_sum = call(
         row_outputs(half),
-        [partial, partial, both],
+        [partial, partial, both, struct(*col_grads.shape)],
         back_rows,
         tokens,
         down_taken,
         grad_rows,
         cotangent,
         up_taken,
-    )
-    sums, col_sum, branches = call(
-        join,
-        [struct(2 * grid_rows, block), struct(*col_grads.shape), both],
-        kept,
-        from_partner(leaving, "loop", 0),
         col_grads,
         over_dp(col_grads, dps - 1),
-        branches,
-        aliases=((4, 2),),
-    )
-    (sums,) = call(add, [struct(*sums.shape)], sums, over_dp(sums, dps - 1))
+    )
+    kept, leaving = call(add_halves, [taken, taken], sums, sums_got)
+
+    def to_partner(value, apart):
+        pairs = [(s, s ^ (apart * loops + 1)) for s in range(dps * loops)]
+        return lax.ppermute(value, ("dp", "loop"), pairs)
+
+    parts = (kept, over_dp(kept, 1), to_partner(leaving, 1), from_partner(leaving, "loop", 0))
     scale = 1.0 / math.sqrt(dps * toks)
     token = struct(8, 128, wide)
     g_up_second, g_down_first, done = call(
@@ -546,8 +544,7 @@
     g_up_first, g_down_second = call(
         total_grads(scale),
         [struct(rows * all_cols, block, wide)] * 2,
-        sums,
-        over_dp(sums, 1),
+        *parts,
         place,
         done,
         to_hbm=2,

time: 45.9 us -> 43.9 us (0.956)
  waiting for transfers between devices: 16.2 us -> 14.3 us
    ppermute x4, waiting for transfers between devices: 5.55 us -> 3.59 us  [over_dp(): return lax.ppermute(value, 'dp', [(s, s ^ apart) for s in range(dps)])]
    pallas_call x12 -> x11, Pallas kernels: 9.84 us -> 9.81 us  [call(): pl.pallas_call(body, out_shape=outs, in_specs=[whole] * len(args), out_sp...]
  transfers between devices with their start and end apart: 16 -> 17, of which waited for: 11 -> 10; matrix products, arithmetic and copies ran while one was open for 0% -> 0% of each run, Pallas kernels for 15% -> 15%
where the time goes in v4:
time: 43.9 us; the launch traced here: 43.8 us
  starting transfers between devices  18.9 us (43%)
  waiting for transfers between devices  14.3 us (33%)
  Pallas kernels  9.81 us (22%)
  between operations  0.76 us (2%)
    pallas_call x11, Pallas kernels, call(): pl.pallas_call(body, out_shape=outs, in_specs=[whole] * len(args), out_sp...  9.81 us
    ppermute x4, starting transfers between devices, over_dp(): return lax.ppermute(value, 'dp', [(s, s ^ apart) for s in range(dps)])  8.68 us
    ppermute x6, starting transfers between devices, exchange(): return [bufs[0]] + [lax.ppermute(bufs[q], axis, pairs[q]) for q in order]  8.07 us
    ppermute x6, waiting for transfers between devices, exchange(): return [bufs[0]] + [lax.ppermute(bufs[q], axis, pairs[q]) for q in order]  7.86 us
    ppermute x4, waiting for transfers between devices, over_dp(): return lax.ppermute(value, 'dp', [(s, s ^ apart) for s in range(dps)])  3.59 us
    ppermute x6, waiting for transfers between devices, from_partner(): return lax.ppermute(value, axis, pairs)  2.8 us
    ppermute x6, starting transfers between devices, from_partner(): return lax.ppermute(value, axis, pairs)  2.07 us
  transfers between devices with their start and end apart: 17, of which 10 were waited for; matrix products, arithmetic and copies ran while one was open for 0% of the time, Pallas kernels for 15%

profile of v4, /device:TPU:0, one launch (start us, length us, event | category | flops | bytes accessed | tf_op | source)
XLA Modules:
  0.0 43.8 jit_solution(14988131982923777959)
XLA Ops:
  1.7 0.6 %collective-permute-done.refs_3_ = bf16[256,128]{1,0:T(8,128)(2,1)S(1)} collective-permute-done((bf16[256,128]{1,0:T(8,128)(2,1)}, bf16[256,128]{1,0:T(8,128)(2,1)S(1)}, u32[]{:S(2)}, u32[]{:S(2)}) %collective-permute-start) | collective-permute-done | bytes 65568 | tf_op jit(solution)/shard_map/ppermute | solution.py:14
  2.9 1.2 %collective-permute-done.3.refs_1_.refs_5_ = bf16[1024,512]{1,0:T(8,128)(2,1)S(1)} collective-permute-done((bf16[1024,512]{1,0:T(8,128)(2,1)}, bf16[1024,512]{1,0:T(8,128)(2,1)S(1)}, u32[]{:S(2)}, u32[]{:S(2)}) %collective-permute-start.3) | collective-permute-done | bytes 1048608 | tf_op jit(solution)/shard_map/ppermute | solution.py:14
  4.2 0.8 %shard_map.128 = (bf16[64,512]{1,0:T(8,128)(2,1)S(1)}, bf16[64,512]{1,0:T(8,128)(2,1)S(1)}, bf16[64,512]{1,0:T(8,128)(2,1)S(1)}, bf16[64,512]{1,0:T(8,128)(2,1)S(1)}, bf16[256,128]{1,0:T(8,128)(2,1)S(1)}) custom-call(bf16[1024,512]{1,0:T(8,128)(2,1)S(1)} %copy-done, bf16[1024,512]{1,0:T(8,128)(2,1)S(1)} %collective-permute-done.3.refs_1_.refs_5_, ...), custom_call_target="tpu_custom_call" | custom-call | flops 10000000 | bytes 30000 | tf_op jit(solution)/shard_map/pallas_call | solution.py:152
  5.0 0.6 %collective-permute-done.2.refs_1_.refs_7_ = bf16[1024,512]{1,0:T(8,128)(2,1)S(1)} collective-permute-done((bf16[1024,512]{1,0:T(8,128)(2,1)}, bf16[1024,512]{1,0:T(8,128)(2,1)S(1)}, u32[]{:S(2)}, u32[]{:S(2)}) %collective-permute-start.2) | collective-permute-done | bytes 1048608 | tf_op jit(solution)/shard_map/ppermute | solution.py:14
  5.7 0.8 %shard_map.129 = (bf16[128,512]{1,0:T(8,128)(2,1)S(1)}, bf16[128,512]{1,0:T(8,128)(2,1)S(1)}, bf16[128,512]{1,0:T(8,128)(2,1)S(1)}, bf16[128,512]{1,0:T(8,128)(2,1)S(1)}, bf16[256,128]{1,0:T(8,128)(2,1)S(1)}) custom-call(bf16[1024,512]{1,0:T(8,128)(2,1)S(1)} %copy-done.1, bf16[1024,512]{1,0:T(8,128)(2,1)S(1)} %collective-permute-done.2.refs_1_.refs_7_, ...), custom_call_target="tpu_custom_call" | custom-call | flops 10000000 | bytes 30000 | tf_op jit(solution)/shard_map/pallas_call | solution.py:152
  6.5 3.9 %collective-permute-start.4 = (bf16[128,512]{1,0:T(8,128)(2,1)S(1)}, bf16[128,512]{1,0:T(8,128)(2,1)S(1)}, u32[]{:S(2)}, u32[]{:S(2)}) collective-permute-start(bf16[128,512]{1,0:T(8,128)(2,1)S(1)} %get-tuple-element.58), channel_id=1, source_target_pairs={{0,6},{1,7},{2,4},{3,5},{4,2},{5,3},{6,0},{7,1},{8,14},{9,15},{10,... | collective-permute-start | bytes 393224 | tf_op jit(solution)/shard_map/ppermute | solution.py:414
  11.0 3.3 %collective-permute-done.4.refs_1_ = bf16[128,512]{1,0:T(8,128)(2,1)S(1)} collective-permute-done((bf16[128,512]{1,0:T(8,128)(2,1)S(1)}, bf16[128,512]{1,0:T(8,128)(2,1)S(1)}, u32[]{:S(2)}, u32[]{:S(2)}) %collective-permute-start.4) | collective-permute-done | bytes 131104 | tf_op jit(solution)/shard_map/ppermute | solution.py:414
  14.3 2.7 %collective-permute-done.5.refs_2_ = bf16[128,512]{1,0:T(8,128)(2,1)S(1)} collective-permute-done((bf16[128,512]{1,0:T(8,128)(2,1)S(1)}, bf16[128,512]{1,0:T(8,128)(2,1)S(1)}, u32[]{:S(2)}, u32[]{:S(2)}) %collective-permute-start.5) | collective-permute-done | bytes 131104 | tf_op jit(solution)/shard_map/ppermute | solution.py:414
  17.3 1.3 %shard_map.130 = (bf16[128,512]{1,0:T(8,128)(2,1)S(1)}, bf16[128,512]{1,0:T(8,128)(2,1)S(1)}, bf16[128,512]{1,0:T(8,128)(2,1)S(1)}, bf16[128,512]{1,0:T(8,128)(2...) custom-call(bf16[128,512]{1,0:T(8,128)(2,1)S(1)} %get-tuple-element., ...), custom_call_target="tpu_custom_call" | custom-call | flops 10000000 | bytes 30000 | tf_op jit(solution)/shard_map/pallas_call | solution.py:152
  18.6 1.6 %collective-permute-start.7 = (bf16[128,512]{1,0:T(8,128)(2,1)S(1)}, bf16[128,512]{1,0:T(8,128)(2,1)S(1)}, u32[]{:S(2)}, u32[]{:S(2)}) collective-permute-start(bf16[128,512]{1,0:T(8,128)(2,1)S(1)} %get-tuple-element.62), channel_id=1, source_target_pairs={{0,2},{1,3},{2,0},{3,1},{4,6},{5,7},{6,4},{7,5},{8,10},{9,11},{10,... | collective-permute-start | bytes 393224 | tf_op jit(solution)/shard_map/ppermute | solution.py:414
  20.2 0.6 %collective-permute-start.8 = (bf16[128,512]{1,0:T(8,128)(2,1)S(1)}, bf16[128,512]{1,0:T(8,128)(2,1)S(1)}, u32[]{:S(2)}, u32[]{:S(2)}) collective-permute-start(bf16[128,512]{1,0:T(8,128)(2,1)S(1)} %get-tuple-element.63), channel_id=1, source_target_pairs={{0,4},{1,5},{2,6},{3,7},{4,0},{5,1},{6,2},{7,3},{8,12},{9,13},{10,... | collective-permute-start | bytes 393224 | tf_op jit(solution)/shard_map/ppermute | solution.py:414
  20.8 1.4 %collective-permute-start.9 = (bf16[128,512]{1,0:T(8,128)(2,1)S(1)}, bf16[128,512]{1,0:T(8,128)(2,1)S(1)}, u32[]{:S(2)}, u32[]{:S(2)}) collective-permute-start(bf16[128,512]{1,0:T(8,128)(2,1)S(1)} %get-tuple-element.64), channel_id=1, source_target_pairs={{0,6},{1,7},{2,4},{3,5},{4,2},{5,3},{6,0},{7,1},{8,14},{9,15},{10,... | collective-permute-start | bytes 393224 | tf_op jit(solution)/shard_map/ppermute | solution.py:414
  22.8 3.7 %collective-permute-start.10 = (bf16[512,128]{1,0:T(8,128)(2,1)S(1)}, bf16[512,128]{1,0:T(8,128)(2,1)S(1)}, u32[]{:S(2)}, u32[]{:S(2)}) collective-permute-start(bf16[512,128]{1,0:T(8,128)(2,1)S(1)} %shard_map.131.refs_9_.refs_6_), channel_id=1, source_target_pairs={{0,24},{8,16},{16,8},{24,0},{1,25},{9,17},{17,9},{25,1},{2,26},{10... | collective-permute-start | bytes 393224 | tf_op jit(solution)/shard_map/ppermute | solution.py:490
  26.4 1.6 %collective-permute-done.8.refs_2_ = bf16[128,512]{1,0:T(8,128)(2,1)S(1)} collective-permute-done((bf16[128,512]{1,0:T(8,128)(2,1)S(1)}, bf16[128,512]{1,0:T(8,128)(2,1)S(1)}, u32[]{:S(2)}, u32[]{:S(2)}) %collective-permute-start.8) | collective-permute-done | bytes 131104 | tf_op jit(solution)/shard_map/ppermute | solution.py:414
  28.1 1.5 %shard_map.132 = (bf16[512,128]{1,0:T(8,128)(2,1)S(1)}, bf16[256,512]{1,0:T(8,128)(2,1)S(1)}, bf16[256,512]{1,0:T(8,128)(2,1)S(1)}) custom-call(bf16[128,512]{1,0:T(8,128)(2,1)S(1)} %get-tuple-element.61.refs_0_, bf16[128,512]{1,0:T(8,128)(2,1)S(1)} %collective-permute-done.7.refs_1_, bf16[128,512]{1,0:T(8,128)(2,1)S(1)} %collective-permute-done.8.refs_2_, ...), custom_call_target="tpu_custom_call" | custom-call | flops 10000000 | bytes 30000 | tf_op jit(solution)/shard_map/pallas_call | solution.py:152
  29.6 3.6 %collective-permute-start.13 = (bf16[512,128]{1,0:T(8,128)(2,1)S(1)}, bf16[512,128]{1,0:T(8,128)(2,1)S(1)}, u32[]{:S(2)}, u32[]{:S(2)}) collective-permute-start(bf16[512,128]{1,0:T(8,128)(2,1)S(1)} %get-tuple-element.81.left_ref), channel_id=1, source_target_pairs={{0,24},{8,16},{16,8},{24,0},{1,25},{9,17},{17,9},{25,1},{2,26},{10... | collective-permute-start | bytes 393224 | tf_op jit(solution)/shard_map/ppermute | solution.py:490
  33.2 1.3 %shard_map.133 = (f32[1024,512]{1,0:T(8,128)S(1)}, f32[1024,512]{1,0:T(8,128)S(1)}, bf16[2048,512]{1,0:T(8,128)(2,1)S(1)}, bf16[512,128]{1,0:T(8,128)(2,1)S(1)}) custom-call(bf16[256,512]{1,0:T(8,128)(2,1)S(1)} %get-tuple-element.70.refs_0_, bf16[1024,512]{1,0:T(8,128)(2,1)S(1)} %copy-done, bf16[256,128]{1,0:T(8,128)(2,1)S(1)} %get-tuple-element.71.refs_2_, ...), custom_call_target="tpu_custom_call" | custom-call | flops 10000000 | bytes 30000 | tf_op jit(solution)/shard_map/pallas_call | solution.py:152
  34.7 3.0 %collective-permute-done.13.right_ref = bf16[512,128]{1,0:T(8,128)(2,1)S(1)} collective-permute-done((bf16[512,128]{1,0:T(8,128)(2,1)S(1)}, bf16[512,128]{1,0:T(8,128)(2,1)S(1)}, u32[]{:S(2)}, u32[]{:S(2)}) %collective-permute-start.13) | collective-permute-done | bytes 131104 | tf_op jit(solution)/shard_map/ppermute | solution.py:490
  37.7 0.8 %collective-permute-start.16 = (bf16[256,128]{1,0:T(8,128)(2,1)S(1)}, bf16[256,128]{1,0:T(8,128)(2,1)S(1)}, u32[]{:S(2)}, u32[]{:S(2)}) collective-permute-start(bf16[256,128]{1,0:T(8,128)(2,1)S(1)} %get-tuple-element.83), channel_id=1, source_target_pairs={{0,1},{1,0},{2,3},{3,2},{4,5},{5,4},{6,7},{7,6},{8,9},{9,8},{10,11... | collective-permute-start | bytes 196616 | tf_op jit(solution)/shard_map/ppermute | solution.py:14
  38.5 1.3 %collective-permute-start.14 = (bf16[256,128]{1,0:T(8,128)(2,1)S(1)}, bf16[256,128]{1,0:T(8,128)(2,1)S(1)}, u32[]{:S(2)}, u32[]{:S(2)}) collective-permute-start(bf16[256,128]{1,0:T(8,128)(2,1)S(1)} %get-tuple-element.82.refs_0_), channel_id=1, source_target_pairs={{0,8},{8,0},{16,24},{24,16},{1,9},{9,1},{17,25},{25,17},{2,10},{10... | collective-permute-start | bytes 196616 | tf_op jit(solution)/shard_map/ppermute | solution.py:490
  39.9 0.7 %shard_map.134 = (f32[256,128]{1,0:T(8,128)}, f32[256,128]{1,0:T(8,128)}, f32[8,128]{1,0:T(8,128)S(1)}) custom-call(bf16[512,128]{1,0:T(8,128)(2,1)S(1)} %get-tuple-element.77.sum_ref, bf16[512,128]{1,0:T(8,128)(2,1)S(1)} %collective-permute-done.12.got_ref), custom_call_target="tpu_custom_call" | custom-call | flops 28000000000 | bytes 84000000 | tf_op jit(solution)/shard_map/pallas_call | solution.py:152
  40.6 1.6 %shard_map.135 = (bf16[1024,512]{1,0:T(8,128)(2,1)}, bf16[1024,512]{1,0:T(8,128)(2,1)}, f32[8,128]{1,0:T(8,128)S(1)}) custom-call(f32[1024,512]{1,0:T(8,128)S(1)} %get-tuple-element.74.mixed_ref, f32[1024,512]{1,0:T(8,128)S(1)} %get-tuple-element.75.grad_ref, bf16[2048,512]{1,0:T(8,128)(2,1)S(1)} %collective-permute-done.11.got_ref, ...), custom_call_target="tpu_custom_call" | custom-call | flops 10000000 | bytes 30000 | tf_op jit(solution)/shard_map/pallas_call | solution.py:152
  42.2 0.6 %collective-permute-done.14.refs_1_ = bf16[256,128]{1,0:T(8,128)(2,1)S(1)} collective-permute-done((bf16[256,128]{1,0:T(8,128)(2,1)S(1)}, bf16[256,128]{1,0:T(8,128)(2,1)S(1)}, u32[]{:S(2)}, u32[]{:S(2)}) %collective-permute-start.14) | collective-permute-done | bytes 65568 | tf_op jit(solution)/shard_map/ppermute | solution.py:490
  42.8 0.9 %shard_map.137 = (f32[256,128]{1,0:T(8,128)}, f32[256,128]{1,0:T(8,128)}) custom-call(bf16[256,128]{1,0:T(8,128)(2,1)S(1)} %get-tuple-element.82.refs_0_, bf16[256,128]{1,0:T(8,128)(2,1)S(1)} %collective-permute-done.14.refs_1_, bf16[256,128]{1,0:T(8,128)(2,1)S(1)} %collective-permute-done.15.refs_2_, bf16[256,128]{1,0:T(8,128)(2,1)S(1)} %collective-permute-done.16.refs_3_, ...), custom_call_target="tpu_custom_call" | custom-call | flops 10000000 | bytes 30000 | tf_op jit(solution)/shard_map/pallas_call | solution.py:152
  (37 shorter events, 3.5 us)
Async XLA Ops:
  0.6 1.6 %collective-permute-start = (bf16[256,128]{1,0:T(8,128)(2,1)}, bf16[256,128]{1,0:T(8,128)(2,1)S(1)}, u32[]{:S(2)}, u32[]{:S(2)}) collective-permute-start(bf16[256,128]{1,0:T(8,128)(2,1)} %bitcast.10), channel_id=1, source_target_pairs={{0,1},{1,0},{2,3},{3,2},{4,5},{5,4},{6,7},{7,6},{8,9},{9,8},{10,11... | collective-permute-start | bytes 196616 | tf_op jit(solution)/shard_map/ppermute | solution.py:14
  1.1 3.0 %copy-start = (bf16[1024,512]{1,0:T(8,128)(2,1)S(1)}, bf16[1024,512]{1,0:T(8,128)(2,1)}, u32[]{:S(2)}) copy-start(bf16[1024,512]{1,0:T(8,128)(2,1)} %refs_1_.1) | copy-start | bytes 3145732
  1.2 3.0 %copy-start.2 = (bf16[16,16,128]{2,1,0:T(8,128)(2,1)S(1)}, bf16[16,16,128]{2,1,0:T(8,128)(2,1)}, u32[]{:S(2)}) copy-start(bf16[16,16,128]{2,1,0:T(8,128)(2,1)} %param.10) | copy-start | bytes 196612
  1.2 1.5 %collective-permute-start.1 = (bf16[256,128]{1,0:T(8,128)(2,1)}, bf16[256,128]{1,0:T(8,128)(2,1)S(1)}, u32[]{:S(2)}, u32[]{:S(2)}) collective-permute-start(bf16[256,128]{1,0:T(8,128)(2,1)} %bitcast.14), channel_id=1, source_target_pairs={{0,1},{1,0},{2,3},{3,2},{4,5},{5,4},{6,7},{7,6},{8,9},{9,8},{10,11... | collective-permute-start | bytes 196616 | tf_op jit(solution)/shard_map/ppermute | solution.py:14
  1.2 2.9 %collective-permute-start.3 = (bf16[1024,512]{1,0:T(8,128)(2,1)}, bf16[1024,512]{1,0:T(8,128)(2,1)S(1)}, u32[]{:S(2)}, u32[]{:S(2)}) collective-permute-start(bf16[1024,512]{1,0:T(8,128)(2,1)} %refs_1_.1), channel_id=1, source_target_pairs={{0,1},{1,0},{2,3},{3,2},{4,5},{5,4},{6,7},{7,6},{8,9},{9,8},{10,11... | collective-permute-start | bytes 3145736 | tf_op jit(solution)/shard_map/ppermute | solution.py:14
  2.6 3.0 %collective-permute-start.2 = (bf16[1024,512]{1,0:T(8,128)(2,1)}, bf16[1024,512]{1,0:T(8,128)(2,1)S(1)}, u32[]{:S(2)}, u32[]{:S(2)}) collective-permute-start(bf16[1024,512]{1,0:T(8,128)(2,1)} %refs_4_.3), channel_id=1, source_target_pairs={{0,1},{1,0},{2,3},{3,2},{4,5},{5,4},{6,7},{7,6},{8,9},{9,8},{10,11... | collective-permute-start | bytes 3145736 | tf_op jit(solution)/shard_map/ppermute | solution.py:14
  2.9 2.7 %copy-start.1 = (bf16[1024,512]{1,0:T(8,128)(2,1)S(1)}, bf16[1024,512]{1,0:T(8,128)(2,1)}, u32[]{:S(2)}) copy-start(bf16[1024,512]{1,0:T(8,128)(2,1)} %refs_4_.3) | copy-start | bytes 3145732
  4.2 13.1 %copy-start.3 = (bf16[2,128,128]{2,1,0:T(8,128)(2,1)S(1)}, bf16[2,128,128]{2,1,0:T(8,128)(2,1)}, u32[]{:S(2)}) copy-start(bf16[2,128,128]{2,1,0:T(8,128)(2,1)} %param.11) | copy-start | bytes 196612
  4.2 13.1 %copy-start.4 = (bf16[2,128,128]{2,1,0:T(8,128)(2,1)S(1)}, bf16[2,128,128]{2,1,0:T(8,128)(2,1)}, u32[]{:S(2)}) copy-start(bf16[2,128,128]{2,1,0:T(8,128)(2,1)} %param.12) | copy-start | bytes 196612
  4.2 13.1 %copy-start.6 = (s32[128]{0:T(128)S(1)}, s32[128]{0:T(128)}, u32[]{:S(2)}) copy-start(s32[128]{0:T(128)} %param.14) | copy-start | bytes 1540
  4.2 13.1 %copy-start.7 = (s32[128]{0:T(128)S(1)}, s32[128]{0:T(128)}, u32[]{:S(2)}) copy-start(s32[128]{0:T(128)} %param.15) | copy-start | bytes 1540
  6.5 7.8 %collective-permute-start.4 = (bf16[128,512]{1,0:T(8,128)(2,1)S(1)}, bf16[128,512]{1,0:T(8,128)(2,1)S(1)}, u32[]{:S(2)}, u32[]{:S(2)}) collective-permute-start(bf16[128,512]{1,0:T(8,128)(2,1)S(1)} %get-tuple-element.58), channel_id=1, source_target_pairs={{0,6},{1,7},{2,4},{3,5},{4,2},{5,3},{6,0},{7,1},{8,14},{9,15},{10,... | collective-permute-start | bytes 393224 | tf_op jit(solution)/shard_map/ppermute | solution.py:414
  10.4 6.6 %collective-permute-start.5 = (bf16[128,512]{1,0:T(8,128)(2,1)S(1)}, bf16[128,512]{1,0:T(8,128)(2,1)S(1)}, u32[]{:S(2)}, u32[]{:S(2)}) collective-permute-start(bf16[128,512]{1,0:T(8,128)(2,1)S(1)} %get-tuple-element.59), channel_id=1, source_target_pairs={{0,4},{1,5},{2,6},{3,7},{4,0},{5,1},{6,2},{7,3},{8,12},{9,13},{10,... | collective-permute-start | bytes 393224 | tf_op jit(solution)/shard_map/ppermute | solution.py:414
  10.9 6.4 %collective-permute-start.6 = (bf16[128,512]{1,0:T(8,128)(2,1)S(1)}, bf16[128,512]{1,0:T(8,128)(2,1)S(1)}, u32[]{:S(2)}, u32[]{:S(2)}) collective-permute-start(bf16[128,512]{1,0:T(8,128)(2,1)S(1)} %get-tuple-element.60), channel_id=1, source_target_pairs={{0,2},{1,3},{2,0},{3,1},{4,6},{5,7},{6,4},{7,5},{8,10},{9,11},{10,... | collective-permute-start | bytes 393224 | tf_op jit(solution)/shard_map/ppermute | solution.py:414
  18.6 7.8 %collective-permute-start.7 = (bf16[128,512]{1,0:T(8,128)(2,1)S(1)}, bf16[128,512]{1,0:T(8,128)(2,1)S(1)}, u32[]{:S(2)}, u32[]{:S(2)}) collective-permute-start(bf16[128,512]{1,0:T(8,128)(2,1)S(1)} %get-tuple-element.62), channel_id=1, source_target_pairs={{0,2},{1,3},{2,0},{3,1},{4,6},{5,7},{6,4},{7,5},{8,10},{9,11},{10,... | collective-permute-start | bytes 393224 | tf_op jit(solution)/shard_map/ppermute | solution.py:414
  20.2 7.9 %collective-permute-start.8 = (bf16[128,512]{1,0:T(8,128)(2,1)S(1)}, bf16[128,512]{1,0:T(8,128)(2,1)S(1)}, u32[]{:S(2)}, u32[]{:S(2)}) collective-permute-start(bf16[128,512]{1,0:T(8,128)(2,1)S(1)} %get-tuple-element.63), channel_id=1, source_target_pairs={{0,4},{1,5},{2,6},{3,7},{4,0},{5,1},{6,2},{7,3},{8,12},{9,13},{10,... | collective-permute-start | bytes 393224 | tf_op jit(solution)/shard_map/ppermute | solution.py:414
  20.8 7.3 %collective-permute-start.9 = (bf16[128,512]{1,0:T(8,128)(2,1)S(1)}, bf16[128,512]{1,0:T(8,128)(2,1)S(1)}, u32[]{:S(2)}, u32[]{:S(2)}) collective-permute-start(bf16[128,512]{1,0:T(8,128)(2,1)S(1)} %get-tuple-element.64), channel_id=1, source_target_pairs={{0,6},{1,7},{2,4},{3,5},{4,2},{5,3},{6,0},{7,1},{8,14},{9,15},{10,... | collective-permute-start | bytes 393224 | tf_op jit(solution)/shard_map/ppermute | solution.py:414
  22.8 10.5 %collective-permute-start.10 = (bf16[512,128]{1,0:T(8,128)(2,1)S(1)}, bf16[512,128]{1,0:T(8,128)(2,1)S(1)}, u32[]{:S(2)}, u32[]{:S(2)}) collective-permute-start(bf16[512,128]{1,0:T(8,128)(2,1)S(1)} %shard_map.131.refs_9_.refs_6_), channel_id=1, source_target_pairs={{0,24},{8,16},{16,8},{24,0},{1,25},{9,17},{17,9},{25,1},{2,26},{10... | collective-permute-start | bytes 393224 | tf_op jit(solution)/shard_map/ppermute | solution.py:490
  29.6 8.0 %collective-permute-start.13 = (bf16[512,128]{1,0:T(8,128)(2,1)S(1)}, bf16[512,128]{1,0:T(8,128)(2,1)S(1)}, u32[]{:S(2)}, u32[]{:S(2)}) collective-permute-start(bf16[512,128]{1,0:T(8,128)(2,1)S(1)} %get-tuple-element.81.left_ref), channel_id=1, source_target_pairs={{0,24},{8,16},{16,8},{24,0},{1,25},{9,17},{17,9},{25,1},{2,26},{10... | collective-permute-start | bytes 393224 | tf_op jit(solution)/shard_map/ppermute | solution.py:490
  34.5 5.4 %collective-permute-start.12 = (bf16[512,128]{1,0:T(8,128)(2,1)S(1)}, bf16[512,128]{1,0:T(8,128)(2,1)S(1)}, u32[]{:S(2)}, u32[]{:S(2)}) collective-permute-start(bf16[512,128]{1,0:T(8,128)(2,1)S(1)} %get-tuple-element.77.sum_ref), channel_id=1, source_target_pairs={{0,8},{8,0},{16,24},{24,16},{1,9},{9,1},{17,25},{25,17},{2,10},{10... | collective-permute-start | bytes 393224 | tf_op jit(solution)/shard_map/ppermute | solution.py:490
  34.6 6.0 %collective-permute-start.11 = (bf16[2048,512]{1,0:T(8,128)(2,1)S(1)}, bf16[2048,512]{1,0:T(8,128)(2,1)S(1)}, u32[]{:S(2)}, u32[]{:S(2)}) collective-permute-start(bf16[2048,512]{1,0:T(8,128)(2,1)S(1)} %get-tuple-element.76), channel_id=1, source_target_pairs={{0,1},{1,0},{2,3},{3,2},{4,5},{5,4},{6,7},{7,6},{8,9},{9,8},{10,11... | collective-permute-start | bytes 6291464 | tf_op jit(solution)/shard_map/ppermute | solution.py:14
  37.6 5.2 %collective-permute-start.15 = (bf16[256,128]{1,0:T(8,128)(2,1)S(1)}, bf16[256,128]{1,0:T(8,128)(2,1)S(1)}, u32[]{:S(2)}, u32[]{:S(2)}) collective-permute-start(bf16[256,128]{1,0:T(8,128)(2,1)S(1)} %get-tuple-element.83), channel_id=1, source_target_pairs={{0,9},{1,8},{2,11},{3,10},{4,13},{5,12},{6,15},{7,14},{8,1},{9,0},... | collective-permute-start | bytes 196616 | tf_op jit(solution)/shard_map/ppermute | solution.py:522
  37.7 5.1 %collective-permute-start.16 = (bf16[256,128]{1,0:T(8,128)(2,1)S(1)}, bf16[256,128]{1,0:T(8,128)(2,1)S(1)}, u32[]{:S(2)}, u32[]{:S(2)}) collective-permute-start(bf16[256,128]{1,0:T(8,128)(2,1)S(1)} %get-tuple-element.83), channel_id=1, source_target_pairs={{0,1},{1,0},{2,3},{3,2},{4,5},{5,4},{6,7},{7,6},{8,9},{9,8},{10,11... | collective-permute-start | bytes 196616 | tf_op jit(solution)/shard_map/ppermute | solution.py:14
  38.5 4.3 %collective-permute-start.14 = (bf16[256,128]{1,0:T(8,128)(2,1)S(1)}, bf16[256,128]{1,0:T(8,128)(2,1)S(1)}, u32[]{:S(2)}, u32[]{:S(2)}) collective-permute-start(bf16[256,128]{1,0:T(8,128)(2,1)S(1)} %get-tuple-element.82.refs_0_), channel_id=1, source_target_pairs={{0,8},{8,0},{16,24},{24,16},{1,9},{9,1},{17,25},{25,17},{2,10},{10... | collective-permute-start | bytes 196616 | tf_op jit(solution)/shard_map/ppermute | solution.py:490
  (1 other events, 2.7 us)

commit v5 on v4

--- a/solution.py
+++ b/solution.py
@@ -139,6 +139,10 @@
 
 VMEM_LIMIT = 16 * 2**20
 COL_MICROS = 28
+FIRST_ORDER = (1, 2, 3)
+BACK_ORDER = (2, 1, 3)
+COL_APART = (2, 1)
+ROW_APART = (2, 1)
 
 
 def dot(left, right, left_dim=1, right_dim=0):
@@ -244,8 +248,8 @@
     return body
 
 
-def by_distance(bufs):
-    return [bufs[0], *bufs[:0:-1]]
+def by_distance(bufs, order):
+    return [bufs[0], *(bufs[1 + order.index(q)] for q in range(1, len(bufs)))]
 
 
 def one_col(bufs, at, deep):
@@ -262,7 +266,7 @@
     deep = 2 * rows
 
     def body(*refs):
-        bufs, rest = by_distance(refs[:chips]), refs[chips:]
+        bufs, rest = by_distance(refs[:chips], FIRST_ORDER), refs[chips:]
         up_ref, down_ref, perm_up_ref, perm_down_ref = rest[:4]
         outs, rest = rest[4 : 4 + chips], rest[4 + chips :]
         activated_ref, grad_pre_ref, take_up_ref, take_down_ref = rest
@@ -296,7 +300,7 @@
     deep = 2 * rows
 
     def body(*refs):
-        bufs = by_distance(refs[:chips])
+        bufs = by_distance(refs[:chips], FIRST_ORDER)
         activated_ref, grad_pre_ref, take_up_ref, take_down_ref, out_ref = refs[chips:]
         size = chips * deep
         for b in range(cols):
@@ -317,7 +321,8 @@
     narrow = jnp.bfloat16
 
     def body(*refs):
-        bufs, (tok_ref, x_ref, cot_ref, d_ref, order_ref) = refs[:chips], refs[chips : chips + 5]
+        bufs = by_distance(refs[:chips], BACK_ORDER)
+        tok_ref, x_ref, cot_ref, d_ref, order_ref = refs[chips : chips + 5]
         grads_ref, back_ref, grad_ref = refs[-3:]
         parity = lax.axis_index("loop") % 2
         pair_blocks = tok_ref.shape[0] // half
@@ -407,10 +412,8 @@
     return body
 
 
-def exchange(bufs, axis, far_first):
-    count = len(bufs)
-    order = range(count - 1, 0, -1) if far_first else range(1, count)
-    pairs = {q: [(s, s ^ (2 * q)) for s in range(2 * count)] for q in order}
+def exchange(bufs, axis, order):
+    pairs = {q: [(s, s ^ (2 * q)) for s in range(2 * len(bufs))] for q in order}
     return [bufs[0]] + [lax.ppermute(bufs[q], axis, pairs[q]) for q in order]
 
 
@@ -464,7 +467,7 @@
     *sent, down_taken = rows_out(
         buf, cotangent, other_d, down_rows, other_down, take, order, *sent
     )
-    cells = exchange(sent, "loop", True)
+    cells = exchange(sent, "loop", FIRST_ORDER)
     square = struct(cols * size, size)
     *sent, activated, grad_pre, take_up, take_down = call(
         columns(chips, rows, cols),
@@ -475,7 +478,7 @@
         perm_up.reshape(1, size),
         perm_down.reshape(1, size),
     )
-    back = exchange(sent, "loop", False)
+    back = exchange(sent, "loop", BACK_ORDER)
     (col_grads,) = call(
         column_grads(chips, rows, cols),
         [struct(2 * cols * size, size)],
@@ -500,7 +503,7 @@
         order_back,
         col_grads,
     )
-    sums_got = over_dp(sums, dps - 1)
+    sums_got = over_dp(sums, ROW_APART[0])
     partial = struct(feature_rows, toks, wide)
     both = struct(2 * feature_rows, toks)
     mixed, grad_tokens, branches, col_sum = call(
@@ -513,7 +516,7 @@
         cotangent,
         up_taken,
         col_grads,
-        over_dp(col_grads, dps - 1),
+        over_dp(col_grads, COL_APART[0]),
     )
     kept, leaving = call(add_halves, [taken, taken], sums, sums_got)
 
@@ -521,14 +524,14 @@
         pairs = [(s, s ^ (apart * loops + 1)) for s in range(dps * loops)]
         return lax.ppermute(value, ("dp", "loop"), pairs)
 
-    parts = (kept, over_dp(kept, 1), to_partner(leaving, 1), from_partner(leaving, "loop", 0))
+    parts = (kept, over_dp(kept, ROW_APART[1]), to_partner(leaving, ROW_APART[1]), from_partner(leaving, "loop", 0))
     scale = 1.0 / math.sqrt(dps * toks)
     token = struct(8, 128, wide)
     g_up_second, g_down_first, done = call(
         total_col_grads(scale),
         [struct(*square.shape, wide)] * 2 + [token],
         col_sum,
-        over_dp(col_sum, 1),
+        over_dp(col_sum, COL_APART[1]),
         to_hbm=2,
         micros=COL_MICROS,
     )

time: 43.9 us -> 42.4 us (0.966)
  waiting for transfers between devices: 14.3 us -> 13.3 us
  starting transfers between devices: 18.9 us -> 18.3 us
    ppermute x4, waiting for transfers between devices: 3.59 us -> 2.41 us  [over_dp(): return lax.ppermute(value, 'dp', [(s, s ^ apart) for s in range(dps)])]
    ppermute x4, starting transfers between devices: 8.68 us -> 8.21 us  [over_dp(): return lax.ppermute(value, 'dp', [(s, s ^ apart) for s in range(dps)])]
  transfers between devices with their start and end apart: 17 -> 17, of which waited for: 10 -> 10; matrix products, arithmetic and copies ran while one was open for 0% -> 0% of each run, Pallas kernels for 15% -> 16%
where the time goes in v5:
time: 42.4 us; the launch traced here: 42.2 us
  starting transfers between devices  18.3 us (43%)
  waiting for transfers between devices  13.3 us (31%)
  Pallas kernels  9.81 us (23%)
  between operations  0.75 us (2%)
    pallas_call x11, Pallas kernels, call(): pl.pallas_call(body, out_shape=outs, in_specs=[whole] * len(args), out_sp...  9.81 us
    ppermute x4, starting transfers between devices, over_dp(): return lax.ppermute(value, 'dp', [(s, s ^ apart) for s in range(dps)])  8.21 us
    ppermute x6, waiting for transfers between devices, exchange(): return [bufs[0]] + [lax.ppermute(bufs[q], axis, pairs[q]) for q in order]  8.08 us
    ppermute x6, starting transfers between devices, exchange(): return [bufs[0]] + [lax.ppermute(bufs[q], axis, pairs[q]) for q in order]  8.02 us
    ppermute x6, waiting for transfers between devices, from_partner(): return lax.ppermute(value, axis, pairs)  2.8 us
    ppermute x4, waiting for transfers between devices, over_dp(): return lax.ppermute(value, 'dp', [(s, s ^ apart) for s in range(dps)])  2.41 us
    ppermute x6, starting transfers between devices, from_partner(): return lax.ppermute(value, axis, pairs)  2.02 us
  transfers between devices with their start and end apart: 17, of which 10 were waited for; matrix products, arithmetic and copies ran while one was open for 0% of the time, Pallas kernels for 16%

profile of v5, /device:TPU:0, one launch (start us, length us, event | category | flops | bytes accessed | tf_op | source)
XLA Modules:
  0.0 42.2 jit_solution(4886486422869801077)
XLA Ops:
  2.9 1.2 %collective-permute-done.3.refs_1_.refs_5_ = bf16[1024,512]{1,0:T(8,128)(2,1)S(1)} collective-permute-done((bf16[1024,512]{1,0:T(8,128)(2,1)}, bf16[1024,512]{1,0:T(8,128)(2,1)S(1)}, u32[]{:S(2)}, u32[]{:S(2)}) %collective-permute-start.3) | collective-permute-done | bytes 1048608 | tf_op jit(solution)/shard_map/ppermute | solution.py:14
  4.2 0.8 %shard_map.128 = (bf16[64,512]{1,0:T(8,128)(2,1)S(1)}, bf16[64,512]{1,0:T(8,128)(2,1)S(1)}, bf16[64,512]{1,0:T(8,128)(2,1)S(1)}, bf16[64,512]{1,0:T(8,128)(2,1)S(1)}, bf16[256,128]{1,0:T(8,128)(2,1)S(1)}) custom-call(bf16[1024,512]{1,0:T(8,128)(2,1)S(1)} %copy-done, bf16[1024,512]{1,0:T(8,128)(2,1)S(1)} %collective-permute-done.3.refs_1_.refs_5_, ...), custom_call_target="tpu_custom_call" | custom-call | flops 10000000 | bytes 30000 | tf_op jit(solution)/shard_map/pallas_call | solution.py:156
  5.0 0.6 %collective-permute-done.2.refs_1_.refs_7_ = bf16[1024,512]{1,0:T(8,128)(2,1)S(1)} collective-permute-done((bf16[1024,512]{1,0:T(8,128)(2,1)}, bf16[1024,512]{1,0:T(8,128)(2,1)S(1)}, u32[]{:S(2)}, u32[]{:S(2)}) %collective-permute-start.2) | collective-permute-done | bytes 1048608 | tf_op jit(solution)/shard_map/ppermute | solution.py:14
  5.7 0.8 %shard_map.129 = (bf16[128,512]{1,0:T(8,128)(2,1)S(1)}, bf16[128,512]{1,0:T(8,128)(2,1)S(1)}, bf16[128,512]{1,0:T(8,128)(2,1)S(1)}, bf16[128,512]{1,0:T(8,128)(2,1)S(1)}, bf16[256,128]{1,0:T(8,128)(2,1)S(1)}) custom-call(bf16[1024,512]{1,0:T(8,128)(2,1)S(1)} %copy-done.1, bf16[1024,512]{1,0:T(8,128)(2,1)S(1)} %collective-permute-done.2.refs_1_.refs_7_, ...), custom_call_target="tpu_custom_call" | custom-call | flops 10000000 | bytes 30000 | tf_op jit(solution)/shard_map/pallas_call | solution.py:156
  6.5 2.9 %collective-permute-start.4 = (bf16[128,512]{1,0:T(8,128)(2,1)S(1)}, bf16[128,512]{1,0:T(8,128)(2,1)S(1)}, u32[]{:S(2)}, u32[]{:S(2)}) collective-permute-start(bf16[128,512]{1,0:T(8,128)(2,1)S(1)} %get-tuple-element.58), channel_id=1, source_target_pairs={{0,2},{1,3},{2,0},{3,1},{4,6},{5,7},{6,4},{7,5},{8,10},{9,11},{10,... | collective-permute-start | bytes 393224 | tf_op jit(solution)/shard_map/ppermute | solution.py:417
  9.4 1.5 %collective-permute-start.5 = (bf16[128,512]{1,0:T(8,128)(2,1)S(1)}, bf16[128,512]{1,0:T(8,128)(2,1)S(1)}, u32[]{:S(2)}, u32[]{:S(2)}) collective-permute-start(bf16[128,512]{1,0:T(8,128)(2,1)S(1)} %get-tuple-element.59), channel_id=1, source_target_pairs={{0,4},{1,5},{2,6},{3,7},{4,0},{5,1},{6,2},{7,3},{8,12},{9,13},{10,... | collective-permute-start | bytes 393224 | tf_op jit(solution)/shard_map/ppermute | solution.py:417
  11.0 2.4 %collective-permute-done.4.refs_1_ = bf16[128,512]{1,0:T(8,128)(2,1)S(1)} collective-permute-done((bf16[128,512]{1,0:T(8,128)(2,1)S(1)}, bf16[128,512]{1,0:T(8,128)(2,1)S(1)}, u32[]{:S(2)}, u32[]{:S(2)}) %collective-permute-start.4) | collective-permute-done | bytes 131104 | tf_op jit(solution)/shard_map/ppermute | solution.py:417
  13.3 4.2 %collective-permute-done.5.refs_2_ = bf16[128,512]{1,0:T(8,128)(2,1)S(1)} collective-permute-done((bf16[128,512]{1,0:T(8,128)(2,1)S(1)}, bf16[128,512]{1,0:T(8,128)(2,1)S(1)}, u32[]{:S(2)}, u32[]{:S(2)}) %collective-permute-start.5) | collective-permute-done | bytes 131104 | tf_op jit(solution)/shard_map/ppermute | solution.py:417
  17.5 1.3 %shard_map.130 = (bf16[128,512]{1,0:T(8,128)(2,1)S(1)}, bf16[128,512]{1,0:T(8,128)(2,1)S(1)}, bf16[128,512]{1,0:T(8,128)(2,1)S(1)}, bf16[128,512]{1,0:T(8,128)(2...) custom-call(bf16[128,512]{1,0:T(8,128)(2,1)S(1)} %get-tuple-element., ...), custom_call_target="tpu_custom_call" | custom-call | flops 10000000 | bytes 30000 | tf_op jit(solution)/shard_map/pallas_call | solution.py:156
  18.9 1.6 %collective-permute-start.7 = (bf16[128,512]{1,0:T(8,128)(2,1)S(1)}, bf16[128,512]{1,0:T(8,128)(2,1)S(1)}, u32[]{:S(2)}, u32[]{:S(2)}) collective-permute-start(bf16[128,512]{1,0:T(8,128)(2,1)S(1)} %get-tuple-element.62), channel_id=1, source_target_pairs={{0,4},{1,5},{2,6},{3,7},{4,0},{5,1},{6,2},{7,3},{8,12},{9,13},{10,... | collective-permute-start | bytes 393224 | tf_op jit(solution)/shard_map/ppermute | solution.py:417
  21.0 1.4 %collective-permute-start.9 = (bf16[128,512]{1,0:T(8,128)(2,1)S(1)}, bf16[128,512]{1,0:T(8,128)(2,1)S(1)}, u32[]{:S(2)}, u32[]{:S(2)}) collective-permute-start(bf16[128,512]{1,0:T(8,128)(2,1)S(1)} %get-tuple-element.64), channel_id=1, source_target_pairs={{0,6},{1,7},{2,4},{3,5},{4,2},{5,3},{6,0},{7,1},{8,14},{9,15},{10,... | collective-permute-start | bytes 393224 | tf_op jit(solution)/shard_map/ppermute | solution.py:417
  23.0 2.7 %collective-permute-start.10 = (bf16[512,128]{1,0:T(8,128)(2,1)S(1)}, bf16[512,128]{1,0:T(8,128)(2,1)S(1)}, u32[]{:S(2)}, u32[]{:S(2)}) collective-permute-start(bf16[512,128]{1,0:T(8,128)(2,1)S(1)} %shard_map.131.refs_9_.refs_6_), channel_id=1, source_target_pairs={{0,16},{8,24},{16,0},{24,8},{1,17},{9,25},{17,1},{25,9},{2,18},{10... | collective-permute-start | bytes 393224 | tf_op jit(solution)/shard_map/ppermute | solution.py:493
  26.0 1.3 %collective-permute-done.9.refs_3_ = bf16[128,512]{1,0:T(8,128)(2,1)S(1)} collective-permute-done((bf16[128,512]{1,0:T(8,128)(2,1)S(1)}, bf16[128,512]{1,0:T(8,128)(2,1)S(1)}, u32[]{:S(2)}, u32[]{:S(2)}) %collective-permute-start.9) | collective-permute-done | bytes 131104 | tf_op jit(solution)/shard_map/ppermute | solution.py:417
  27.2 1.5 %shard_map.132 = (bf16[512,128]{1,0:T(8,128)(2,1)S(1)}, bf16[256,512]{1,0:T(8,128)(2,1)S(1)}, bf16[256,512]{1,0:T(8,128)(2,1)S(1)}) custom-call(bf16[128,512]{1,0:T(8,128)(2,1)S(1)} %get-tuple-element.61.refs_0_, bf16[128,512]{1,0:T(8,128)(2,1)S(1)} %collective-permute-done.7.refs_1_, bf16[128,512]{1,0:T(8,128)(2,1)S(1)} %collective-permute-done.8.refs_2_, ...), custom_call_target="tpu_custom_call" | custom-call | flops 10000000 | bytes 30000 | tf_op jit(solution)/shard_map/pallas_call | solution.py:156
  28.8 2.6 %collective-permute-start.13 = (bf16[512,128]{1,0:T(8,128)(2,1)S(1)}, bf16[512,128]{1,0:T(8,128)(2,1)S(1)}, u32[]{:S(2)}, u32[]{:S(2)}) collective-permute-start(bf16[512,128]{1,0:T(8,128)(2,1)S(1)} %get-tuple-element.81.left_ref), channel_id=1, source_target_pairs={{0,16},{8,24},{16,0},{24,8},{1,17},{9,25},{17,1},{25,9},{2,18},{10... | collective-permute-start | bytes 393224 | tf_op jit(solution)/shard_map/ppermute | solution.py:493
  31.4 1.3 %shard_map.133 = (f32[1024,512]{1,0:T(8,128)S(1)}, f32[1024,512]{1,0:T(8,128)S(1)}, bf16[2048,512]{1,0:T(8,128)(2,1)S(1)}, bf16[512,128]{1,0:T(8,128)(2,1)S(1)}) custom-call(bf16[256,512]{1,0:T(8,128)(2,1)S(1)} %get-tuple-element.70.refs_0_, bf16[1024,512]{1,0:T(8,128)(2,1)S(1)} %copy-done, bf16[256,128]{1,0:T(8,128)(2,1)S(1)} %get-tuple-element.71.refs_2_, ...), custom_call_target="tpu_custom_call" | custom-call | flops 10000000 | bytes 30000 | tf_op jit(solution)/shard_map/pallas_call | solution.py:156
  32.7 1.6 %collective-permute-start.12 = (bf16[512,128]{1,0:T(8,128)(2,1)S(1)}, bf16[512,128]{1,0:T(8,128)(2,1)S(1)}, u32[]{:S(2)}, u32[]{:S(2)}) collective-permute-start(bf16[512,128]{1,0:T(8,128)(2,1)S(1)} %get-tuple-element.77.sum_ref), channel_id=1, source_target_pairs={{0,8},{8,0},{16,24},{24,16},{1,9},{9,1},{17,25},{25,17},{2,10},{10... | collective-permute-start | bytes 393224 | tf_op jit(solution)/shard_map/ppermute | solution.py:493
  34.3 1.8 %collective-permute-done.13.right_ref = bf16[512,128]{1,0:T(8,128)(2,1)S(1)} collective-permute-done((bf16[512,128]{1,0:T(8,128)(2,1)S(1)}, bf16[512,128]{1,0:T(8,128)(2,1)S(1)}, u32[]{:S(2)}, u32[]{:S(2)}) %collective-permute-start.13) | collective-permute-done | bytes 131104 | tf_op jit(solution)/shard_map/ppermute | solution.py:493
  36.2 0.8 %collective-permute-start.16 = (bf16[256,128]{1,0:T(8,128)(2,1)S(1)}, bf16[256,128]{1,0:T(8,128)(2,1)S(1)}, u32[]{:S(2)}, u32[]{:S(2)}) collective-permute-start(bf16[256,128]{1,0:T(8,128)(2,1)S(1)} %get-tuple-element.83), channel_id=1, source_target_pairs={{0,1},{1,0},{2,3},{3,2},{4,5},{5,4},{6,7},{7,6},{8,9},{9,8},{10,11... | collective-permute-start | bytes 196616 | tf_op jit(solution)/shard_map/ppermute | solution.py:14
  37.0 1.3 %collective-permute-start.14 = (bf16[256,128]{1,0:T(8,128)(2,1)S(1)}, bf16[256,128]{1,0:T(8,128)(2,1)S(1)}, u32[]{:S(2)}, u32[]{:S(2)}) collective-permute-start(bf16[256,128]{1,0:T(8,128)(2,1)S(1)} %get-tuple-element.82.refs_0_), channel_id=1, source_target_pairs={{0,8},{8,0},{16,24},{24,16},{1,9},{9,1},{17,25},{25,17},{2,10},{10... | collective-permute-start | bytes 196616 | tf_op jit(solution)/shard_map/ppermute | solution.py:493
  38.3 0.7 %shard_map.134 = (f32[256,128]{1,0:T(8,128)}, f32[256,128]{1,0:T(8,128)}, f32[8,128]{1,0:T(8,128)S(1)}) custom-call(bf16[512,128]{1,0:T(8,128)(2,1)S(1)} %get-tuple-element.77.sum_ref, bf16[512,128]{1,0:T(8,128)(2,1)S(1)} %collective-permute-done.12.got_ref), custom_call_target="tpu_custom_call" | custom-call | flops 28000000000 | bytes 84000000 | tf_op jit(solution)/shard_map/pallas_call | solution.py:156
  39.0 1.6 %shard_map.135 = (bf16[1024,512]{1,0:T(8,128)(2,1)}, bf16[1024,512]{1,0:T(8,128)(2,1)}, f32[8,128]{1,0:T(8,128)S(1)}) custom-call(f32[1024,512]{1,0:T(8,128)S(1)} %get-tuple-element.74.mixed_ref, f32[1024,512]{1,0:T(8,128)S(1)} %get-tuple-element.75.grad_ref, bf16[2048,512]{1,0:T(8,128)(2,1)S(1)} %collective-permute-done.11.got_ref, ...), custom_call_target="tpu_custom_call" | custom-call | flops 10000000 | bytes 30000 | tf_op jit(solution)/shard_map/pallas_call | solution.py:156
  40.6 0.7 %collective-permute-done.14.refs_1_ = bf16[256,128]{1,0:T(8,128)(2,1)S(1)} collective-permute-done((bf16[256,128]{1,0:T(8,128)(2,1)S(1)}, bf16[256,128]{1,0:T(8,128)(2,1)S(1)}, u32[]{:S(2)}, u32[]{:S(2)}) %collective-permute-start.14) | collective-permute-done | bytes 65568 | tf_op jit(solution)/shard_map/ppermute | solution.py:493
  41.3 0.9 %shard_map.137 = (f32[256,128]{1,0:T(8,128)}, f32[256,128]{1,0:T(8,128)}) custom-call(bf16[256,128]{1,0:T(8,128)(2,1)S(1)} %get-tuple-element.82.refs_0_, bf16[256,128]{1,0:T(8,128)(2,1)S(1)} %collective-permute-done.14.refs_1_, bf16[256,128]{1,0:T(8,128)(2,1)S(1)} %collective-permute-done.15.refs_2_, bf16[256,128]{1,0:T(8,128)(2,1)S(1)} %collective-permute-done.16.refs_3_, ...), custom_call_target="tpu_custom_call" | custom-call | flops 10000000 | bytes 30000 | tf_op jit(solution)/shard_map/pallas_call | solution.py:156
  (37 shorter events, 3.9 us)
Async XLA Ops:
  0.6 1.6 %collective-permute-start = (bf16[256,128]{1,0:T(8,128)(2,1)}, bf16[256,128]{1,0:T(8,128)(2,1)S(1)}, u32[]{:S(2)}, u32[]{:S(2)}) collective-permute-start(bf16[256,128]{1,0:T(8,128)(2,1)} %bitcast.10), channel_id=1, source_target_pairs={{0,1},{1,0},{2,3},{3,2},{4,5},{5,4},{6,7},{7,6},{8,9},{9,8},{10,11... | collective-permute-start | bytes 196616 | tf_op jit(solution)/shard_map/ppermute | solution.py:14
  1.1 3.0 %copy-start = (bf16[1024,512]{1,0:T(8,128)(2,1)S(1)}, bf16[1024,512]{1,0:T(8,128)(2,1)}, u32[]{:S(2)}) copy-start(bf16[1024,512]{1,0:T(8,128)(2,1)} %refs_1_.1) | copy-start | bytes 3145732
  1.2 3.0 %copy-start.2 = (bf16[16,16,128]{2,1,0:T(8,128)(2,1)S(1)}, bf16[16,16,128]{2,1,0:T(8,128)(2,1)}, u32[]{:S(2)}) copy-start(bf16[16,16,128]{2,1,0:T(8,128)(2,1)} %param.10) | copy-start | bytes 196612
  1.2 1.5 %collective-permute-start.1 = (bf16[256,128]{1,0:T(8,128)(2,1)}, bf16[256,128]{1,0:T(8,128)(2,1)S(1)}, u32[]{:S(2)}, u32[]{:S(2)}) collective-permute-start(bf16[256,128]{1,0:T(8,128)(2,1)} %bitcast.14), channel_id=1, source_target_pairs={{0,1},{1,0},{2,3},{3,2},{4,5},{5,4},{6,7},{7,6},{8,9},{9,8},{10,11... | collective-permute-start | bytes 196616 | tf_op jit(solution)/shard_map/ppermute | solution.py:14
  1.2 2.9 %collective-permute-start.3 = (bf16[1024,512]{1,0:T(8,128)(2,1)}, bf16[1024,512]{1,0:T(8,128)(2,1)S(1)}, u32[]{:S(2)}, u32[]{:S(2)}) collective-permute-start(bf16[1024,512]{1,0:T(8,128)(2,1)} %refs_1_.1), channel_id=1, source_target_pairs={{0,1},{1,0},{2,3},{3,2},{4,5},{5,4},{6,7},{7,6},{8,9},{9,8},{10,11... | collective-permute-start | bytes 3145736 | tf_op jit(solution)/shard_map/ppermute | solution.py:14
  2.6 3.0 %collective-permute-start.2 = (bf16[1024,512]{1,0:T(8,128)(2,1)}, bf16[1024,512]{1,0:T(8,128)(2,1)S(1)}, u32[]{:S(2)}, u32[]{:S(2)}) collective-permute-start(bf16[1024,512]{1,0:T(8,128)(2,1)} %refs_4_.3), channel_id=1, source_target_pairs={{0,1},{1,0},{2,3},{3,2},{4,5},{5,4},{6,7},{7,6},{8,9},{9,8},{10,11... | collective-permute-start | bytes 3145736 | tf_op jit(solution)/shard_map/ppermute | solution.py:14
  2.9 2.7 %copy-start.1 = (bf16[1024,512]{1,0:T(8,128)(2,1)S(1)}, bf16[1024,512]{1,0:T(8,128)(2,1)}, u32[]{:S(2)}) copy-start(bf16[1024,512]{1,0:T(8,128)(2,1)} %refs_4_.3) | copy-start | bytes 3145732
  4.2 13.3 %copy-start.3 = (bf16[2,128,128]{2,1,0:T(8,128)(2,1)S(1)}, bf16[2,128,128]{2,1,0:T(8,128)(2,1)}, u32[]{:S(2)}) copy-start(bf16[2,128,128]{2,1,0:T(8,128)(2,1)} %param.11) | copy-start | bytes 196612
  4.2 13.3 %copy-start.4 = (bf16[2,128,128]{2,1,0:T(8,128)(2,1)S(1)}, bf16[2,128,128]{2,1,0:T(8,128)(2,1)}, u32[]{:S(2)}) copy-start(bf16[2,128,128]{2,1,0:T(8,128)(2,1)} %param.12) | copy-start | bytes 196612
  4.2 13.3 %copy-start.6 = (s32[128]{0:T(128)S(1)}, s32[128]{0:T(128)}, u32[]{:S(2)}) copy-start(s32[128]{0:T(128)} %param.14) | copy-start | bytes 1540
  4.2 13.3 %copy-start.7 = (s32[128]{0:T(128)S(1)}, s32[128]{0:T(128)}, u32[]{:S(2)}) copy-start(s32[128]{0:T(128)} %param.15) | copy-start | bytes 1540
  6.5 6.8 %collective-permute-start.4 = (bf16[128,512]{1,0:T(8,128)(2,1)S(1)}, bf16[128,512]{1,0:T(8,128)(2,1)S(1)}, u32[]{:S(2)}, u32[]{:S(2)}) collective-permute-start(bf16[128,512]{1,0:T(8,128)(2,1)S(1)} %get-tuple-element.58), channel_id=1, source_target_pairs={{0,2},{1,3},{2,0},{3,1},{4,6},{5,7},{6,4},{7,5},{8,10},{9,11},{10,... | collective-permute-start | bytes 393224 | tf_op jit(solution)/shard_map/ppermute | solution.py:417
  9.4 8.1 %collective-permute-start.5 = (bf16[128,512]{1,0:T(8,128)(2,1)S(1)}, bf16[128,512]{1,0:T(8,128)(2,1)S(1)}, u32[]{:S(2)}, u32[]{:S(2)}) collective-permute-start(bf16[128,512]{1,0:T(8,128)(2,1)S(1)} %get-tuple-element.59), channel_id=1, source_target_pairs={{0,4},{1,5},{2,6},{3,7},{4,0},{5,1},{6,2},{7,3},{8,12},{9,13},{10,... | collective-permute-start | bytes 393224 | tf_op jit(solution)/shard_map/ppermute | solution.py:417
  10.9 6.5 %collective-permute-start.6 = (bf16[128,512]{1,0:T(8,128)(2,1)S(1)}, bf16[128,512]{1,0:T(8,128)(2,1)S(1)}, u32[]{:S(2)}, u32[]{:S(2)}) collective-permute-start(bf16[128,512]{1,0:T(8,128)(2,1)S(1)} %get-tuple-element.60), channel_id=1, source_target_pairs={{0,6},{1,7},{2,4},{3,5},{4,2},{5,3},{6,0},{7,1},{8,14},{9,15},{10,... | collective-permute-start | bytes 393224 | tf_op jit(solution)/shard_map/ppermute | solution.py:417
  18.9 6.8 %collective-permute-start.7 = (bf16[128,512]{1,0:T(8,128)(2,1)S(1)}, bf16[128,512]{1,0:T(8,128)(2,1)S(1)}, u32[]{:S(2)}, u32[]{:S(2)}) collective-permute-start(bf16[128,512]{1,0:T(8,128)(2,1)S(1)} %get-tuple-element.62), channel_id=1, source_target_pairs={{0,4},{1,5},{2,6},{3,7},{4,0},{5,1},{6,2},{7,3},{8,12},{9,13},{10,... | collective-permute-start | bytes 393224 | tf_op jit(solution)/shard_map/ppermute | solution.py:417
  20.4 5.5 %collective-permute-start.8 = (bf16[128,512]{1,0:T(8,128)(2,1)S(1)}, bf16[128,512]{1,0:T(8,128)(2,1)S(1)}, u32[]{:S(2)}, u32[]{:S(2)}) collective-permute-start(bf16[128,512]{1,0:T(8,128)(2,1)S(1)} %get-tuple-element.63), channel_id=1, source_target_pairs={{0,2},{1,3},{2,0},{3,1},{4,6},{5,7},{6,4},{7,5},{8,10},{9,11},{10,... | collective-permute-start | bytes 393224 | tf_op jit(solution)/shard_map/ppermute | solution.py:417
  21.0 6.2 %collective-permute-start.9 = (bf16[128,512]{1,0:T(8,128)(2,1)S(1)}, bf16[128,512]{1,0:T(8,128)(2,1)S(1)}, u32[]{:S(2)}, u32[]{:S(2)}) collective-permute-start(bf16[128,512]{1,0:T(8,128)(2,1)S(1)} %get-tuple-element.64), channel_id=1, source_target_pairs={{0,6},{1,7},{2,4},{3,5},{4,2},{5,3},{6,0},{7,1},{8,14},{9,15},{10,... | collective-permute-start | bytes 393224 | tf_op jit(solution)/shard_map/ppermute | solution.py:417
  23.0 8.4 %collective-permute-start.10 = (bf16[512,128]{1,0:T(8,128)(2,1)S(1)}, bf16[512,128]{1,0:T(8,128)(2,1)S(1)}, u32[]{:S(2)}, u32[]{:S(2)}) collective-permute-start(bf16[512,128]{1,0:T(8,128)(2,1)S(1)} %shard_map.131.refs_9_.refs_6_), channel_id=1, source_target_pairs={{0,16},{8,24},{16,0},{24,8},{1,17},{9,25},{17,1},{25,9},{2,18},{10... | collective-permute-start | bytes 393224 | tf_op jit(solution)/shard_map/ppermute | solution.py:493
  28.8 7.3 %collective-permute-start.13 = (bf16[512,128]{1,0:T(8,128)(2,1)S(1)}, bf16[512,128]{1,0:T(8,128)(2,1)S(1)}, u32[]{:S(2)}, u32[]{:S(2)}) collective-permute-start(bf16[512,128]{1,0:T(8,128)(2,1)S(1)} %get-tuple-element.81.left_ref), channel_id=1, source_target_pairs={{0,16},{8,24},{16,0},{24,8},{1,17},{9,25},{17,1},{25,9},{2,18},{10... | collective-permute-start | bytes 393224 | tf_op jit(solution)/shard_map/ppermute | solution.py:493
  32.7 5.6 %collective-permute-start.12 = (bf16[512,128]{1,0:T(8,128)(2,1)S(1)}, bf16[512,128]{1,0:T(8,128)(2,1)S(1)}, u32[]{:S(2)}, u32[]{:S(2)}) collective-permute-start(bf16[512,128]{1,0:T(8,128)(2,1)S(1)} %get-tuple-element.77.sum_ref), channel_id=1, source_target_pairs={{0,8},{8,0},{16,24},{24,16},{1,9},{9,1},{17,25},{25,17},{2,10},{10... | collective-permute-start | bytes 393224 | tf_op jit(solution)/shard_map/ppermute | solution.py:493
  34.3 4.7 %collective-permute-start.11 = (bf16[2048,512]{1,0:T(8,128)(2,1)S(1)}, bf16[2048,512]{1,0:T(8,128)(2,1)S(1)}, u32[]{:S(2)}, u32[]{:S(2)}) collective-permute-start(bf16[2048,512]{1,0:T(8,128)(2,1)S(1)} %get-tuple-element.76), channel_id=1, source_target_pairs={{0,1},{1,0},{2,3},{3,2},{4,5},{5,4},{6,7},{7,6},{8,9},{9,8},{10,11... | collective-permute-start | bytes 6291464 | tf_op jit(solution)/shard_map/ppermute | solution.py:14
  36.1 5.2 %collective-permute-start.15 = (bf16[256,128]{1,0:T(8,128)(2,1)S(1)}, bf16[256,128]{1,0:T(8,128)(2,1)S(1)}, u32[]{:S(2)}, u32[]{:S(2)}) collective-permute-start(bf16[256,128]{1,0:T(8,128)(2,1)S(1)} %get-tuple-element.83), channel_id=1, source_target_pairs={{0,9},{1,8},{2,11},{3,10},{4,13},{5,12},{6,15},{7,14},{8,1},{9,0},... | collective-permute-start | bytes 196616 | tf_op jit(solution)/shard_map/ppermute | solution.py:525
  36.2 5.1 %collective-permute-start.16 = (bf16[256,128]{1,0:T(8,128)(2,1)S(1)}, bf16[256,128]{1,0:T(8,128)(2,1)S(1)}, u32[]{:S(2)}, u32[]{:S(2)}) collective-permute-start(bf16[256,128]{1,0:T(8,128)(2,1)S(1)} %get-tuple-element.83), channel_id=1, source_target_pairs={{0,1},{1,0},{2,3},{3,2},{4,5},{5,4},{6,7},{7,6},{8,9},{9,8},{10,11... | collective-permute-start | bytes 196616 | tf_op jit(solution)/shard_map/ppermute | solution.py:14
  37.0 4.3 %collective-permute-start.14 = (bf16[256,128]{1,0:T(8,128)(2,1)S(1)}, bf16[256,128]{1,0:T(8,128)(2,1)S(1)}, u32[]{:S(2)}, u32[]{:S(2)}) collective-permute-start(bf16[256,128]{1,0:T(8,128)(2,1)S(1)} %get-tuple-element.82.refs_0_), channel_id=1, source_target_pairs={{0,8},{8,0},{16,24},{24,16},{1,9},{9,1},{17,25},{25,17},{2,10},{10... | collective-permute-start | bytes 196616 | tf_op jit(solution)/shard_map/ppermute | solution.py:493
  (1 other events, 2.7 us)

commit v6 on v5

--- a/solution.py
+++ b/solution.py
@@ -223,27 +223,44 @@
     return body
 
 
-def first_rows(chips, rows, cols, half):
-    narrow = jnp.bfloat16
-
+def take_weights(take_ref, weight_refs, parity, out_ref):
+    taken = [own_first(dot(take_ref[...], ref[...], 0, 0), parity) for ref in weight_refs]
+    out_ref[...] = jnp.concatenate(taken, 0).astype(out_ref.dtype)
+
+
+def send_rows(own_ref, other_ref, taken_ref, order_ref, grid_ref, outs, at, half, parity):
+    pair_blocks = own_ref.shape[0] // half
+    high = taken_ref.shape[0] // pair_blocks
+    for place, block in enumerate(pair_blocks_of(parity, pair_blocks)):
+        part = slice(place * high, (place + 1) * high)
+        features = block_rows(own_ref, other_ref, block * half, half)
+        grid_ref[part, :] = dot(taken_ref[part, :], features).astype(grid_ref.dtype)
+    sent = dot(order_ref[...], grid_ref[...]).astype(grid_ref.dtype)
+    unit = sent.shape[0] // len(outs)
+    for q, out in enumerate(outs):
+        out[at * unit : (at + 1) * unit, :] = sent[q * unit : (q + 1) * unit]
+
+
+def token_rows(chips, half):
     def body(*refs):
-        (own_ref, other_ref, *weights, take_ref, order_ref) = refs[:6]
-        earlier, outs, (taken_ref, grid_ref) = refs[6 : -chips - 2], refs[-chips - 2 : -2], refs[-2:]
+        own_ref, other_ref, *weights, take_ref, order_ref = refs[:8]
+        outs, (up_ref, down_ref, grid_ref) = refs[8 : 8 + chips], refs[8 + chips :]
         parity = lax.axis_index("loop") % 2
-        pair_blocks = own_ref.shape[0] // half
-        taken = [own_first(dot(take_ref[...], ref[...], 0, 0), parity) for ref in weights]
-        taken_ref[...] = jnp.concatenate(taken, 0).astype(narrow)
-        high = taken_ref.shape[0] // pair_blocks
-        for at, block in enumerate(pair_blocks_of(parity, pair_blocks)):
-            part = slice(at * high, (at + 1) * high)
-            features = block_rows(own_ref, other_ref, block * half, half)
-            grid_ref[part, :] = dot(taken_ref[part, :], features).astype(narrow)
-        sent = dot(order_ref[...], grid_ref[...]).astype(narrow)
-        unit = 2 * rows * cols
-        for q, out in enumerate(outs):
-            if earlier:
-                out[:unit, :] = earlier[q][...]
-            out[out.shape[0] - unit :, :] = sent[q * unit : (q + 1) * unit]
+        take_weights(take_ref, weights[:2], parity, up_ref)
+        send_rows(own_ref, other_ref, up_ref, order_ref, grid_ref, outs, 0, half, parity)
+        take_weights(take_ref, weights[2:], parity, down_ref)
+
+    return body
+
+
+def cotangent_rows(chips, half):
+    def body(*refs):
+        own_ref, other_ref, down_ref, order_ref = refs[:4]
+        earlier, outs, grid_ref = refs[4 : 4 + chips], refs[4 + chips : -1], refs[-1]
+        for out, ref in zip(outs, earlier, strict=True):
+            out[: ref.shape[0], :] = ref[...]
+        parity = lax.axis_index("loop") % 2
+        send_rows(own_ref, other_ref, down_ref, order_ref, grid_ref, outs, 1, half, parity)
 
     return body
 
@@ -261,17 +278,13 @@
         out[at * deep : (at + 1) * deep, :] = value[q * deep : (q + 1) * deep]
 
 
-def columns(chips, rows, cols):
+def column_weights(rows, cols):
     narrow = jnp.bfloat16
-    deep = 2 * rows
-
-    def body(*refs):
-        bufs, rest = by_distance(refs[:chips], FIRST_ORDER), refs[chips:]
-        up_ref, down_ref, perm_up_ref, perm_down_ref = rest[:4]
-        outs, rest = rest[4 : 4 + chips], rest[4 + chips :]
-        activated_ref, grad_pre_ref, take_up_ref, take_down_ref = rest
+
+    def body(up_ref, down_ref, perm_up_ref, perm_down_ref, *outs):
+        up_out, down_out, take_up_ref, take_down_ref = outs
         me = lax.axis_index("loop")
-        size = chips * deep
+        size = take_up_ref.shape[0]
         lead = lax.broadcasted_iota(jnp.int32, (size, size), 0)
         lane = lax.broadcasted_iota(jnp.int32, (size, size), 1)
         row = ((lead // rows) ^ me) * rows + lead % rows
@@ -281,8 +294,23 @@
         ).astype(narrow)
         for b in range(cols):
             span = slice(b * size, (b + 1) * size)
-            up = dot(up_ref[span, :], take_up_ref[...], 1, 1).astype(narrow)
-            down = dot(take_down_ref[...], down_ref[span, :]).astype(narrow)
+            up_out[span, :] = dot(up_ref[span, :], take_up_ref[...], 1, 1).astype(narrow)
+            down_out[span, :] = dot(take_down_ref[...], down_ref[span, :]).astype(narrow)
+
+    return body
+
+
+def columns(chips, rows, cols):
+    narrow = jnp.bfloat16
+    deep = 2 * rows
+
+    def body(*refs):
+        bufs, (up_ref, down_ref) = by_distance(refs[:chips], FIRST_ORDER), refs[chips : chips + 2]
+        outs, (activated_ref, grad_pre_ref) = refs[chips + 2 : -2], refs[-2:]
+        size = chips * deep
+        for b in range(cols):
+            span = slice(b * size, (b + 1) * size)
+            up, down = up_ref[span, :], down_ref[span, :]
             gelu_val, slope = gelu_parts(dot(up, one_col(bufs, b, deep)))
             activated = gelu_val.astype(narrow)
             activated_ref[span, :] = activated
@@ -379,17 +407,18 @@
     out_ref[...] = total.astype(out_ref.dtype)
 
 
-def add_halves(left_ref, right_ref, kept_ref, leave_ref):
+def add_halves(left_ref, right_ref, kept_ref, *leave_refs):
     size = kept_ref.shape[0]
-    for at, out in enumerate((kept_ref, leave_ref)):
+    for at, outs in enumerate(((kept_ref, leave_refs[0]), leave_refs[1:])):
         span = slice(at * size, (at + 1) * size)
         total = left_ref[span, :].astype(jnp.float32) + right_ref[span, :].astype(jnp.float32)
-        out[...] = total.astype(out.dtype)
+        for out in outs:
+            out[...] = total.astype(out.dtype)
 
 
 def total_grads(scale):
     def body(*refs):
-        parts, place_ref, outs = refs[:4], refs[4], refs[-2:]
+        parts, place_ref, outs = [refs[at] for at in (0, 2, 1, 3)], refs[4], refs[-2:]
         size = parts[0].shape[0] // 2
         near, far = place_ref[:, :size], place_ref[:, size:]
         place = jnp.concatenate([near, near, far, far], 1)
@@ -455,28 +484,46 @@
     leaving, other_up, other_down = lax.optimization_barrier((cotangent, other_up, other_down))
     other_d = from_partner(leaving, "loop", 0)
 
-    def rows_out(out, *args):
-        return call(
-            first_rows(chips, rows, cols, half),
-            [out] * chips + [taken],
-            *args,
-            scratch=[pltpu.VMEM(grid.shape, narrow)],
-        )
-
-    *sent, up_taken = rows_out(half_buf, tokens, other_x, up_rows, other_up, take, order)
-    *sent, down_taken = rows_out(
-        buf, cotangent, other_d, down_rows, other_down, take, order, *sent
+    *sent, up_taken, down_taken = call(
+        token_rows(chips, half),
+        [half_buf] * chips + [taken] * 2,
+        tokens,
+        other_x,
+        up_rows,
+        other_up,
+        down_rows,
+        other_down,
+        take,
+        order,
+        scratch=[pltpu.VMEM(grid.shape, narrow)],
+    )
+    sent = call(
+        cotangent_rows(chips, half),
+        [buf] * chips,
+        cotangent,
+        other_d,
+        down_taken,
+        order,
+        *sent,
+        scratch=[pltpu.VMEM(grid.shape, narrow)],
     )
     cells = exchange(sent, "loop", FIRST_ORDER)
     square = struct(cols * size, size)
-    *sent, activated, grad_pre, take_up, take_down = call(
-        columns(chips, rows, cols),
-        [buf] * chips + [grid] * 2 + [struct(size, size)] * 2,
-        *cells,
+    up_cols, down_cols, take_up, take_down = call(
+        column_weights(rows, cols),
+        [square] * 2 + [struct(size, size)] * 2,
         up_second.reshape(square.shape),
         down_first.reshape(square.shape),
         perm_up.reshape(1, size),
         perm_down.reshape(1, size),
+        micros=2,
+    )
+    *sent, activated, grad_pre = call(
+        columns(chips, rows, cols),
+        [buf] * chips + [grid] * 2,
+        *cells,
+        up_cols,
+        down_cols,
     )
     back = exchange(sent, "loop", BACK_ORDER)
     (col_grads,) = call(
@@ -518,13 +565,17 @@
         col_grads,
         over_dp(col_grads, COL_APART[0]),
     )
-    kept, leaving = call(add_halves, [taken, taken], sums, sums_got)
+    kept, to_next, to_other, to_core = call(add_halves, [taken] * 4, sums, sums_got)
 
     def to_partner(value, apart):
         pairs = [(s, s ^ (apart * loops + 1)) for s in range(dps * loops)]
         return lax.ppermute(value, ("dp", "loop"), pairs)
 
-    parts = (kept, over_dp(kept, ROW_APART[1]), to_partner(leaving, ROW_APART[1]), from_partner(leaving, "loop", 0))
+    got = {}
+    got['c'] = to_partner(to_other, ROW_APART[1])
+    got['z'] = over_dp(to_next, ROW_APART[1])
+    got['p'] = from_partner(to_core, "loop", 0)
+    parts = (kept, got['c'], got['z'], got['p'])
     scale = 1.0 / math.sqrt(dps * toks)
     token = struct(8, 128, wide)
     g_up_second, g_down_first, done = call(

time: 42.4 us -> 41.1 us (0.969)
  waiting for transfers between devices: 13.3 us -> 12.4 us
    ppermute x6, starting transfers between devices: 2.02 us -> 1.23 us  [from_partner(): return lax.ppermute(value, axis, pairs)]
    ppermute x4, starting transfers between devices: 8.21 us -> 8.86 us  [over_dp(): return lax.ppermute(value, 'dp', [(s, s ^ apart) for s in range(dps)])]
    ppermute x4, waiting for transfers between devices: 2.41 us -> 1.87 us  [over_dp(): return lax.ppermute(value, 'dp', [(s, s ^ apart) for s in range(dps)])]
    pallas_call x11 -> x12, Pallas kernels: 9.81 us -> 9.68 us  [call(): pl.pallas_call(body, out_shape=outs, in_specs=[whole] * len(args), out_sp...]
  transfers between devices with their start and end apart: 17 -> 17, of which waited for: 10 -> 12; matrix products, arithmetic and copies ran while one was open for 0% -> 0% of each run, Pallas kernels for 16% -> 17%
where the time goes in v6:
time: 41.1 us; the launch traced here: 41 us
  starting transfers between devices  18.2 us (44%)
  waiting for transfers between devices  12.4 us (30%)
  Pallas kernels  9.68 us (24%)
  between operations  0.75 us (2%)
    pallas_call x12, Pallas kernels, call(): pl.pallas_call(body, out_shape=outs, in_specs=[whole] * len(args), out_sp...  9.68 us
    ppermute x4, starting transfers between devices, over_dp(): return lax.ppermute(value, 'dp', [(s, s ^ apart) for s in range(dps)])  8.86 us
    ppermute x6, starting transfers between devices, exchange(): return [bufs[0]] + [lax.ppermute(bufs[q], axis, pairs[q]) for q in order]  8.02 us
    ppermute x6, waiting for transfers between devices, exchange(): return [bufs[0]] + [lax.ppermute(bufs[q], axis, pairs[q]) for q in order]  7.74 us
    ppermute x6, waiting for transfers between devices, from_partner(): return lax.ppermute(value, axis, pairs)  2.74 us
    ppermute x4, waiting for transfers between devices, over_dp(): return lax.ppermute(value, 'dp', [(s, s ^ apart) for s in range(dps)])  1.87 us
    ppermute x6, starting transfers between devices, from_partner(): return lax.ppermute(value, axis, pairs)  1.23 us
  transfers between devices with their start and end apart: 17, of which 12 were waited for; matrix products, arithmetic and copies ran while one was open for 0% of the time, Pallas kernels for 17%

profile of v6, /device:TPU:0, one launch (start us, length us, event | category | flops | bytes accessed | tf_op | source)
XLA Modules:
  0.0 41.0 jit_solution(12230376381436311455)
XLA Ops:
  1.7 0.6 %collective-permute-done.refs_3_ = bf16[256,128]{1,0:T(8,128)(2,1)S(1)} collective-permute-done((bf16[256,128]{1,0:T(8,128)(2,1)}, bf16[256,128]{1,0:T(8,128)(2,1)S(1)}, u32[]{:S(2)}, u32[]{:S(2)}) %collective-permute-start) | collective-permute-done | bytes 65568 | tf_op jit(solution)/shard_map/ppermute | solution.py:14
  2.9 1.2 %collective-permute-done.3.refs_1_.refs_5_ = bf16[1024,512]{1,0:T(8,128)(2,1)S(1)} collective-permute-done((bf16[1024,512]{1,0:T(8,128)(2,1)}, bf16[1024,512]{1,0:T(8,128)(2,1)S(1)}, u32[]{:S(2)}, u32[]{:S(2)}) %collective-permute-start.3) | collective-permute-done | bytes 1048608 | tf_op jit(solution)/shard_map/ppermute | solution.py:14
  4.2 0.9 %shard_map.128 = (bf16[64,512]{1,0:T(8,128)(2,1)S(1)}, bf16[64,512]{1,0:T(8,128)(2,1)S(1)}, bf16[64,512]{1,0:T(8,128)(2,1)S(1)}, bf16[64,512]{1,0:T(8,128)(2,1)S...) custom-call(bf16[1024,512]{1,0:T(8,128)(2,1)S(1)} %copy-done.1, ...), custom_call_target="tpu_custom_call" | custom-call | flops 10000000 | bytes 30000 | tf_op jit(solution)/shard_map/pallas_call | solution.py:156
  5.7 0.6 %shard_map.129 = (bf16[128,512]{1,0:T(8,128)(2,1)S(1)}, bf16[128,512]{1,0:T(8,128)(2,1)S(1)}, bf16[128,512]{1,0:T(8,128)(2,1)S(1)}, bf16[128,512]{1,0:T(8,128)(2,1)S(1)}) custom-call(bf16[1024,512]{1,0:T(8,128)(2,1)S(1)} %copy-done, bf16[1024,512]{1,0:T(8,128)(2,1)S(1)} %collective-permute-done.2.refs_1_.refs_7_, ...), custom_call_target="tpu_custom_call" | custom-call | flops 10000000 | bytes 30000 | tf_op jit(solution)/shard_map/pallas_call | solution.py:156
  6.3 2.9 %collective-permute-start.4 = (bf16[128,512]{1,0:T(8,128)(2,1)S(1)}, bf16[128,512]{1,0:T(8,128)(2,1)S(1)}, u32[]{:S(2)}, u32[]{:S(2)}) collective-permute-start(bf16[128,512]{1,0:T(8,128)(2,1)S(1)} %get-tuple-element.63), channel_id=1, source_target_pairs={{0,2},{1,3},{2,0},{3,1},{4,6},{5,7},{6,4},{7,5},{8,10},{9,11},{10,... | collective-permute-start | bytes 393224 | tf_op jit(solution)/shard_map/ppermute | solution.py:446
  9.2 1.5 %collective-permute-start.5 = (bf16[128,512]{1,0:T(8,128)(2,1)S(1)}, bf16[128,512]{1,0:T(8,128)(2,1)S(1)}, u32[]{:S(2)}, u32[]{:S(2)}) collective-permute-start(bf16[128,512]{1,0:T(8,128)(2,1)S(1)} %get-tuple-element.64), channel_id=1, source_target_pairs={{0,4},{1,5},{2,6},{3,7},{4,0},{5,1},{6,2},{7,3},{8,12},{9,13},{10,... | collective-permute-start | bytes 393224 | tf_op jit(solution)/shard_map/ppermute | solution.py:446
  11.1 2.0 %collective-permute-done.4.refs_1_ = bf16[128,512]{1,0:T(8,128)(2,1)S(1)} collective-permute-done((bf16[128,512]{1,0:T(8,128)(2,1)S(1)}, bf16[128,512]{1,0:T(8,128)(2,1)S(1)}, u32[]{:S(2)}, u32[]{:S(2)}) %collective-permute-start.4) | collective-permute-done | bytes 131104 | tf_op jit(solution)/shard_map/ppermute | solution.py:446
  13.1 4.2 %collective-permute-done.5.refs_2_ = bf16[128,512]{1,0:T(8,128)(2,1)S(1)} collective-permute-done((bf16[128,512]{1,0:T(8,128)(2,1)S(1)}, bf16[128,512]{1,0:T(8,128)(2,1)S(1)}, u32[]{:S(2)}, u32[]{:S(2)}) %collective-permute-start.5) | collective-permute-done | bytes 131104 | tf_op jit(solution)/shard_map/ppermute | solution.py:446
  17.2 1.0 %shard_map.131 = (bf16[128,512]{1,0:T(8,128)(2,1)S(1)}, bf16[128,512]{1,0:T(8,128)(2,1)S(1)}, bf16[128,512]{1,0:T(8,128)(2,1)S(1)}, bf16[128,512]{1,0:T(8,128)(2...) custom-call(bf16[128,512]{1,0:T(8,128)(2,1)S(1)} %get-tuple-element.62.refs_0_, ...), custom_call_target="tpu_custom_call" | custom-call | flops 10000000 | bytes 30000 | tf_op jit(solution)/shard_map/pallas_call | solution.py:156
  18.3 1.6 %collective-permute-start.7 = (bf16[128,512]{1,0:T(8,128)(2,1)S(1)}, bf16[128,512]{1,0:T(8,128)(2,1)S(1)}, u32[]{:S(2)}, u32[]{:S(2)}) collective-permute-start(bf16[128,512]{1,0:T(8,128)(2,1)S(1)} %get-tuple-element.69), channel_id=1, source_target_pairs={{0,4},{1,5},{2,6},{3,7},{4,0},{5,1},{6,2},{7,3},{8,12},{9,13},{10,... | collective-permute-start | bytes 393224 | tf_op jit(solution)/shard_map/ppermute | solution.py:446
  20.4 1.4 %collective-permute-start.9 = (bf16[128,512]{1,0:T(8,128)(2,1)S(1)}, bf16[128,512]{1,0:T(8,128)(2,1)S(1)}, u32[]{:S(2)}, u32[]{:S(2)}) collective-permute-start(bf16[128,512]{1,0:T(8,128)(2,1)S(1)} %get-tuple-element.71), channel_id=1, source_target_pairs={{0,6},{1,7},{2,4},{3,5},{4,2},{5,3},{6,0},{7,1},{8,14},{9,15},{10,... | collective-permute-start | bytes 393224 | tf_op jit(solution)/shard_map/ppermute | solution.py:446
  21.8 0.6 %shard_map.132.refs_9_.refs_6_ = bf16[512,128]{1,0:T(8,128)(2,1)S(1)} custom-call(bf16[128,512]{1,0:T(8,128)(2,1)S(1)} %get-tuple-element.62.refs_0_, bf16[128,512]{1,0:T(8,128)(2,1)S(1)} %collective-permute-done.4.refs_1_, bf16[128,512]{1,0:T(8,128)(2,1)S(1)} %collective-permute-done.5.refs_2_, bf16[128,512]{1,0:T(8,128)(2,1)S(1)} %collective-permute-done.6.refs_3_, ...), custom_call_target="tpu_custom_call" | custom-call | flops 10000000 | bytes 30000 | tf_op jit(solution)/shard_map/pallas_call | solution.py:156
  22.4 2.7 %collective-permute-start.10 = (bf16[512,128]{1,0:T(8,128)(2,1)S(1)}, bf16[512,128]{1,0:T(8,128)(2,1)S(1)}, u32[]{:S(2)}, u32[]{:S(2)}) collective-permute-start(bf16[512,128]{1,0:T(8,128)(2,1)S(1)} %shard_map.132.refs_9_.refs_6_), channel_id=1, source_target_pairs={{0,16},{8,24},{16,0},{24,8},{1,17},{9,25},{17,1},{25,9},{2,18},{10... | collective-permute-start | bytes 393224 | tf_op jit(solution)/shard_map/ppermute | solution.py:540
  25.4 1.3 %collective-permute-done.9.refs_3_ = bf16[128,512]{1,0:T(8,128)(2,1)S(1)} collective-permute-done((bf16[128,512]{1,0:T(8,128)(2,1)S(1)}, bf16[128,512]{1,0:T(8,128)(2,1)S(1)}, u32[]{:S(2)}, u32[]{:S(2)}) %collective-permute-start.9) | collective-permute-done | bytes 131104 | tf_op jit(solution)/shard_map/ppermute | solution.py:446
  26.6 1.5 %shard_map.133 = (bf16[512,128]{1,0:T(8,128)(2,1)S(1)}, bf16[256,512]{1,0:T(8,128)(2,1)S(1)}, bf16[256,512]{1,0:T(8,128)(2,1)S(1)}) custom-call(bf16[128,512]{1,0:T(8,128)(2,1)S(1)} %get-tuple-element.68.refs_0_, bf16[128,512]{1,0:T(8,128)(2,1)S(1)} %collective-permute-done.7.refs_1_, bf16[128,512]{1,0:T(8,128)(2,1)S(1)} %collective-permute-done.8.refs_2_, ...), custom_call_target="tpu_custom_call" | custom-call | flops 10000000 | bytes 30000 | tf_op jit(solution)/shard_map/pallas_call | solution.py:156
  28.2 2.6 %collective-permute-start.13 = (bf16[512,128]{1,0:T(8,128)(2,1)S(1)}, bf16[512,128]{1,0:T(8,128)(2,1)S(1)}, u32[]{:S(2)}, u32[]{:S(2)}) collective-permute-start(bf16[512,128]{1,0:T(8,128)(2,1)S(1)} %get-tuple-element.87.left_ref), channel_id=1, source_target_pairs={{0,16},{8,24},{16,0},{24,8},{1,17},{9,25},{17,1},{25,9},{2,18},{10... | collective-permute-start | bytes 393224 | tf_op jit(solution)/shard_map/ppermute | solution.py:540
  30.8 1.3 %shard_map.134 = (f32[1024,512]{1,0:T(8,128)S(1)}, f32[1024,512]{1,0:T(8,128)S(1)}, bf16[2048,512]{1,0:T(8,128)(2,1)S(1)}, bf16[512,128]{1,0:T(8,128)(2,1)S(1)}) custom-call(bf16[256,512]{1,0:T(8,128)(2,1)S(1)} %get-tuple-element.77.refs_0_, bf16[1024,512]{1,0:T(8,128)(2,1)S(1)} %copy-done.1, bf16[256,128]{1,0:T(8,128)(2,1)S(1)} %get-tuple-element.57.refs_2_, ...), custom_call_target="tpu_custom_call" | custom-call | flops 10000000 | bytes 30000 | tf_op jit(solution)/shard_map/pallas_call | solution.py:156
  32.1 1.6 %collective-permute-start.12 = (bf16[512,128]{1,0:T(8,128)(2,1)S(1)}, bf16[512,128]{1,0:T(8,128)(2,1)S(1)}, u32[]{:S(2)}, u32[]{:S(2)}) collective-permute-start(bf16[512,128]{1,0:T(8,128)(2,1)S(1)} %get-tuple-element.83.sum_ref), channel_id=1, source_target_pairs={{0,8},{8,0},{16,24},{24,16},{1,9},{9,1},{17,25},{25,17},{2,10},{10... | collective-permute-start | bytes 393224 | tf_op jit(solution)/shard_map/ppermute | solution.py:540
  33.7 0.6 %collective-permute-done.13.right_ref = bf16[512,128]{1,0:T(8,128)(2,1)S(1)} collective-permute-done((bf16[512,128]{1,0:T(8,128)(2,1)S(1)}, bf16[512,128]{1,0:T(8,128)(2,1)S(1)}, u32[]{:S(2)}, u32[]{:S(2)}) %collective-permute-start.13) | collective-permute-done | bytes 131104 | tf_op jit(solution)/shard_map/ppermute | solution.py:540
  34.5 1.9 %collective-permute-start.15 = (bf16[256,128]{1,0:T(8,128)(2,1)S(1)}, bf16[256,128]{1,0:T(8,128)(2,1)S(1)}, u32[]{:S(2)}, u32[]{:S(2)}) collective-permute-start(bf16[256,128]{1,0:T(8,128)(2,1)S(1)} %get-tuple-element.90), channel_id=1, source_target_pairs={{0,8},{8,0},{16,24},{24,16},{1,9},{9,1},{17,25},{25,17},{2,10},{10... | collective-permute-start | bytes 196616 | tf_op jit(solution)/shard_map/ppermute | solution.py:540
  36.4 0.7 %collective-permute-done.12.got_ref = bf16[512,128]{1,0:T(8,128)(2,1)S(1)} collective-permute-done((bf16[512,128]{1,0:T(8,128)(2,1)S(1)}, bf16[512,128]{1,0:T(8,128)(2,1)S(1)}, u32[]{:S(2)}, u32[]{:S(2)}) %collective-permute-start.12) | collective-permute-done | bytes 131104 | tf_op jit(solution)/shard_map/ppermute | solution.py:540
  37.1 0.7 %shard_map.135 = (f32[256,128]{1,0:T(8,128)}, f32[256,128]{1,0:T(8,128)}, f32[8,128]{1,0:T(8,128)S(1)}) custom-call(bf16[512,128]{1,0:T(8,128)(2,1)S(1)} %get-tuple-element.83.sum_ref, bf16[512,128]{1,0:T(8,128)(2,1)S(1)} %collective-permute-done.12.got_ref), custom_call_target="tpu_custom_call" | custom-call | flops 28000000000 | bytes 84000000 | tf_op jit(solution)/shard_map/pallas_call | solution.py:156
  37.9 1.6 %shard_map.136 = (bf16[1024,512]{1,0:T(8,128)(2,1)}, bf16[1024,512]{1,0:T(8,128)(2,1)}, f32[8,128]{1,0:T(8,128)S(1)}) custom-call(f32[1024,512]{1,0:T(8,128)S(1)} %get-tuple-element.80.mixed_ref, f32[1024,512]{1,0:T(8,128)S(1)} %get-tuple-element.81.grad_ref, bf16[2048,512]{1,0:T(8,128)(2,1)S(1)} %collective-permute-done.11.got_ref, ...), custom_call_target="tpu_custom_call" | custom-call | flops 10000000 | bytes 30000 | tf_op jit(solution)/shard_map/pallas_call | solution.py:156
  40.1 0.9 %shard_map.138 = (f32[256,128]{1,0:T(8,128)}, f32[256,128]{1,0:T(8,128)}) custom-call(bf16[256,128]{1,0:T(8,128)(2,1)S(1)} %get-tuple-element.88.refs_0_, bf16[256,128]{1,0:T(8,128)(2,1)S(1)} %collective-permute-done.14.refs_1_, bf16[256,128]{1,0:T(8,128)(2,1)S(1)} %collective-permute-done.15.refs_2_, bf16[256,128]{1,0:T(8,128)(2,1)S(1)} %collective-permute-done.16.refs_3_, ...), custom_call_target="tpu_custom_call" | custom-call | flops 10000000 | bytes 30000 | tf_op jit(solution)/shard_map/pallas_call | solution.py:156
  (38 shorter events, 4.2 us)
Async XLA Ops:
  0.6 1.6 %collective-permute-start = (bf16[256,128]{1,0:T(8,128)(2,1)}, bf16[256,128]{1,0:T(8,128)(2,1)S(1)}, u32[]{:S(2)}, u32[]{:S(2)}) collective-permute-start(bf16[256,128]{1,0:T(8,128)(2,1)} %bitcast.10), channel_id=1, source_target_pairs={{0,1},{1,0},{2,3},{3,2},{4,5},{5,4},{6,7},{7,6},{8,9},{9,8},{10,11... | collective-permute-start | bytes 196616 | tf_op jit(solution)/shard_map/ppermute | solution.py:14
  1.1 3.0 %copy-start.1 = (bf16[1024,512]{1,0:T(8,128)(2,1)S(1)}, bf16[1024,512]{1,0:T(8,128)(2,1)}, u32[]{:S(2)}) copy-start(bf16[1024,512]{1,0:T(8,128)(2,1)} %refs_1_.1) | copy-start | bytes 3145732
  1.2 3.0 %copy-start.2 = (bf16[16,16,128]{2,1,0:T(8,128)(2,1)S(1)}, bf16[16,16,128]{2,1,0:T(8,128)(2,1)}, u32[]{:S(2)}) copy-start(bf16[16,16,128]{2,1,0:T(8,128)(2,1)} %param.10) | copy-start | bytes 196612
  1.2 3.0 %copy-start.3 = (bf16[16,16,128]{2,1,0:T(8,128)(2,1)S(1)}, bf16[16,16,128]{2,1,0:T(8,128)(2,1)}, u32[]{:S(2)}) copy-start(bf16[16,16,128]{2,1,0:T(8,128)(2,1)} %param.13) | copy-start | bytes 196612
  1.2 1.5 %collective-permute-start.1 = (bf16[256,128]{1,0:T(8,128)(2,1)}, bf16[256,128]{1,0:T(8,128)(2,1)S(1)}, u32[]{:S(2)}, u32[]{:S(2)}) collective-permute-start(bf16[256,128]{1,0:T(8,128)(2,1)} %bitcast.12), channel_id=1, source_target_pairs={{0,1},{1,0},{2,3},{3,2},{4,5},{5,4},{6,7},{7,6},{8,9},{9,8},{10,11... | collective-permute-start | bytes 196616 | tf_op jit(solution)/shard_map/ppermute | solution.py:14
  1.3 2.9 %collective-permute-start.3 = (bf16[1024,512]{1,0:T(8,128)(2,1)}, bf16[1024,512]{1,0:T(8,128)(2,1)S(1)}, u32[]{:S(2)}, u32[]{:S(2)}) collective-permute-start(bf16[1024,512]{1,0:T(8,128)(2,1)} %refs_1_.1), channel_id=1, source_target_pairs={{0,1},{1,0},{2,3},{3,2},{4,5},{5,4},{6,7},{7,6},{8,9},{9,8},{10,11... | collective-permute-start | bytes 3145736 | tf_op jit(solution)/shard_map/ppermute | solution.py:14
  2.6 3.0 %collective-permute-start.2 = (bf16[1024,512]{1,0:T(8,128)(2,1)}, bf16[1024,512]{1,0:T(8,128)(2,1)S(1)}, u32[]{:S(2)}, u32[]{:S(2)}) collective-permute-start(bf16[1024,512]{1,0:T(8,128)(2,1)} %refs_4_.3), channel_id=1, source_target_pairs={{0,1},{1,0},{2,3},{3,2},{4,5},{5,4},{6,7},{7,6},{8,9},{9,8},{10,11... | collective-permute-start | bytes 3145736 | tf_op jit(solution)/shard_map/ppermute | solution.py:14
  4.2 6.6 %copy-start.4 = (bf16[2,128,128]{2,1,0:T(8,128)(2,1)S(1)}, bf16[2,128,128]{2,1,0:T(8,128)(2,1)}, u32[]{:S(2)}) copy-start(bf16[2,128,128]{2,1,0:T(8,128)(2,1)} %param.11) | copy-start | bytes 196612
  4.2 6.5 %copy-start.5 = (bf16[2,128,128]{2,1,0:T(8,128)(2,1)S(1)}, bf16[2,128,128]{2,1,0:T(8,128)(2,1)}, u32[]{:S(2)}) copy-start(bf16[2,128,128]{2,1,0:T(8,128)(2,1)} %param.12) | copy-start | bytes 196612
  4.2 6.5 %copy-start.6 = (s32[128]{0:T(128)S(1)}, s32[128]{0:T(128)}, u32[]{:S(2)}) copy-start(s32[128]{0:T(128)} %param.14) | copy-start | bytes 1540
  4.2 6.5 %copy-start.7 = (s32[128]{0:T(128)S(1)}, s32[128]{0:T(128)}, u32[]{:S(2)}) copy-start(s32[128]{0:T(128)} %param.15) | copy-start | bytes 1540
  6.3 6.8 %collective-permute-start.4 = (bf16[128,512]{1,0:T(8,128)(2,1)S(1)}, bf16[128,512]{1,0:T(8,128)(2,1)S(1)}, u32[]{:S(2)}, u32[]{:S(2)}) collective-permute-start(bf16[128,512]{1,0:T(8,128)(2,1)S(1)} %get-tuple-element.63), channel_id=1, source_target_pairs={{0,2},{1,3},{2,0},{3,1},{4,6},{5,7},{6,4},{7,5},{8,10},{9,11},{10,... | collective-permute-start | bytes 393224 | tf_op jit(solution)/shard_map/ppermute | solution.py:446
  9.2 8.1 %collective-permute-start.5 = (bf16[128,512]{1,0:T(8,128)(2,1)S(1)}, bf16[128,512]{1,0:T(8,128)(2,1)S(1)}, u32[]{:S(2)}, u32[]{:S(2)}) collective-permute-start(bf16[128,512]{1,0:T(8,128)(2,1)S(1)} %get-tuple-element.64), channel_id=1, source_target_pairs={{0,4},{1,5},{2,6},{3,7},{4,0},{5,1},{6,2},{7,3},{8,12},{9,13},{10,... | collective-permute-start | bytes 393224 | tf_op jit(solution)/shard_map/ppermute | solution.py:446
  10.7 6.5 %collective-permute-start.6 = (bf16[128,512]{1,0:T(8,128)(2,1)S(1)}, bf16[128,512]{1,0:T(8,128)(2,1)S(1)}, u32[]{:S(2)}, u32[]{:S(2)}) collective-permute-start(bf16[128,512]{1,0:T(8,128)(2,1)S(1)} %get-tuple-element.65), channel_id=1, source_target_pairs={{0,6},{1,7},{2,4},{3,5},{4,2},{5,3},{6,0},{7,1},{8,14},{9,15},{10,... | collective-permute-start | bytes 393224 | tf_op jit(solution)/shard_map/ppermute | solution.py:446
  18.3 6.8 %collective-permute-start.7 = (bf16[128,512]{1,0:T(8,128)(2,1)S(1)}, bf16[128,512]{1,0:T(8,128)(2,1)S(1)}, u32[]{:S(2)}, u32[]{:S(2)}) collective-permute-start(bf16[128,512]{1,0:T(8,128)(2,1)S(1)} %get-tuple-element.69), channel_id=1, source_target_pairs={{0,4},{1,5},{2,6},{3,7},{4,0},{5,1},{6,2},{7,3},{8,12},{9,13},{10,... | collective-permute-start | bytes 393224 | tf_op jit(solution)/shard_map/ppermute | solution.py:446
  19.9 5.5 %collective-permute-start.8 = (bf16[128,512]{1,0:T(8,128)(2,1)S(1)}, bf16[128,512]{1,0:T(8,128)(2,1)S(1)}, u32[]{:S(2)}, u32[]{:S(2)}) collective-permute-start(bf16[128,512]{1,0:T(8,128)(2,1)S(1)} %get-tuple-element.70), channel_id=1, source_target_pairs={{0,2},{1,3},{2,0},{3,1},{4,6},{5,7},{6,4},{7,5},{8,10},{9,11},{10,... | collective-permute-start | bytes 393224 | tf_op jit(solution)/shard_map/ppermute | solution.py:446
  20.4 6.2 %collective-permute-start.9 = (bf16[128,512]{1,0:T(8,128)(2,1)S(1)}, bf16[128,512]{1,0:T(8,128)(2,1)S(1)}, u32[]{:S(2)}, u32[]{:S(2)}) collective-permute-start(bf16[128,512]{1,0:T(8,128)(2,1)S(1)} %get-tuple-element.71), channel_id=1, source_target_pairs={{0,6},{1,7},{2,4},{3,5},{4,2},{5,3},{6,0},{7,1},{8,14},{9,15},{10,... | collective-permute-start | bytes 393224 | tf_op jit(solution)/shard_map/ppermute | solution.py:446
  22.4 8.4 %collective-permute-start.10 = (bf16[512,128]{1,0:T(8,128)(2,1)S(1)}, bf16[512,128]{1,0:T(8,128)(2,1)S(1)}, u32[]{:S(2)}, u32[]{:S(2)}) collective-permute-start(bf16[512,128]{1,0:T(8,128)(2,1)S(1)} %shard_map.132.refs_9_.refs_6_), channel_id=1, source_target_pairs={{0,16},{8,24},{16,0},{24,8},{1,17},{9,25},{17,1},{25,9},{2,18},{10... | collective-permute-start | bytes 393224 | tf_op jit(solution)/shard_map/ppermute | solution.py:540
  28.2 6.2 %collective-permute-start.13 = (bf16[512,128]{1,0:T(8,128)(2,1)S(1)}, bf16[512,128]{1,0:T(8,128)(2,1)S(1)}, u32[]{:S(2)}, u32[]{:S(2)}) collective-permute-start(bf16[512,128]{1,0:T(8,128)(2,1)S(1)} %get-tuple-element.87.left_ref), channel_id=1, source_target_pairs={{0,16},{8,24},{16,0},{24,8},{1,17},{9,25},{17,1},{25,9},{2,18},{10... | collective-permute-start | bytes 393224 | tf_op jit(solution)/shard_map/ppermute | solution.py:540
  32.1 5.0 %collective-permute-start.12 = (bf16[512,128]{1,0:T(8,128)(2,1)S(1)}, bf16[512,128]{1,0:T(8,128)(2,1)S(1)}, u32[]{:S(2)}, u32[]{:S(2)}) collective-permute-start(bf16[512,128]{1,0:T(8,128)(2,1)S(1)} %get-tuple-element.83.sum_ref), channel_id=1, source_target_pairs={{0,8},{8,0},{16,24},{24,16},{1,9},{9,1},{17,25},{25,17},{2,10},{10... | collective-permute-start | bytes 393224 | tf_op jit(solution)/shard_map/ppermute | solution.py:540
  33.7 4.2 %collective-permute-start.11 = (bf16[2048,512]{1,0:T(8,128)(2,1)S(1)}, bf16[2048,512]{1,0:T(8,128)(2,1)S(1)}, u32[]{:S(2)}, u32[]{:S(2)}) collective-permute-start(bf16[2048,512]{1,0:T(8,128)(2,1)S(1)} %get-tuple-element.82), channel_id=1, source_target_pairs={{0,1},{1,0},{2,3},{3,2},{4,5},{5,4},{6,7},{7,6},{8,9},{9,8},{10,11... | collective-permute-start | bytes 6291464 | tf_op jit(solution)/shard_map/ppermute | solution.py:14
  34.4 5.1 %collective-permute-start.14 = (bf16[256,128]{1,0:T(8,128)(2,1)S(1)}, bf16[256,128]{1,0:T(8,128)(2,1)S(1)}, u32[]{:S(2)}, u32[]{:S(2)}) collective-permute-start(bf16[256,128]{1,0:T(8,128)(2,1)S(1)} %get-tuple-element.89), channel_id=1, source_target_pairs={{0,9},{1,8},{2,11},{3,10},{4,13},{5,12},{6,15},{7,14},{8,1},{9,0},... | collective-permute-start | bytes 196616 | tf_op jit(solution)/shard_map/ppermute | solution.py:572
  34.5 5.6 %collective-permute-start.15 = (bf16[256,128]{1,0:T(8,128)(2,1)S(1)}, bf16[256,128]{1,0:T(8,128)(2,1)S(1)}, u32[]{:S(2)}, u32[]{:S(2)}) collective-permute-start(bf16[256,128]{1,0:T(8,128)(2,1)S(1)} %get-tuple-element.90), channel_id=1, source_target_pairs={{0,8},{8,0},{16,24},{24,16},{1,9},{9,1},{17,25},{25,17},{2,10},{10... | collective-permute-start | bytes 196616 | tf_op jit(solution)/shard_map/ppermute | solution.py:540
  36.4 3.7 %collective-permute-start.16 = (bf16[256,128]{1,0:T(8,128)(2,1)S(1)}, bf16[256,128]{1,0:T(8,128)(2,1)S(1)}, u32[]{:S(2)}, u32[]{:S(2)}) collective-permute-start(bf16[256,128]{1,0:T(8,128)(2,1)S(1)} %get-tuple-element.91), channel_id=1, source_target_pairs={{0,1},{1,0},{2,3},{3,2},{4,5},{5,4},{6,7},{7,6},{8,9},{9,8},{10,11... | collective-permute-start | bytes 196616 | tf_op jit(solution)/shard_map/ppermute | solution.py:14
  (1 other events, 2.7 us)

commit v7 on v6

--- a/solution.py
+++ b/solution.py
@@ -265,6 +265,17 @@
     return body
 
 
+def turn_blocks(half):
+    def body(own_ref, other_ref, _, out_ref):
+        parity = lax.axis_index("loop") % 2
+        pair_blocks = own_ref.shape[0] // half
+        for at, block in enumerate(pair_blocks_of(parity, pair_blocks)):
+            features = block_rows(own_ref, other_ref, block * half, half)
+            out_ref[:, at * 2 * half : (at + 1) * 2 * half] = features.T
+
+    return body
+
+
 def by_distance(bufs, order):
     return [bufs[0], *(bufs[1 + order.index(q)] for q in range(1, len(bufs)))]
 
@@ -281,8 +292,8 @@
 def column_weights(rows, cols):
     narrow = jnp.bfloat16
 
-    def body(up_ref, down_ref, perm_up_ref, perm_down_ref, *outs):
-        up_out, down_out, take_up_ref, take_down_ref = outs
+    def body(up_ref, down_ref, perm_up_ref, perm_down_ref, _, *outs):
+        up_out, up_turned, down_out, down_turned, take_up_ref, take_down_ref = outs
         me = lax.axis_index("loop")
         size = take_up_ref.shape[0]
         lead = lax.broadcasted_iota(jnp.int32, (size, size), 0)
@@ -294,8 +305,12 @@
         ).astype(narrow)
         for b in range(cols):
             span = slice(b * size, (b + 1) * size)
-            up_out[span, :] = dot(up_ref[span, :], take_up_ref[...], 1, 1).astype(narrow)
-            down_out[span, :] = dot(take_down_ref[...], down_ref[span, :]).astype(narrow)
+            up = dot(up_ref[span, :], take_up_ref[...], 1, 1)
+            down = dot(take_down_ref[...], down_ref[span, :])
+            up_out[span, :] = up.astype(narrow)
+            up_turned[span, :] = up.T.astype(narrow)
+            down_out[span, :] = down.astype(narrow)
+            down_turned[span, :] = down.T.astype(narrow)
 
     return body
 
@@ -305,20 +320,20 @@
     deep = 2 * rows
 
     def body(*refs):
-        bufs, (up_ref, down_ref) = by_distance(refs[:chips], FIRST_ORDER), refs[chips : chips + 2]
-        outs, (activated_ref, grad_pre_ref) = refs[chips + 2 : -2], refs[-2:]
+        bufs, weights = by_distance(refs[:chips], FIRST_ORDER), refs[chips : chips + 4]
+        outs, (activated_ref, grad_pre_ref) = refs[-chips - 2 : -2], refs[-2:]
         size = chips * deep
         for b in range(cols):
             span = slice(b * size, (b + 1) * size)
-            up, down = up_ref[span, :], down_ref[span, :]
+            up, up_turned, down, down_turned = (ref[span, :] for ref in weights)
             gelu_val, slope = gelu_parts(dot(up, one_col(bufs, b, deep)))
             activated = gelu_val.astype(narrow)
             activated_ref[span, :] = activated
             spread(outs, b, deep, dot(down, activated).astype(narrow))
-            grad_act = dot(down, one_col(bufs, cols + b, deep), 0, 0)
+            grad_act = dot(down_turned, one_col(bufs, cols + b, deep))
             grad_pre = (grad_act * slope).astype(narrow)
             grad_pre_ref[span, :] = grad_pre
-            spread(outs, cols + b, deep, dot(up, grad_pre, 0, 0).astype(narrow))
+            spread(outs, cols + b, deep, dot(up_turned, grad_pre).astype(narrow))
 
     return body
 
@@ -329,7 +344,7 @@
 
     def body(*refs):
         bufs = by_distance(refs[:chips], FIRST_ORDER)
-        activated_ref, grad_pre_ref, take_up_ref, take_down_ref, out_ref = refs[chips:]
+        activated_ref, grad_pre_ref, out_ref = refs[chips:]
         size = chips * deep
         for b in range(cols):
             span = slice(b * size, (b + 1) * size)
@@ -337,10 +352,8 @@
             grad = one_col(bufs, cols + b, deep)
             g_up = dot(grad_pre_ref[span, :], hid, 1, 1).astype(narrow)
             g_down = dot(grad, activated_ref[span, :], 1, 1).astype(narrow)
-            out_ref[span, :] = dot(g_up, take_up_ref[...]).astype(narrow)
-            out_ref[cols * size + b * size : cols * size + (b + 1) * size, :] = dot(
-                take_down_ref[...], g_down, 0, 0
-            ).astype(narrow)
+            out_ref[span, :] = g_up
+            out_ref[cols * size + b * size : cols * size + (b + 1) * size, :] = g_down
 
     return body
 
@@ -350,21 +363,23 @@
 
     def body(*refs):
         bufs = by_distance(refs[:chips], BACK_ORDER)
-        tok_ref, x_ref, cot_ref, d_ref, order_ref = refs[chips : chips + 5]
+        x_ref, d_ref, order_ref = refs[chips : chips + 3]
         grads_ref, back_ref, grad_ref = refs[-3:]
         parity = lax.axis_index("loop") % 2
-        pair_blocks = tok_ref.shape[0] // half
+        block = 2 * half
         unit = 2 * rows * cols
-        jobs = ((1, grad_ref, tok_ref, x_ref), (0, back_ref, cot_ref, d_ref))
-        for at, (job, grid_ref, own_ref, other_ref) in enumerate(jobs):
-            sent = one_col(bufs, job, unit)
-            grid_ref[...] = dot(order_ref[...], sent).astype(narrow)
+        pair_blocks = x_ref.shape[1] // block
+        jobs = ((1, grad_ref, x_ref), (0, back_ref, d_ref))
+        for at, (job, grid_ref, turned_ref) in enumerate(jobs):
+            grid_ref[...] = dot(order_ref[...], one_col(bufs, job, unit)).astype(narrow)
             high = grid_ref.shape[0] // pair_blocks
             grads = []
-            for place, block in enumerate(pair_blocks_of(parity, pair_blocks)):
-                part = slice(place * high, (place + 1) * high)
-                features = block_rows(own_ref, other_ref, block * half, half)
-                grads.append(dot(grid_ref[part, :], features, 1, 1))
+            for place in range(0, pair_blocks, 2):
+                both = dot(
+                    grid_ref[place * high : (place + 2) * high, :],
+                    turned_ref[:, place * block : (place + 2) * block],
+                )
+                grads += [both[:high, :block], both[high:, block:]]
             both = own_first(jnp.concatenate(grads, 0), parity).astype(narrow)
             size = both.shape[0] // 2
             for turn in range(2):
@@ -430,13 +445,17 @@
 
 
 def total_col_grads(scale):
-    def body(sum_ref, got_ref, up_ref, down_ref, done_ref):
+    def body(sum_ref, got_ref, take_up_ref, take_down_ref, up_ref, down_ref, done_ref):
         done_ref[...] = jnp.zeros_like(done_ref)
-        size = up_ref.shape[0]
-        for at, out in enumerate((up_ref, down_ref)):
-            span = slice(at * size, (at + 1) * size)
-            both = sum_ref[span, :].astype(jnp.float32) + got_ref[span, :].astype(jnp.float32)
-            out[...] = both * scale
+        size = take_up_ref.shape[0]
+        count = up_ref.shape[0]
+        for start in range(0, count, size):
+            near = slice(start, start + size)
+            far = slice(count + start, count + start + size)
+            up = [dot(ref[near, :], take_up_ref[...]) for ref in (sum_ref, got_ref)]
+            down = [dot(take_down_ref[...], ref[far, :], 0, 0) for ref in (sum_ref, got_ref)]
+            up_ref[near, :] = (up[0] + up[1]) * scale
+            down_ref[near, :] = (down[0] + down[1]) * scale
 
     return body
 
@@ -509,21 +528,26 @@
     )
     cells = exchange(sent, "loop", FIRST_ORDER)
     square = struct(cols * size, size)
-    up_cols, down_cols, take_up, take_down = call(
+    *col_weights, take_up, take_down = call(
         column_weights(rows, cols),
-        [square] * 2 + [struct(size, size)] * 2,
+        [square] * 4 + [struct(size, size)] * 2,
         up_second.reshape(square.shape),
         down_first.reshape(square.shape),
         perm_up.reshape(1, size),
         perm_down.reshape(1, size),
+        sent[0],
         micros=2,
     )
+    turned = struct(toks, 2 * feature_rows)
+    (x_turned,) = call(turn_blocks(half), [turned], tokens, other_x, sent[0], micros=1)
+    (d_turned,) = call(turn_blocks(half), [turned], cotangent, other_d, sent[0], micros=1)
     *sent, activated, grad_pre = call(
         columns(chips, rows, cols),
         [buf] * chips + [grid] * 2,
         *cells,
-        up_cols,
-        down_cols,
+        *col_weights,
+        x_turned,
+        d_turned,
     )
     back = exchange(sent, "loop", BACK_ORDER)
     (col_grads,) = call(
@@ -532,8 +556,6 @@
         *cells,
         activated,
         grad_pre,
-        take_up,
-        take_down,
     )
 
     def over_dp(value, apart):
@@ -543,10 +565,8 @@
         row_grads(chips, rows, cols, half),
         [struct(2 * grid_rows, block), grid, grid],
         *back,
-        tokens,
-        other_x,
-        cotangent,
-        other_d,
+        x_turned,
+        d_turned,
         order_back,
         col_grads,
     )
@@ -583,6 +603,8 @@
         [struct(*square.shape, wide)] * 2 + [token],
         col_sum,
         over_dp(col_sum, COL_APART[1]),
+        take_up,
+        take_down,
         to_hbm=2,
         micros=COL_MICROS,
     )

time: 41.1 us -> 41.2 us (level)
  waiting for transfers between devices: 12.4 us -> 11.3 us
  Pallas kernels: 9.68 us -> 10.5 us
    ppermute x6, waiting for transfers between devices: 7.74 us -> 6.56 us  [exchange(): return [bufs[0]] + [lax.ppermute(bufs[q], axis, pairs[q]) for q in order]]
    pallas_call x12 -> x14, Pallas kernels: 9.68 us -> 10.5 us  [call(): pl.pallas_call(body, out_shape=outs, in_specs=[whole] * len(args), out_sp...]
  transfers between devices with their start and end apart: 17 -> 17, of which waited for: 12 -> 12; matrix products, arithmetic and copies ran while one was open for 0% -> 0% of each run, Pallas kernels for 17% -> 20%
where the time goes in v7:
time: 41.2 us; the launch traced here: 41 us
  starting transfers between devices  18.4 us (45%)
  waiting for transfers between devices  11.3 us (27%)
  Pallas kernels  10.5 us (25%)
  between operations  0.77 us (2%)
    pallas_call x14, Pallas kernels, call(): pl.pallas_call(body, out_shape=outs, in_specs=[whole] * len(args), out_sp...  10.5 us
    ppermute x4, starting transfers between devices, over_dp(): return lax.ppermute(value, 'dp', [(s, s ^ apart) for s in range(dps)])  8.87 us
    ppermute x6, starting transfers between devices, exchange(): return [bufs[0]] + [lax.ppermute(bufs[q], axis, pairs[q]) for q in order]  8.02 us
    ppermute x6, waiting for transfers between devices, exchange(): return [bufs[0]] + [lax.ppermute(bufs[q], axis, pairs[q]) for q in order]  6.56 us
    ppermute x6, waiting for transfers between devices, from_partner(): return lax.ppermute(value, axis, pairs)  2.81 us
    ppermute x4, waiting for transfers between devices, over_dp(): return lax.ppermute(value, 'dp', [(s, s ^ apart) for s in range(dps)])  1.97 us
    ppermute x6, starting transfers between devices, from_partner(): return lax.ppermute(value, axis, pairs)  1.39 us
  transfers between devices with their start and end apart: 17, of which 12 were waited for; matrix products, arithmetic and copies ran while one was open for 0% of the time, Pallas kernels for 20%

profile of v7, /device:TPU:0, one launch (start us, length us, event | category | flops | bytes accessed | tf_op | source)
XLA Modules:
  0.0 41.0 jit_solution(15720991517382423518)
XLA Ops:
  1.7 0.6 %collective-permute-done.refs_3_ = bf16[256,128]{1,0:T(8,128)(2,1)S(1)} collective-permute-done((bf16[256,128]{1,0:T(8,128)(2,1)}, bf16[256,128]{1,0:T(8,128)(2,1)S(1)}, u32[]{:S(2)}, u32[]{:S(2)}) %collective-permute-start) | collective-permute-done | bytes 65568 | tf_op jit(solution)/shard_map/ppermute | solution.py:14
  2.9 1.2 %collective-permute-done.3.refs_1_.other_ref = bf16[1024,512]{1,0:T(8,128)(2,1)S(1)} collective-permute-done((bf16[1024,512]{1,0:T(8,128)(2,1)}, bf16[1024,512]{1,0:T(8,128)(2,1)S(1)}, u32[]{:S(2)}, u32[]{:S(2)}) %collective-permute-start.3) | collective-permute-done | bytes 1048608 | tf_op jit(solution)/shard_map/ppermute | solution.py:14
  4.2 0.9 %shard_map.128 = (bf16[64,512]{1,0:T(8,128)(2,1)S(1)}, bf16[64,512]{1,0:T(8,128)(2,1)S(1)}, bf16[64,512]{1,0:T(8,128)(2,1)S(1)}, bf16[64,512]{1,0:T(8,128)(2,1)S...) custom-call(bf16[1024,512]{1,0:T(8,128)(2,1)S(1)} %copy-done.1, ...), custom_call_target="tpu_custom_call" | custom-call | flops 10000000 | bytes 30000 | tf_op jit(solution)/shard_map/pallas_call | solution.py:156
  5.7 0.6 %shard_map.129 = (bf16[128,512]{1,0:T(8,128)(2,1)S(1)}, bf16[128,512]{1,0:T(8,128)(2,1)S(1)}, bf16[128,512]{1,0:T(8,128)(2,1)S(1)}, bf16[128,512]{1,0:T(8,128)(2,1)S(1)}) custom-call(bf16[1024,512]{1,0:T(8,128)(2,1)S(1)} %copy-done, bf16[1024,512]{1,0:T(8,128)(2,1)S(1)} %collective-permute-done.2.refs_1_.other_ref, ...), custom_call_target="tpu_custom_call" | custom-call | flops 10000000 | bytes 30000 | tf_op jit(solution)/shard_map/pallas_call | solution.py:156
  6.3 2.9 %collective-permute-start.4 = (bf16[128,512]{1,0:T(8,128)(2,1)S(1)}, bf16[128,512]{1,0:T(8,128)(2,1)S(1)}, u32[]{:S(2)}, u32[]{:S(2)}) collective-permute-start(bf16[128,512]{1,0:T(8,128)(2,1)S(1)} %get-tuple-element.65), channel_id=1, source_target_pairs={{0,2},{1,3},{2,0},{3,1},{4,6},{5,7},{6,4},{7,5},{8,10},{9,11},{10,... | collective-permute-start | bytes 393224 | tf_op jit(solution)/shard_map/ppermute | solution.py:465
  9.2 1.5 %collective-permute-start.5 = (bf16[128,512]{1,0:T(8,128)(2,1)S(1)}, bf16[128,512]{1,0:T(8,128)(2,1)S(1)}, u32[]{:S(2)}, u32[]{:S(2)}) collective-permute-start(bf16[128,512]{1,0:T(8,128)(2,1)S(1)} %get-tuple-element.66), channel_id=1, source_target_pairs={{0,4},{1,5},{2,6},{3,7},{4,0},{5,1},{6,2},{7,3},{8,12},{9,13},{10,... | collective-permute-start | bytes 393224 | tf_op jit(solution)/shard_map/ppermute | solution.py:465
  11.1 0.7 %shard_map.131.refs_8_.refs_4_ = bf16[512,2048]{1,0:T(8,128)(2,1)S(1)} custom-call(bf16[1024,512]{1,0:T(8,128)(2,1)S(1)} %copy-done.1, bf16[1024,512]{1,0:T(8,128)(2,1)S(1)} %collective-permute-done.3.refs_1_.other_ref, bf16[128,512]{1,0:T(8,128)(2,1)S(1)} %get-tuple-element.64._.refs_0_), custom_call_target="tpu_custom_call" | custom-call | flops 1000000000 | bytes 3000000 | tf_op jit(solution)/shard_map/pallas_call | solution.py:156
  11.8 0.7 %shard_map.132.refs_9_.refs_5_ = bf16[512,2048]{1,0:T(8,128)(2,1)S(1)} custom-call(bf16[1024,512]{1,0:T(8,128)(2,1)S(1)} %copy-done, bf16[1024,512]{1,0:T(8,128)(2,1)S(1)} %collective-permute-done.2.refs_1_.other_ref, bf16[128,512]{1,0:T(8,128)(2,1)S(1)} %get-tuple-element.64._.refs_0_), custom_call_target="tpu_custom_call" | custom-call | flops 1000000000 | bytes 3000000 | tf_op jit(solution)/shard_map/pallas_call | solution.py:156
  13.1 4.2 %collective-permute-done.5.refs_2_ = bf16[128,512]{1,0:T(8,128)(2,1)S(1)} collective-permute-done((bf16[128,512]{1,0:T(8,128)(2,1)S(1)}, bf16[128,512]{1,0:T(8,128)(2,1)S(1)}, u32[]{:S(2)}, u32[]{:S(2)}) %collective-permute-start.5) | collective-permute-done | bytes 131104 | tf_op jit(solution)/shard_map/ppermute | solution.py:465
  17.2 1.0 %shard_map.133 = (bf16[128,512]{1,0:T(8,128)(2,1)S(1)}, bf16[128,512]{1,0:T(8,128)(2,1)S(1)}, bf16[128,512]{1,0:T(8,128)(2,1)S(1)}, bf16[128,512]{1,0:T(8,128)(2...) custom-call(bf16[128,512]{1,0:T(8,128)(2,1)S(1)} %get-tuple-element.64._.refs_0_, ...), custom_call_target="tpu_custom_call" | custom-call | flops 10000000 | bytes 30000 | tf_op jit(solution)/shard_map/pallas_call | solution.py:156
  18.3 1.6 %collective-permute-start.7 = (bf16[128,512]{1,0:T(8,128)(2,1)S(1)}, bf16[128,512]{1,0:T(8,128)(2,1)S(1)}, u32[]{:S(2)}, u32[]{:S(2)}) collective-permute-start(bf16[128,512]{1,0:T(8,128)(2,1)S(1)} %get-tuple-element.73), channel_id=1, source_target_pairs={{0,4},{1,5},{2,6},{3,7},{4,0},{5,1},{6,2},{7,3},{8,12},{9,13},{10,... | collective-permute-start | bytes 393224 | tf_op jit(solution)/shard_map/ppermute | solution.py:465
  20.4 1.4 %collective-permute-start.9 = (bf16[128,512]{1,0:T(8,128)(2,1)S(1)}, bf16[128,512]{1,0:T(8,128)(2,1)S(1)}, u32[]{:S(2)}, u32[]{:S(2)}) collective-permute-start(bf16[128,512]{1,0:T(8,128)(2,1)S(1)} %get-tuple-element.75), channel_id=1, source_target_pairs={{0,6},{1,7},{2,4},{3,5},{4,2},{5,3},{6,0},{7,1},{8,14},{9,15},{10,... | collective-permute-start | bytes 393224 | tf_op jit(solution)/shard_map/ppermute | solution.py:465
  22.1 2.7 %collective-permute-start.10 = (bf16[512,128]{1,0:T(8,128)(2,1)S(1)}, bf16[512,128]{1,0:T(8,128)(2,1)S(1)}, u32[]{:S(2)}, u32[]{:S(2)}) collective-permute-start(bf16[512,128]{1,0:T(8,128)(2,1)S(1)} %shard_map.134.refs_7_.refs_6_), channel_id=1, source_target_pairs={{0,16},{8,24},{16,0},{24,8},{1,17},{9,25},{17,1},{25,9},{2,18},{10... | collective-permute-start | bytes 393224 | tf_op jit(solution)/shard_map/ppermute | solution.py:562
  25.4 1.3 %collective-permute-done.9.refs_3_ = bf16[128,512]{1,0:T(8,128)(2,1)S(1)} collective-permute-done((bf16[128,512]{1,0:T(8,128)(2,1)S(1)}, bf16[128,512]{1,0:T(8,128)(2,1)S(1)}, u32[]{:S(2)}, u32[]{:S(2)}) %collective-permute-start.9) | collective-permute-done | bytes 131104 | tf_op jit(solution)/shard_map/ppermute | solution.py:465
  26.6 1.1 %shard_map.135 = (bf16[512,128]{1,0:T(8,128)(2,1)S(1)}, bf16[256,512]{1,0:T(8,128)(2,1)S(1)}, bf16[256,512]{1,0:T(8,128)(2,1)S(1)}) custom-call(bf16[128,512]{1,0:T(8,128)(2,1)S(1)} %get-tuple-element.72.refs_0_, bf16[128,512]{1,0:T(8,128)(2,1)S(1)} %collective-permute-done.7.refs_1_, bf16[128,512]{1,0:T(8,128)(2,1)S(1)} %collective-permute-done.8.refs_2_, ...), custom_call_target="tpu_custom_call" | custom-call | flops 10000000 | bytes 30000 | tf_op jit(solution)/shard_map/pallas_call | solution.py:156
  27.7 2.7 %collective-permute-start.13 = (bf16[512,128]{1,0:T(8,128)(2,1)S(1)}, bf16[512,128]{1,0:T(8,128)(2,1)S(1)}, u32[]{:S(2)}, u32[]{:S(2)}) collective-permute-start(bf16[512,128]{1,0:T(8,128)(2,1)S(1)} %get-tuple-element.91.left_ref), channel_id=1, source_target_pairs={{0,16},{8,24},{16,0},{24,8},{1,17},{9,25},{17,1},{25,9},{2,18},{10... | collective-permute-start | bytes 393224 | tf_op jit(solution)/shard_map/ppermute | solution.py:562
  30.4 1.3 %shard_map.136 = (f32[1024,512]{1,0:T(8,128)S(1)}, f32[1024,512]{1,0:T(8,128)S(1)}, bf16[2048,512]{1,0:T(8,128)(2,1)S(1)}, bf16[512,128]{1,0:T(8,128)(2,1)S(1)}) custom-call(bf16[256,512]{1,0:T(8,128)(2,1)S(1)} %get-tuple-element.79.refs_0_, bf16[1024,512]{1,0:T(8,128)(2,1)S(1)} %copy-done.1, bf16[256,128]{1,0:T(8,128)(2,1)S(1)} %get-tuple-element.59.refs_2_, ...), custom_call_target="tpu_custom_call" | custom-call | flops 10000000 | bytes 30000 | tf_op jit(solution)/shard_map/pallas_call | solution.py:156
  31.6 1.9 %collective-permute-start.12 = (bf16[512,128]{1,0:T(8,128)(2,1)S(1)}, bf16[512,128]{1,0:T(8,128)(2,1)S(1)}, u32[]{:S(2)}, u32[]{:S(2)}) collective-permute-start(bf16[512,128]{1,0:T(8,128)(2,1)S(1)} %get-tuple-element.85.sum_ref), channel_id=1, source_target_pairs={{0,8},{8,0},{16,24},{24,16},{1,9},{9,1},{17,25},{25,17},{2,10},{10... | collective-permute-start | bytes 393224 | tf_op jit(solution)/shard_map/ppermute | solution.py:562
  33.5 0.7 %collective-permute-done.13.right_ref = bf16[512,128]{1,0:T(8,128)(2,1)S(1)} collective-permute-done((bf16[512,128]{1,0:T(8,128)(2,1)S(1)}, bf16[512,128]{1,0:T(8,128)(2,1)S(1)}, u32[]{:S(2)}, u32[]{:S(2)}) %collective-permute-start.13) | collective-permute-done | bytes 131104 | tf_op jit(solution)/shard_map/ppermute | solution.py:562
  34.3 1.6 %collective-permute-start.15 = (bf16[256,128]{1,0:T(8,128)(2,1)S(1)}, bf16[256,128]{1,0:T(8,128)(2,1)S(1)}, u32[]{:S(2)}, u32[]{:S(2)}) collective-permute-start(bf16[256,128]{1,0:T(8,128)(2,1)S(1)} %get-tuple-element.94), channel_id=1, source_target_pairs={{0,8},{8,0},{16,24},{24,16},{1,9},{9,1},{17,25},{25,17},{2,10},{10... | collective-permute-start | bytes 196616 | tf_op jit(solution)/shard_map/ppermute | solution.py:562
  36.7 0.9 %shard_map.137 = (f32[256,128]{1,0:T(8,128)}, f32[256,128]{1,0:T(8,128)}, f32[8,128]{1,0:T(8,128)S(1)}) custom-call(bf16[512,128]{1,0:T(8,128)(2,1)S(1)} %get-tuple-element.85.sum_ref, bf16[512,128]{1,0:T(8,128)(2,1)S(1)} %collective-permute-done.12.got_ref, bf16[128,128]{1,0:T(8,128)(2,1)S(1)} %get-tuple-element.86.take_up_ref, ...), custom_call_target="tpu_custom_call" | custom-call | flops 28000000000 | bytes 84000000 | tf_op jit(solution)/shard_map/pallas_call | solution.py:156
  37.7 1.6 %shard_map.138 = (bf16[1024,512]{1,0:T(8,128)(2,1)}, bf16[1024,512]{1,0:T(8,128)(2,1)}, f32[8,128]{1,0:T(8,128)S(1)}) custom-call(f32[1024,512]{1,0:T(8,128)S(1)} %get-tuple-element.82.mixed_ref, f32[1024,512]{1,0:T(8,128)S(1)} %get-tuple-element.83.grad_ref, bf16[2048,512]{1,0:T(8,128)(2,1)S(1)} %collective-permute-done.11.got_ref, ...), custom_call_target="tpu_custom_call" | custom-call | flops 10000000 | bytes 30000 | tf_op jit(solution)/shard_map/pallas_call | solution.py:156
  39.3 0.8 %collective-permute-done.15.refs_2_ = bf16[256,128]{1,0:T(8,128)(2,1)S(1)} collective-permute-done((bf16[256,128]{1,0:T(8,128)(2,1)S(1)}, bf16[256,128]{1,0:T(8,128)(2,1)S(1)}, u32[]{:S(2)}, u32[]{:S(2)}) %collective-permute-start.15) | collective-permute-done | bytes 65568 | tf_op jit(solution)/shard_map/ppermute | solution.py:562
  40.1 1.0 %shard_map.140 = (f32[256,128]{1,0:T(8,128)}, f32[256,128]{1,0:T(8,128)}) custom-call(bf16[256,128]{1,0:T(8,128)(2,1)S(1)} %get-tuple-element.92.refs_0_, bf16[256,128]{1,0:T(8,128)(2,1)S(1)} %collective-permute-done.14.refs_1_, bf16[256,128]{1,0:T(8,128)(2,1)S(1)} %collective-permute-done.15.refs_2_, bf16[256,128]{1,0:T(8,128)(2,1)S(1)} %collective-permute-done.16.refs_3_, ...), custom_call_target="tpu_custom_call" | custom-call | flops 10000000 | bytes 30000 | tf_op jit(solution)/shard_map/pallas_call | solution.py:156
  (40 shorter events, 5.5 us)
Async XLA Ops:
  0.6 1.6 %collective-permute-start = (bf16[256,128]{1,0:T(8,128)(2,1)}, bf16[256,128]{1,0:T(8,128)(2,1)S(1)}, u32[]{:S(2)}, u32[]{:S(2)}) collective-permute-start(bf16[256,128]{1,0:T(8,128)(2,1)} %bitcast.10), channel_id=1, source_target_pairs={{0,1},{1,0},{2,3},{3,2},{4,5},{5,4},{6,7},{7,6},{8,9},{9,8},{10,11... | collective-permute-start | bytes 196616 | tf_op jit(solution)/shard_map/ppermute | solution.py:14
  1.1 3.0 %copy-start.1 = (bf16[1024,512]{1,0:T(8,128)(2,1)S(1)}, bf16[1024,512]{1,0:T(8,128)(2,1)}, u32[]{:S(2)}) copy-start(bf16[1024,512]{1,0:T(8,128)(2,1)} %refs_1_.1) | copy-start | bytes 3145732
  1.2 3.0 %copy-start.2 = (bf16[16,16,128]{2,1,0:T(8,128)(2,1)S(1)}, bf16[16,16,128]{2,1,0:T(8,128)(2,1)}, u32[]{:S(2)}) copy-start(bf16[16,16,128]{2,1,0:T(8,128)(2,1)} %param.10) | copy-start | bytes 196612
  1.2 3.0 %copy-start.3 = (bf16[16,16,128]{2,1,0:T(8,128)(2,1)S(1)}, bf16[16,16,128]{2,1,0:T(8,128)(2,1)}, u32[]{:S(2)}) copy-start(bf16[16,16,128]{2,1,0:T(8,128)(2,1)} %param.13) | copy-start | bytes 196612
  1.2 1.5 %collective-permute-start.1 = (bf16[256,128]{1,0:T(8,128)(2,1)}, bf16[256,128]{1,0:T(8,128)(2,1)S(1)}, u32[]{:S(2)}, u32[]{:S(2)}) collective-permute-start(bf16[256,128]{1,0:T(8,128)(2,1)} %bitcast.12), channel_id=1, source_target_pairs={{0,1},{1,0},{2,3},{3,2},{4,5},{5,4},{6,7},{7,6},{8,9},{9,8},{10,11... | collective-permute-start | bytes 196616 | tf_op jit(solution)/shard_map/ppermute | solution.py:14
  1.3 2.9 %collective-permute-start.3 = (bf16[1024,512]{1,0:T(8,128)(2,1)}, bf16[1024,512]{1,0:T(8,128)(2,1)S(1)}, u32[]{:S(2)}, u32[]{:S(2)}) collective-permute-start(bf16[1024,512]{1,0:T(8,128)(2,1)} %refs_1_.1), channel_id=1, source_target_pairs={{0,1},{1,0},{2,3},{3,2},{4,5},{5,4},{6,7},{7,6},{8,9},{9,8},{10,11... | collective-permute-start | bytes 3145736 | tf_op jit(solution)/shard_map/ppermute | solution.py:14
  2.6 3.0 %collective-permute-start.2 = (bf16[1024,512]{1,0:T(8,128)(2,1)}, bf16[1024,512]{1,0:T(8,128)(2,1)S(1)}, u32[]{:S(2)}, u32[]{:S(2)}) collective-permute-start(bf16[1024,512]{1,0:T(8,128)(2,1)} %refs_4_.1), channel_id=1, source_target_pairs={{0,1},{1,0},{2,3},{3,2},{4,5},{5,4},{6,7},{7,6},{8,9},{9,8},{10,11... | collective-permute-start | bytes 3145736 | tf_op jit(solution)/shard_map/ppermute | solution.py:14
  4.2 6.6 %copy-start.4 = (bf16[2,128,128]{2,1,0:T(8,128)(2,1)S(1)}, bf16[2,128,128]{2,1,0:T(8,128)(2,1)}, u32[]{:S(2)}) copy-start(bf16[2,128,128]{2,1,0:T(8,128)(2,1)} %param.11) | copy-start | bytes 196612
  4.2 6.5 %copy-start.5 = (bf16[2,128,128]{2,1,0:T(8,128)(2,1)S(1)}, bf16[2,128,128]{2,1,0:T(8,128)(2,1)}, u32[]{:S(2)}) copy-start(bf16[2,128,128]{2,1,0:T(8,128)(2,1)} %param.12) | copy-start | bytes 196612
  4.2 6.5 %copy-start.6 = (s32[128]{0:T(128)S(1)}, s32[128]{0:T(128)}, u32[]{:S(2)}) copy-start(s32[128]{0:T(128)} %param.14) | copy-start | bytes 1540
  4.2 6.5 %copy-start.7 = (s32[128]{0:T(128)S(1)}, s32[128]{0:T(128)}, u32[]{:S(2)}) copy-start(s32[128]{0:T(128)} %param.15) | copy-start | bytes 1540
  6.3 6.8 %collective-permute-start.4 = (bf16[128,512]{1,0:T(8,128)(2,1)S(1)}, bf16[128,512]{1,0:T(8,128)(2,1)S(1)}, u32[]{:S(2)}, u32[]{:S(2)}) collective-permute-start(bf16[128,512]{1,0:T(8,128)(2,1)S(1)} %get-tuple-element.65), channel_id=1, source_target_pairs={{0,2},{1,3},{2,0},{3,1},{4,6},{5,7},{6,4},{7,5},{8,10},{9,11},{10,... | collective-permute-start | bytes 393224 | tf_op jit(solution)/shard_map/ppermute | solution.py:465
  9.2 8.1 %collective-permute-start.5 = (bf16[128,512]{1,0:T(8,128)(2,1)S(1)}, bf16[128,512]{1,0:T(8,128)(2,1)S(1)}, u32[]{:S(2)}, u32[]{:S(2)}) collective-permute-start(bf16[128,512]{1,0:T(8,128)(2,1)S(1)} %get-tuple-element.66), channel_id=1, source_target_pairs={{0,4},{1,5},{2,6},{3,7},{4,0},{5,1},{6,2},{7,3},{8,12},{9,13},{10,... | collective-permute-start | bytes 393224 | tf_op jit(solution)/shard_map/ppermute | solution.py:465
  10.7 6.5 %collective-permute-start.6 = (bf16[128,512]{1,0:T(8,128)(2,1)S(1)}, bf16[128,512]{1,0:T(8,128)(2,1)S(1)}, u32[]{:S(2)}, u32[]{:S(2)}) collective-permute-start(bf16[128,512]{1,0:T(8,128)(2,1)S(1)} %get-tuple-element.67), channel_id=1, source_target_pairs={{0,6},{1,7},{2,4},{3,5},{4,2},{5,3},{6,0},{7,1},{8,14},{9,15},{10,... | collective-permute-start | bytes 393224 | tf_op jit(solution)/shard_map/ppermute | solution.py:465
  18.3 6.5 %collective-permute-start.7 = (bf16[128,512]{1,0:T(8,128)(2,1)S(1)}, bf16[128,512]{1,0:T(8,128)(2,1)S(1)}, u32[]{:S(2)}, u32[]{:S(2)}) collective-permute-start(bf16[128,512]{1,0:T(8,128)(2,1)S(1)} %get-tuple-element.73), channel_id=1, source_target_pairs={{0,4},{1,5},{2,6},{3,7},{4,0},{5,1},{6,2},{7,3},{8,12},{9,13},{10,... | collective-permute-start | bytes 393224 | tf_op jit(solution)/shard_map/ppermute | solution.py:465
  19.9 5.5 %collective-permute-start.8 = (bf16[128,512]{1,0:T(8,128)(2,1)S(1)}, bf16[128,512]{1,0:T(8,128)(2,1)S(1)}, u32[]{:S(2)}, u32[]{:S(2)}) collective-permute-start(bf16[128,512]{1,0:T(8,128)(2,1)S(1)} %get-tuple-element.74), channel_id=1, source_target_pairs={{0,2},{1,3},{2,0},{3,1},{4,6},{5,7},{6,4},{7,5},{8,10},{9,11},{10,... | collective-permute-start | bytes 393224 | tf_op jit(solution)/shard_map/ppermute | solution.py:465
  20.4 6.2 %collective-permute-start.9 = (bf16[128,512]{1,0:T(8,128)(2,1)S(1)}, bf16[128,512]{1,0:T(8,128)(2,1)S(1)}, u32[]{:S(2)}, u32[]{:S(2)}) collective-permute-start(bf16[128,512]{1,0:T(8,128)(2,1)S(1)} %get-tuple-element.75), channel_id=1, source_target_pairs={{0,6},{1,7},{2,4},{3,5},{4,2},{5,3},{6,0},{7,1},{8,14},{9,15},{10,... | collective-permute-start | bytes 393224 | tf_op jit(solution)/shard_map/ppermute | solution.py:465
  22.1 8.2 %collective-permute-start.10 = (bf16[512,128]{1,0:T(8,128)(2,1)S(1)}, bf16[512,128]{1,0:T(8,128)(2,1)S(1)}, u32[]{:S(2)}, u32[]{:S(2)}) collective-permute-start(bf16[512,128]{1,0:T(8,128)(2,1)S(1)} %shard_map.134.refs_7_.refs_6_), channel_id=1, source_target_pairs={{0,16},{8,24},{16,0},{24,8},{1,17},{9,25},{17,1},{25,9},{2,18},{10... | collective-permute-start | bytes 393224 | tf_op jit(solution)/shard_map/ppermute | solution.py:562
  27.7 6.5 %collective-permute-start.13 = (bf16[512,128]{1,0:T(8,128)(2,1)S(1)}, bf16[512,128]{1,0:T(8,128)(2,1)S(1)}, u32[]{:S(2)}, u32[]{:S(2)}) collective-permute-start(bf16[512,128]{1,0:T(8,128)(2,1)S(1)} %get-tuple-element.91.left_ref), channel_id=1, source_target_pairs={{0,16},{8,24},{16,0},{24,8},{1,17},{9,25},{17,1},{25,9},{2,18},{10... | collective-permute-start | bytes 393224 | tf_op jit(solution)/shard_map/ppermute | solution.py:562
  31.6 5.0 %collective-permute-start.12 = (bf16[512,128]{1,0:T(8,128)(2,1)S(1)}, bf16[512,128]{1,0:T(8,128)(2,1)S(1)}, u32[]{:S(2)}, u32[]{:S(2)}) collective-permute-start(bf16[512,128]{1,0:T(8,128)(2,1)S(1)} %get-tuple-element.85.sum_ref), channel_id=1, source_target_pairs={{0,8},{8,0},{16,24},{24,16},{1,9},{9,1},{17,25},{25,17},{2,10},{10... | collective-permute-start | bytes 393224 | tf_op jit(solution)/shard_map/ppermute | solution.py:562
  33.5 4.2 %collective-permute-start.11 = (bf16[2048,512]{1,0:T(8,128)(2,1)S(1)}, bf16[2048,512]{1,0:T(8,128)(2,1)S(1)}, u32[]{:S(2)}, u32[]{:S(2)}) collective-permute-start(bf16[2048,512]{1,0:T(8,128)(2,1)S(1)} %get-tuple-element.84), channel_id=1, source_target_pairs={{0,1},{1,0},{2,3},{3,2},{4,5},{5,4},{6,7},{7,6},{8,9},{9,8},{10,11... | collective-permute-start | bytes 6291464 | tf_op jit(solution)/shard_map/ppermute | solution.py:14
  34.2 5.1 %collective-permute-start.14 = (bf16[256,128]{1,0:T(8,128)(2,1)S(1)}, bf16[256,128]{1,0:T(8,128)(2,1)S(1)}, u32[]{:S(2)}, u32[]{:S(2)}) collective-permute-start(bf16[256,128]{1,0:T(8,128)(2,1)S(1)} %get-tuple-element.93), channel_id=1, source_target_pairs={{0,9},{1,8},{2,11},{3,10},{4,13},{5,12},{6,15},{7,14},{8,1},{9,0},... | collective-permute-start | bytes 196616 | tf_op jit(solution)/shard_map/ppermute | solution.py:592
  34.3 5.8 %collective-permute-start.15 = (bf16[256,128]{1,0:T(8,128)(2,1)S(1)}, bf16[256,128]{1,0:T(8,128)(2,1)S(1)}, u32[]{:S(2)}, u32[]{:S(2)}) collective-permute-start(bf16[256,128]{1,0:T(8,128)(2,1)S(1)} %get-tuple-element.94), channel_id=1, source_target_pairs={{0,8},{8,0},{16,24},{24,16},{1,9},{9,1},{17,25},{25,17},{2,10},{10... | collective-permute-start | bytes 196616 | tf_op jit(solution)/shard_map/ppermute | solution.py:562
  35.9 4.1 %collective-permute-start.16 = (bf16[256,128]{1,0:T(8,128)(2,1)S(1)}, bf16[256,128]{1,0:T(8,128)(2,1)S(1)}, u32[]{:S(2)}, u32[]{:S(2)}) collective-permute-start(bf16[256,128]{1,0:T(8,128)(2,1)S(1)} %get-tuple-element.95), channel_id=1, source_target_pairs={{0,1},{1,0},{2,3},{3,2},{4,5},{5,4},{6,7},{7,6},{8,9},{9,8},{10,11... | collective-permute-start | bytes 196616 | tf_op jit(solution)/shard_map/ppermute | solution.py:14
  (1 other events, 2.7 us)

commit v8 on v7

--- a/solution.py
+++ b/solution.py
@@ -140,7 +140,7 @@
 VMEM_LIMIT = 16 * 2**20
 COL_MICROS = 28
 FIRST_ORDER = (1, 2, 3)
-BACK_ORDER = (2, 1, 3)
+BACK_ORDER = (1, 2, 3)
 COL_APART = (2, 1)
 ROW_APART = (2, 1)
 

time: 41.2 us -> 41 us (level)
  transfers between devices with their start and end apart: 17 -> 17, of which waited for: 12 -> 10; matrix products, arithmetic and copies ran while one was open for 0% -> 0% of each run, Pallas kernels for 20% -> 20%
where the time goes in v8:
time: 41 us; the launch traced here: 40.8 us
  starting transfers between devices  18.2 us (44%)
  waiting for transfers between devices  11.3 us (28%)
  Pallas kernels  10.5 us (26%)
  between operations  0.77 us (2%)
    pallas_call x14, Pallas kernels, call(): pl.pallas_call(body, out_shape=outs, in_specs=[whole] * len(args), out_sp...  10.5 us
    ppermute x4, starting transfers between devices, over_dp(): return lax.ppermute(value, 'dp', [(s, s ^ apart) for s in range(dps)])  8.85 us
    ppermute x6, starting transfers between devices, exchange(): return [bufs[0]] + [lax.ppermute(bufs[q], axis, pairs[q]) for q in order]  8.02 us
    ppermute x6, waiting for transfers between devices, exchange(): return [bufs[0]] + [lax.ppermute(bufs[q], axis, pairs[q]) for q in order]  6.72 us
    ppermute x6, waiting for transfers between devices, from_partner(): return lax.ppermute(value, axis, pairs)  2.69 us
    ppermute x4, waiting for transfers between devices, over_dp(): return lax.ppermute(value, 'dp', [(s, s ^ apart) for s in range(dps)])  1.9 us
    ppermute x6, starting transfers between devices, from_partner(): return lax.ppermute(value, axis, pairs)  1.23 us
  transfers between devices with their start and end apart: 17, of which 10 were waited for; matrix products, arithmetic and copies ran while one was open for 0% of the time, Pallas kernels for 20%

profile of v8, /device:TPU:0, one launch (start us, length us, event | category | flops | bytes accessed | tf_op | source)
XLA Modules:
  0.0 40.8 jit_solution(13934671788706834546)
XLA Ops:
  1.7 0.6 %collective-permute-done.refs_3_ = bf16[256,128]{1,0:T(8,128)(2,1)S(1)} collective-permute-done((bf16[256,128]{1,0:T(8,128)(2,1)}, bf16[256,128]{1,0:T(8,128)(2,1)S(1)}, u32[]{:S(2)}, u32[]{:S(2)}) %collective-permute-start) | collective-permute-done | bytes 65568 | tf_op jit(solution)/shard_map/ppermute | solution.py:14
  2.9 1.2 %collective-permute-done.3.refs_1_.other_ref = bf16[1024,512]{1,0:T(8,128)(2,1)S(1)} collective-permute-done((bf16[1024,512]{1,0:T(8,128)(2,1)}, bf16[1024,512]{1,0:T(8,128)(2,1)S(1)}, u32[]{:S(2)}, u32[]{:S(2)}) %collective-permute-start.3) | collective-permute-done | bytes 1048608 | tf_op jit(solution)/shard_map/ppermute | solution.py:14
  4.2 0.9 %shard_map.128 = (bf16[64,512]{1,0:T(8,128)(2,1)S(1)}, bf16[64,512]{1,0:T(8,128)(2,1)S(1)}, bf16[64,512]{1,0:T(8,128)(2,1)S(1)}, bf16[64,512]{1,0:T(8,128)(2,1)S...) custom-call(bf16[1024,512]{1,0:T(8,128)(2,1)S(1)} %copy-done.1, ...), custom_call_target="tpu_custom_call" | custom-call | flops 10000000 | bytes 30000 | tf_op jit(solution)/shard_map/pallas_call | solution.py:156
  6.3 2.9 %collective-permute-start.4 = (bf16[128,512]{1,0:T(8,128)(2,1)S(1)}, bf16[128,512]{1,0:T(8,128)(2,1)S(1)}, u32[]{:S(2)}, u32[]{:S(2)}) collective-permute-start(bf16[128,512]{1,0:T(8,128)(2,1)S(1)} %get-tuple-element.65), channel_id=1, source_target_pairs={{0,2},{1,3},{2,0},{3,1},{4,6},{5,7},{6,4},{7,5},{8,10},{9,11},{10,... | collective-permute-start | bytes 393224 | tf_op jit(solution)/shard_map/ppermute | solution.py:465
  9.2 1.5 %collective-permute-start.5 = (bf16[128,512]{1,0:T(8,128)(2,1)S(1)}, bf16[128,512]{1,0:T(8,128)(2,1)S(1)}, u32[]{:S(2)}, u32[]{:S(2)}) collective-permute-start(bf16[128,512]{1,0:T(8,128)(2,1)S(1)} %get-tuple-element.66), channel_id=1, source_target_pairs={{0,4},{1,5},{2,6},{3,7},{4,0},{5,1},{6,2},{7,3},{8,12},{9,13},{10,... | collective-permute-start | bytes 393224 | tf_op jit(solution)/shard_map/ppermute | solution.py:465
  11.1 0.7 %shard_map.131.refs_8_.refs_4_ = bf16[512,2048]{1,0:T(8,128)(2,1)S(1)} custom-call(bf16[1024,512]{1,0:T(8,128)(2,1)S(1)} %copy-done.1, bf16[1024,512]{1,0:T(8,128)(2,1)S(1)} %collective-permute-done.3.refs_1_.other_ref, bf16[128,512]{1,0:T(8,128)(2,1)S(1)} %get-tuple-element.64._.refs_0_), custom_call_target="tpu_custom_call" | custom-call | flops 1000000000 | bytes 3000000 | tf_op jit(solution)/shard_map/pallas_call | solution.py:156
  11.8 0.7 %shard_map.132.refs_9_.refs_5_ = bf16[512,2048]{1,0:T(8,128)(2,1)S(1)} custom-call(bf16[1024,512]{1,0:T(8,128)(2,1)S(1)} %copy-done, bf16[1024,512]{1,0:T(8,128)(2,1)S(1)} %collective-permute-done.2.refs_1_.other_ref, bf16[128,512]{1,0:T(8,128)(2,1)S(1)} %get-tuple-element.64._.refs_0_), custom_call_target="tpu_custom_call" | custom-call | flops 1000000000 | bytes 3000000 | tf_op jit(solution)/shard_map/pallas_call | solution.py:156
  13.1 4.2 %collective-permute-done.5.refs_2_ = bf16[128,512]{1,0:T(8,128)(2,1)S(1)} collective-permute-done((bf16[128,512]{1,0:T(8,128)(2,1)S(1)}, bf16[128,512]{1,0:T(8,128)(2,1)S(1)}, u32[]{:S(2)}, u32[]{:S(2)}) %collective-permute-start.5) | collective-permute-done | bytes 131104 | tf_op jit(solution)/shard_map/ppermute | solution.py:465
  17.2 1.0 %shard_map.133 = (bf16[128,512]{1,0:T(8,128)(2,1)S(1)}, bf16[128,512]{1,0:T(8,128)(2,1)S(1)}, bf16[128,512]{1,0:T(8,128)(2,1)S(1)}, bf16[128,512]{1,0:T(8,128)(2...) custom-call(bf16[128,512]{1,0:T(8,128)(2,1)S(1)} %get-tuple-element.64._.refs_0_, ...), custom_call_target="tpu_custom_call" | custom-call | flops 10000000 | bytes 30000 | tf_op jit(solution)/shard_map/pallas_call | solution.py:156
  18.3 1.3 %collective-permute-start.7 = (bf16[128,512]{1,0:T(8,128)(2,1)S(1)}, bf16[128,512]{1,0:T(8,128)(2,1)S(1)}, u32[]{:S(2)}, u32[]{:S(2)}) collective-permute-start(bf16[128,512]{1,0:T(8,128)(2,1)S(1)} %get-tuple-element.73), channel_id=1, source_target_pairs={{0,2},{1,3},{2,0},{3,1},{4,6},{5,7},{6,4},{7,5},{8,10},{9,11},{10,... | collective-permute-start | bytes 393224 | tf_op jit(solution)/shard_map/ppermute | solution.py:465
  19.6 0.8 %collective-permute-start.8 = (bf16[128,512]{1,0:T(8,128)(2,1)S(1)}, bf16[128,512]{1,0:T(8,128)(2,1)S(1)}, u32[]{:S(2)}, u32[]{:S(2)}) collective-permute-start(bf16[128,512]{1,0:T(8,128)(2,1)S(1)} %get-tuple-element.74), channel_id=1, source_target_pairs={{0,4},{1,5},{2,6},{3,7},{4,0},{5,1},{6,2},{7,3},{8,12},{9,13},{10,... | collective-permute-start | bytes 393224 | tf_op jit(solution)/shard_map/ppermute | solution.py:465
  20.4 1.4 %collective-permute-start.9 = (bf16[128,512]{1,0:T(8,128)(2,1)S(1)}, bf16[128,512]{1,0:T(8,128)(2,1)S(1)}, u32[]{:S(2)}, u32[]{:S(2)}) collective-permute-start(bf16[128,512]{1,0:T(8,128)(2,1)S(1)} %get-tuple-element.75), channel_id=1, source_target_pairs={{0,6},{1,7},{2,4},{3,5},{4,2},{5,3},{6,0},{7,1},{8,14},{9,15},{10,... | collective-permute-start | bytes 393224 | tf_op jit(solution)/shard_map/ppermute | solution.py:465
  22.1 2.7 %collective-permute-start.10 = (bf16[512,128]{1,0:T(8,128)(2,1)S(1)}, bf16[512,128]{1,0:T(8,128)(2,1)S(1)}, u32[]{:S(2)}, u32[]{:S(2)}) collective-permute-start(bf16[512,128]{1,0:T(8,128)(2,1)S(1)} %shard_map.134.refs_7_.refs_6_), channel_id=1, source_target_pairs={{0,16},{8,24},{16,0},{24,8},{1,17},{9,25},{17,1},{25,9},{2,18},{10... | collective-permute-start | bytes 393224 | tf_op jit(solution)/shard_map/ppermute | solution.py:562
  24.8 2.0 %collective-permute-done.8.refs_2_ = bf16[128,512]{1,0:T(8,128)(2,1)S(1)} collective-permute-done((bf16[128,512]{1,0:T(8,128)(2,1)S(1)}, bf16[128,512]{1,0:T(8,128)(2,1)S(1)}, u32[]{:S(2)}, u32[]{:S(2)}) %collective-permute-start.8) | collective-permute-done | bytes 131104 | tf_op jit(solution)/shard_map/ppermute | solution.py:465
  26.8 1.1 %shard_map.135 = (bf16[512,128]{1,0:T(8,128)(2,1)S(1)}, bf16[256,512]{1,0:T(8,128)(2,1)S(1)}, bf16[256,512]{1,0:T(8,128)(2,1)S(1)}) custom-call(bf16[128,512]{1,0:T(8,128)(2,1)S(1)} %get-tuple-element.72.refs_0_, bf16[128,512]{1,0:T(8,128)(2,1)S(1)} %collective-permute-done.7.refs_1_, bf16[128,512]{1,0:T(8,128)(2,1)S(1)} %collective-permute-done.8.refs_2_, ...), custom_call_target="tpu_custom_call" | custom-call | flops 10000000 | bytes 30000 | tf_op jit(solution)/shard_map/pallas_call | solution.py:156
  27.9 2.7 %collective-permute-start.13 = (bf16[512,128]{1,0:T(8,128)(2,1)S(1)}, bf16[512,128]{1,0:T(8,128)(2,1)S(1)}, u32[]{:S(2)}, u32[]{:S(2)}) collective-permute-start(bf16[512,128]{1,0:T(8,128)(2,1)S(1)} %get-tuple-element.91.left_ref), channel_id=1, source_target_pairs={{0,16},{8,24},{16,0},{24,8},{1,17},{9,25},{17,1},{25,9},{2,18},{10... | collective-permute-start | bytes 393224 | tf_op jit(solution)/shard_map/ppermute | solution.py:562
  30.5 1.3 %shard_map.136 = (f32[1024,512]{1,0:T(8,128)S(1)}, f32[1024,512]{1,0:T(8,128)S(1)}, bf16[2048,512]{1,0:T(8,128)(2,1)S(1)}, bf16[512,128]{1,0:T(8,128)(2,1)S(1)}) custom-call(bf16[256,512]{1,0:T(8,128)(2,1)S(1)} %get-tuple-element.79.refs_0_, bf16[1024,512]{1,0:T(8,128)(2,1)S(1)} %copy-done.1, bf16[256,128]{1,0:T(8,128)(2,1)S(1)} %get-tuple-element.59.refs_2_, ...), custom_call_target="tpu_custom_call" | custom-call | flops 10000000 | bytes 30000 | tf_op jit(solution)/shard_map/pallas_call | solution.py:156
  31.8 1.7 %collective-permute-start.12 = (bf16[512,128]{1,0:T(8,128)(2,1)S(1)}, bf16[512,128]{1,0:T(8,128)(2,1)S(1)}, u32[]{:S(2)}, u32[]{:S(2)}) collective-permute-start(bf16[512,128]{1,0:T(8,128)(2,1)S(1)} %get-tuple-element.85.sum_ref), channel_id=1, source_target_pairs={{0,8},{8,0},{16,24},{24,16},{1,9},{9,1},{17,25},{25,17},{2,10},{10... | collective-permute-start | bytes 393224 | tf_op jit(solution)/shard_map/ppermute | solution.py:562
  33.4 0.7 %collective-permute-done.13.right_ref = bf16[512,128]{1,0:T(8,128)(2,1)S(1)} collective-permute-done((bf16[512,128]{1,0:T(8,128)(2,1)S(1)}, bf16[512,128]{1,0:T(8,128)(2,1)S(1)}, u32[]{:S(2)}, u32[]{:S(2)}) %collective-permute-start.13) | collective-permute-done | bytes 131104 | tf_op jit(solution)/shard_map/ppermute | solution.py:562
  34.2 1.9 %collective-permute-start.15 = (bf16[256,128]{1,0:T(8,128)(2,1)S(1)}, bf16[256,128]{1,0:T(8,128)(2,1)S(1)}, u32[]{:S(2)}, u32[]{:S(2)}) collective-permute-start(bf16[256,128]{1,0:T(8,128)(2,1)S(1)} %get-tuple-element.94), channel_id=1, source_target_pairs={{0,8},{8,0},{16,24},{24,16},{1,9},{9,1},{17,25},{25,17},{2,10},{10... | collective-permute-start | bytes 196616 | tf_op jit(solution)/shard_map/ppermute | solution.py:562
  36.2 0.7 %collective-permute-done.12.got_ref = bf16[512,128]{1,0:T(8,128)(2,1)S(1)} collective-permute-done((bf16[512,128]{1,0:T(8,128)(2,1)S(1)}, bf16[512,128]{1,0:T(8,128)(2,1)S(1)}, u32[]{:S(2)}, u32[]{:S(2)}) %collective-permute-start.12) | collective-permute-done | bytes 131104 | tf_op jit(solution)/shard_map/ppermute | solution.py:562
  36.8 0.9 %shard_map.137 = (f32[256,128]{1,0:T(8,128)}, f32[256,128]{1,0:T(8,128)}, f32[8,128]{1,0:T(8,128)S(1)}) custom-call(bf16[512,128]{1,0:T(8,128)(2,1)S(1)} %get-tuple-element.85.sum_ref, bf16[512,128]{1,0:T(8,128)(2,1)S(1)} %collective-permute-done.12.got_ref, bf16[128,128]{1,0:T(8,128)(2,1)S(1)} %get-tuple-element.86.take_up_ref, ...), custom_call_target="tpu_custom_call" | custom-call | flops 28000000000 | bytes 84000000 | tf_op jit(solution)/shard_map/pallas_call | solution.py:156
  37.7 1.6 %shard_map.138 = (bf16[1024,512]{1,0:T(8,128)(2,1)}, bf16[1024,512]{1,0:T(8,128)(2,1)}, f32[8,128]{1,0:T(8,128)S(1)}) custom-call(f32[1024,512]{1,0:T(8,128)S(1)} %get-tuple-element.82.mixed_ref, f32[1024,512]{1,0:T(8,128)S(1)} %get-tuple-element.83.grad_ref, bf16[2048,512]{1,0:T(8,128)(2,1)S(1)} %collective-permute-done.11.got_ref, ...), custom_call_target="tpu_custom_call" | custom-call | flops 10000000 | bytes 30000 | tf_op jit(solution)/shard_map/pallas_call | solution.py:156
  39.9 1.0 %shard_map.140 = (f32[256,128]{1,0:T(8,128)}, f32[256,128]{1,0:T(8,128)}) custom-call(bf16[256,128]{1,0:T(8,128)(2,1)S(1)} %get-tuple-element.92.refs_0_, bf16[256,128]{1,0:T(8,128)(2,1)S(1)} %collective-permute-done.14.refs_1_, bf16[256,128]{1,0:T(8,128)(2,1)S(1)} %collective-permute-done.15.refs_2_, bf16[256,128]{1,0:T(8,128)(2,1)S(1)} %collective-permute-done.16.refs_3_, ...), custom_call_target="tpu_custom_call" | custom-call | flops 10000000 | bytes 30000 | tf_op jit(solution)/shard_map/pallas_call | solution.py:156
  (40 shorter events, 4.8 us)
Async XLA Ops:
  0.6 1.6 %collective-permute-start = (bf16[256,128]{1,0:T(8,128)(2,1)}, bf16[256,128]{1,0:T(8,128)(2,1)S(1)}, u32[]{:S(2)}, u32[]{:S(2)}) collective-permute-start(bf16[256,128]{1,0:T(8,128)(2,1)} %bitcast.10), channel_id=1, source_target_pairs={{0,1},{1,0},{2,3},{3,2},{4,5},{5,4},{6,7},{7,6},{8,9},{9,8},{10,11... | collective-permute-start | bytes 196616 | tf_op jit(solution)/shard_map/ppermute | solution.py:14
  1.1 3.0 %copy-start.1 = (bf16[1024,512]{1,0:T(8,128)(2,1)S(1)}, bf16[1024,512]{1,0:T(8,128)(2,1)}, u32[]{:S(2)}) copy-start(bf16[1024,512]{1,0:T(8,128)(2,1)} %refs_1_.1) | copy-start | bytes 3145732
  1.2 3.0 %copy-start.2 = (bf16[16,16,128]{2,1,0:T(8,128)(2,1)S(1)}, bf16[16,16,128]{2,1,0:T(8,128)(2,1)}, u32[]{:S(2)}) copy-start(bf16[16,16,128]{2,1,0:T(8,128)(2,1)} %param.10) | copy-start | bytes 196612
  1.2 3.0 %copy-start.3 = (bf16[16,16,128]{2,1,0:T(8,128)(2,1)S(1)}, bf16[16,16,128]{2,1,0:T(8,128)(2,1)}, u32[]{:S(2)}) copy-start(bf16[16,16,128]{2,1,0:T(8,128)(2,1)} %param.13) | copy-start | bytes 196612
  1.2 1.5 %collective-permute-start.1 = (bf16[256,128]{1,0:T(8,128)(2,1)}, bf16[256,128]{1,0:T(8,128)(2,1)S(1)}, u32[]{:S(2)}, u32[]{:S(2)}) collective-permute-start(bf16[256,128]{1,0:T(8,128)(2,1)} %bitcast.12), channel_id=1, source_target_pairs={{0,1},{1,0},{2,3},{3,2},{4,5},{5,4},{6,7},{7,6},{8,9},{9,8},{10,11... | collective-permute-start | bytes 196616 | tf_op jit(solution)/shard_map/ppermute | solution.py:14
  1.3 2.9 %collective-permute-start.3 = (bf16[1024,512]{1,0:T(8,128)(2,1)}, bf16[1024,512]{1,0:T(8,128)(2,1)S(1)}, u32[]{:S(2)}, u32[]{:S(2)}) collective-permute-start(bf16[1024,512]{1,0:T(8,128)(2,1)} %refs_1_.1), channel_id=1, source_target_pairs={{0,1},{1,0},{2,3},{3,2},{4,5},{5,4},{6,7},{7,6},{8,9},{9,8},{10,11... | collective-permute-start | bytes 3145736 | tf_op jit(solution)/shard_map/ppermute | solution.py:14
  2.6 3.0 %collective-permute-start.2 = (bf16[1024,512]{1,0:T(8,128)(2,1)}, bf16[1024,512]{1,0:T(8,128)(2,1)S(1)}, u32[]{:S(2)}, u32[]{:S(2)}) collective-permute-start(bf16[1024,512]{1,0:T(8,128)(2,1)} %refs_4_.1), channel_id=1, source_target_pairs={{0,1},{1,0},{2,3},{3,2},{4,5},{5,4},{6,7},{7,6},{8,9},{9,8},{10,11... | collective-permute-start | bytes 3145736 | tf_op jit(solution)/shard_map/ppermute | solution.py:14
  4.2 6.6 %copy-start.4 = (bf16[2,128,128]{2,1,0:T(8,128)(2,1)S(1)}, bf16[2,128,128]{2,1,0:T(8,128)(2,1)}, u32[]{:S(2)}) copy-start(bf16[2,128,128]{2,1,0:T(8,128)(2,1)} %param.11) | copy-start | bytes 196612
  4.2 6.5 %copy-start.5 = (bf16[2,128,128]{2,1,0:T(8,128)(2,1)S(1)}, bf16[2,128,128]{2,1,0:T(8,128)(2,1)}, u32[]{:S(2)}) copy-start(bf16[2,128,128]{2,1,0:T(8,128)(2,1)} %param.12) | copy-start | bytes 196612
  4.2 6.5 %copy-start.6 = (s32[128]{0:T(128)S(1)}, s32[128]{0:T(128)}, u32[]{:S(2)}) copy-start(s32[128]{0:T(128)} %param.14) | copy-start | bytes 1540
  4.2 6.5 %copy-start.7 = (s32[128]{0:T(128)S(1)}, s32[128]{0:T(128)}, u32[]{:S(2)}) copy-start(s32[128]{0:T(128)} %param.15) | copy-start | bytes 1540
  6.3 6.8 %collective-permute-start.4 = (bf16[128,512]{1,0:T(8,128)(2,1)S(1)}, bf16[128,512]{1,0:T(8,128)(2,1)S(1)}, u32[]{:S(2)}, u32[]{:S(2)}) collective-permute-start(bf16[128,512]{1,0:T(8,128)(2,1)S(1)} %get-tuple-element.65), channel_id=1, source_target_pairs={{0,2},{1,3},{2,0},{3,1},{4,6},{5,7},{6,4},{7,5},{8,10},{9,11},{10,... | collective-permute-start | bytes 393224 | tf_op jit(solution)/shard_map/ppermute | solution.py:465
  9.2 8.1 %collective-permute-start.5 = (bf16[128,512]{1,0:T(8,128)(2,1)S(1)}, bf16[128,512]{1,0:T(8,128)(2,1)S(1)}, u32[]{:S(2)}, u32[]{:S(2)}) collective-permute-start(bf16[128,512]{1,0:T(8,128)(2,1)S(1)} %get-tuple-element.66), channel_id=1, source_target_pairs={{0,4},{1,5},{2,6},{3,7},{4,0},{5,1},{6,2},{7,3},{8,12},{9,13},{10,... | collective-permute-start | bytes 393224 | tf_op jit(solution)/shard_map/ppermute | solution.py:465
  10.7 6.5 %collective-permute-start.6 = (bf16[128,512]{1,0:T(8,128)(2,1)S(1)}, bf16[128,512]{1,0:T(8,128)(2,1)S(1)}, u32[]{:S(2)}, u32[]{:S(2)}) collective-permute-start(bf16[128,512]{1,0:T(8,128)(2,1)S(1)} %get-tuple-element.67), channel_id=1, source_target_pairs={{0,6},{1,7},{2,4},{3,5},{4,2},{5,3},{6,0},{7,1},{8,14},{9,15},{10,... | collective-permute-start | bytes 393224 | tf_op jit(solution)/shard_map/ppermute | solution.py:465
  18.3 6.5 %collective-permute-start.7 = (bf16[128,512]{1,0:T(8,128)(2,1)S(1)}, bf16[128,512]{1,0:T(8,128)(2,1)S(1)}, u32[]{:S(2)}, u32[]{:S(2)}) collective-permute-start(bf16[128,512]{1,0:T(8,128)(2,1)S(1)} %get-tuple-element.73), channel_id=1, source_target_pairs={{0,2},{1,3},{2,0},{3,1},{4,6},{5,7},{6,4},{7,5},{8,10},{9,11},{10,... | collective-permute-start | bytes 393224 | tf_op jit(solution)/shard_map/ppermute | solution.py:465
  19.6 7.2 %collective-permute-start.8 = (bf16[128,512]{1,0:T(8,128)(2,1)S(1)}, bf16[128,512]{1,0:T(8,128)(2,1)S(1)}, u32[]{:S(2)}, u32[]{:S(2)}) collective-permute-start(bf16[128,512]{1,0:T(8,128)(2,1)S(1)} %get-tuple-element.74), channel_id=1, source_target_pairs={{0,4},{1,5},{2,6},{3,7},{4,0},{5,1},{6,2},{7,3},{8,12},{9,13},{10,... | collective-permute-start | bytes 393224 | tf_op jit(solution)/shard_map/ppermute | solution.py:465
  20.4 6.4 %collective-permute-start.9 = (bf16[128,512]{1,0:T(8,128)(2,1)S(1)}, bf16[128,512]{1,0:T(8,128)(2,1)S(1)}, u32[]{:S(2)}, u32[]{:S(2)}) collective-permute-start(bf16[128,512]{1,0:T(8,128)(2,1)S(1)} %get-tuple-element.75), channel_id=1, source_target_pairs={{0,6},{1,7},{2,4},{3,5},{4,2},{5,3},{6,0},{7,1},{8,14},{9,15},{10,... | collective-permute-start | bytes 393224 | tf_op jit(solution)/shard_map/ppermute | solution.py:465
  22.1 8.4 %collective-permute-start.10 = (bf16[512,128]{1,0:T(8,128)(2,1)S(1)}, bf16[512,128]{1,0:T(8,128)(2,1)S(1)}, u32[]{:S(2)}, u32[]{:S(2)}) collective-permute-start(bf16[512,128]{1,0:T(8,128)(2,1)S(1)} %shard_map.134.refs_7_.refs_6_), channel_id=1, source_target_pairs={{0,16},{8,24},{16,0},{24,8},{1,17},{9,25},{17,1},{25,9},{2,18},{10... | collective-permute-start | bytes 393224 | tf_op jit(solution)/shard_map/ppermute | solution.py:562
  27.9 6.3 %collective-permute-start.13 = (bf16[512,128]{1,0:T(8,128)(2,1)S(1)}, bf16[512,128]{1,0:T(8,128)(2,1)S(1)}, u32[]{:S(2)}, u32[]{:S(2)}) collective-permute-start(bf16[512,128]{1,0:T(8,128)(2,1)S(1)} %get-tuple-element.91.left_ref), channel_id=1, source_target_pairs={{0,16},{8,24},{16,0},{24,8},{1,17},{9,25},{17,1},{25,9},{2,18},{10... | collective-permute-start | bytes 393224 | tf_op jit(solution)/shard_map/ppermute | solution.py:562
  31.8 5.0 %collective-permute-start.12 = (bf16[512,128]{1,0:T(8,128)(2,1)S(1)}, bf16[512,128]{1,0:T(8,128)(2,1)S(1)}, u32[]{:S(2)}, u32[]{:S(2)}) collective-permute-start(bf16[512,128]{1,0:T(8,128)(2,1)S(1)} %get-tuple-element.85.sum_ref), channel_id=1, source_target_pairs={{0,8},{8,0},{16,24},{24,16},{1,9},{9,1},{17,25},{25,17},{2,10},{10... | collective-permute-start | bytes 393224 | tf_op jit(solution)/shard_map/ppermute | solution.py:562
  33.4 4.3 %collective-permute-start.11 = (bf16[2048,512]{1,0:T(8,128)(2,1)S(1)}, bf16[2048,512]{1,0:T(8,128)(2,1)S(1)}, u32[]{:S(2)}, u32[]{:S(2)}) collective-permute-start(bf16[2048,512]{1,0:T(8,128)(2,1)S(1)} %get-tuple-element.84), channel_id=1, source_target_pairs={{0,1},{1,0},{2,3},{3,2},{4,5},{5,4},{6,7},{7,6},{8,9},{9,8},{10,11... | collective-permute-start | bytes 6291464 | tf_op jit(solution)/shard_map/ppermute | solution.py:14
  34.2 5.2 %collective-permute-start.14 = (bf16[256,128]{1,0:T(8,128)(2,1)S(1)}, bf16[256,128]{1,0:T(8,128)(2,1)S(1)}, u32[]{:S(2)}, u32[]{:S(2)}) collective-permute-start(bf16[256,128]{1,0:T(8,128)(2,1)S(1)} %get-tuple-element.93), channel_id=1, source_target_pairs={{0,9},{1,8},{2,11},{3,10},{4,13},{5,12},{6,15},{7,14},{8,1},{9,0},... | collective-permute-start | bytes 196616 | tf_op jit(solution)/shard_map/ppermute | solution.py:592
  34.2 5.6 %collective-permute-start.15 = (bf16[256,128]{1,0:T(8,128)(2,1)S(1)}, bf16[256,128]{1,0:T(8,128)(2,1)S(1)}, u32[]{:S(2)}, u32[]{:S(2)}) collective-permute-start(bf16[256,128]{1,0:T(8,128)(2,1)S(1)} %get-tuple-element.94), channel_id=1, source_target_pairs={{0,8},{8,0},{16,24},{24,16},{1,9},{9,1},{17,25},{25,17},{2,10},{10... | collective-permute-start | bytes 196616 | tf_op jit(solution)/shard_map/ppermute | solution.py:562
  36.1 3.8 %collective-permute-start.16 = (bf16[256,128]{1,0:T(8,128)(2,1)S(1)}, bf16[256,128]{1,0:T(8,128)(2,1)S(1)}, u32[]{:S(2)}, u32[]{:S(2)}) collective-permute-start(bf16[256,128]{1,0:T(8,128)(2,1)S(1)} %get-tuple-element.95), channel_id=1, source_target_pairs={{0,1},{1,0},{2,3},{3,2},{4,5},{5,4},{6,7},{7,6},{8,9},{9,8},{10,11... | collective-permute-start | bytes 196616 | tf_op jit(solution)/shard_map/ppermute | solution.py:14
  (1 other events, 2.7 us)

commit v9 on v8

--- a/solution.py
+++ b/solution.py
@@ -431,15 +431,24 @@
             out[...] = total.astype(out.dtype)
 
 
+def place_parts(near_ref, far_ref, place_ref, at):
+    size = near_ref.shape[0] // 2
+    span = slice(at * size, (at + 1) * size)
+    return dot(place_ref[...], jnp.concatenate([near_ref[span, :], far_ref[span, :]], 0))
+
+
+def chip_grads(near_ref, far_ref, place_ref, out_ref):
+    size = out_ref.shape[0] // 2
+    for at in range(2):
+        out_ref[at * size : (at + 1) * size, :] = place_parts(near_ref, far_ref, place_ref, at)
+
+
 def total_grads(scale):
-    def body(*refs):
-        parts, place_ref, outs = [refs[at] for at in (0, 2, 1, 3)], refs[4], refs[-2:]
-        size = parts[0].shape[0] // 2
-        near, far = place_ref[:, :size], place_ref[:, size:]
-        place = jnp.concatenate([near, near, far, far], 1)
+    def body(chip_ref, near_ref, far_ref, place_ref, _, *outs):
+        size = outs[0].shape[0]
         for at, out in enumerate(outs):
-            span = slice(at * size, (at + 1) * size)
-            out[...] = dot(place, jnp.concatenate([r[span, :] for r in parts], 0)) * scale
+            chip = chip_ref[at * size : (at + 1) * size, :]
+            out[...] = (chip + place_parts(near_ref, far_ref, place_ref, at)) * scale
 
     return body
 
@@ -595,7 +604,9 @@
     got['c'] = to_partner(to_other, ROW_APART[1])
     got['z'] = over_dp(to_next, ROW_APART[1])
     got['p'] = from_partner(to_core, "loop", 0)
-    parts = (kept, got['c'], got['z'], got['p'])
+    (chip,) = call(
+        chip_grads, [struct(2 * rows * all_cols, block, wide)], kept, got['p'], place
+    )
     scale = 1.0 / math.sqrt(dps * toks)
     token = struct(8, 128, wide)
     g_up_second, g_down_first, done = call(
@@ -620,7 +631,9 @@
     g_up_first, g_down_second = call(
         total_grads(scale),
         [struct(rows * all_cols, block, wide)] * 2,
-        *parts,
+        chip,
+        got['z'],
+        got['c'],
         place,
         done,
         to_hbm=2,

time: 41 us -> 41.2 us (level)
    ppermute x1, waiting for transfers between devices: 0.01 us -> 0.6 us  [to_partner(): return lax.ppermute(value, ('dp', 'loop'), pairs)]
    ppermute x4, waiting for transfers between devices: 1.9 us -> 1.32 us  [over_dp(): return lax.ppermute(value, 'dp', [(s, s ^ apart) for s in range(dps)])]
    pallas_call x14 -> x15, Pallas kernels: 10.5 us -> 10.7 us  [call(): pl.pallas_call(body, out_shape=outs, in_specs=[whole] * len(args), out_sp...]
where the time goes in v9:
time: 41.2 us; the launch traced here: 41.1 us
  starting transfers between devices  18.2 us (44%)
  waiting for transfers between devices  11.3 us (27%)
  Pallas kernels  10.7 us (26%)
  between operations  0.78 us (2%)
    pallas_call x15, Pallas kernels, call(): pl.pallas_call(body, out_shape=outs, in_specs=[whole] * len(args), out_sp...  10.7 us
    ppermute x4, starting transfers between devices, over_dp(): return lax.ppermute(value, 'dp', [(s, s ^ apart) for s in range(dps)])  8.85 us
    ppermute x6, starting transfers between devices, exchange(): return [bufs[0]] + [lax.ppermute(bufs[q], axis, pairs[q]) for q in order]  8.02 us
    ppermute x6, waiting for transfers between devices, exchange(): return [bufs[0]] + [lax.ppermute(bufs[q], axis, pairs[q]) for q in order]  6.72 us
    ppermute x6, waiting for transfers between devices, from_partner(): return lax.ppermute(value, axis, pairs)  2.69 us
    ppermute x4, waiting for transfers between devices, over_dp(): return lax.ppermute(value, 'dp', [(s, s ^ apart) for s in range(dps)])  1.32 us
    ppermute x6, starting transfers between devices, from_partner(): return lax.ppermute(value, axis, pairs)  1.26 us
  transfers between devices with their start and end apart: 17, of which 10 were waited for; matrix products, arithmetic and copies ran while one was open for 0% of the time, Pallas kernels for 20%

profile of v9, /device:TPU:0, one launch (start us, length us, event | category | flops | bytes accessed | tf_op | source)
XLA Modules:
  0.0 41.1 jit_solution(14167680826875154770)
XLA Ops:
  2.9 1.2 %collective-permute-done.3.refs_1_.other_ref = bf16[1024,512]{1,0:T(8,128)(2,1)S(1)} collective-permute-done((bf16[1024,512]{1,0:T(8,128)(2,1)}, bf16[1024,512]{1,0:T(8,128)(2,1)S(1)}, u32[]{:S(2)}, u32[]{:S(2)}) %collective-permute-start.3) | collective-permute-done | bytes 1048608 | tf_op jit(solution)/shard_map/ppermute | solution.py:14
  4.2 0.9 %shard_map.128 = (bf16[64,512]{1,0:T(8,128)(2,1)S(1)}, bf16[64,512]{1,0:T(8,128)(2,1)S(1)}, bf16[64,512]{1,0:T(8,128)(2,1)S(1)}, bf16[64,512]{1,0:T(8,128)(2,1)S...) custom-call(bf16[1024,512]{1,0:T(8,128)(2,1)S(1)} %copy-done.1, ...), custom_call_target="tpu_custom_call" | custom-call | flops 10000000 | bytes 30000 | tf_op jit(solution)/shard_map/pallas_call | solution.py:156
  6.3 2.9 %collective-permute-start.4 = (bf16[128,512]{1,0:T(8,128)(2,1)S(1)}, bf16[128,512]{1,0:T(8,128)(2,1)S(1)}, u32[]{:S(2)}, u32[]{:S(2)}) collective-permute-start(bf16[128,512]{1,0:T(8,128)(2,1)S(1)} %get-tuple-element.65), channel_id=1, source_target_pairs={{0,2},{1,3},{2,0},{3,1},{4,6},{5,7},{6,4},{7,5},{8,10},{9,11},{10,... | collective-permute-start | bytes 393224 | tf_op jit(solution)/shard_map/ppermute | solution.py:474
  9.2 1.5 %collective-permute-start.5 = (bf16[128,512]{1,0:T(8,128)(2,1)S(1)}, bf16[128,512]{1,0:T(8,128)(2,1)S(1)}, u32[]{:S(2)}, u32[]{:S(2)}) collective-permute-start(bf16[128,512]{1,0:T(8,128)(2,1)S(1)} %get-tuple-element.66), channel_id=1, source_target_pairs={{0,4},{1,5},{2,6},{3,7},{4,0},{5,1},{6,2},{7,3},{8,12},{9,13},{10,... | collective-permute-start | bytes 393224 | tf_op jit(solution)/shard_map/ppermute | solution.py:474
  11.1 0.7 %shard_map.131.refs_8_.refs_4_ = bf16[512,2048]{1,0:T(8,128)(2,1)S(1)} custom-call(bf16[1024,512]{1,0:T(8,128)(2,1)S(1)} %copy-done.1, bf16[1024,512]{1,0:T(8,128)(2,1)S(1)} %collective-permute-done.3.refs_1_.other_ref, bf16[128,512]{1,0:T(8,128)(2,1)S(1)} %get-tuple-element.64._.refs_0_), custom_call_target="tpu_custom_call" | custom-call | flops 1000000000 | bytes 3000000 | tf_op jit(solution)/shard_map/pallas_call | solution.py:156
  11.8 0.7 %shard_map.132.refs_9_.refs_5_ = bf16[512,2048]{1,0:T(8,128)(2,1)S(1)} custom-call(bf16[1024,512]{1,0:T(8,128)(2,1)S(1)} %copy-done, bf16[1024,512]{1,0:T(8,128)(2,1)S(1)} %collective-permute-done.2.refs_1_.other_ref, bf16[128,512]{1,0:T(8,128)(2,1)S(1)} %get-tuple-element.64._.refs_0_), custom_call_target="tpu_custom_call" | custom-call | flops 1000000000 | bytes 3000000 | tf_op jit(solution)/shard_map/pallas_call | solution.py:156
  13.1 4.2 %collective-permute-done.5.refs_2_ = bf16[128,512]{1,0:T(8,128)(2,1)S(1)} collective-permute-done((bf16[128,512]{1,0:T(8,128)(2,1)S(1)}, bf16[128,512]{1,0:T(8,128)(2,1)S(1)}, u32[]{:S(2)}, u32[]{:S(2)}) %collective-permute-start.5) | collective-permute-done | bytes 131104 | tf_op jit(solution)/shard_map/ppermute | solution.py:474
  17.2 1.0 %shard_map.133 = (bf16[128,512]{1,0:T(8,128)(2,1)S(1)}, bf16[128,512]{1,0:T(8,128)(2,1)S(1)}, bf16[128,512]{1,0:T(8,128)(2,1)S(1)}, bf16[128,512]{1,0:T(8,128)(2...) custom-call(bf16[128,512]{1,0:T(8,128)(2,1)S(1)} %get-tuple-element.64._.refs_0_, ...), custom_call_target="tpu_custom_call" | custom-call | flops 10000000 | bytes 30000 | tf_op jit(solution)/shard_map/pallas_call | solution.py:156
  18.3 1.3 %collective-permute-start.7 = (bf16[128,512]{1,0:T(8,128)(2,1)S(1)}, bf16[128,512]{1,0:T(8,128)(2,1)S(1)}, u32[]{:S(2)}, u32[]{:S(2)}) collective-permute-start(bf16[128,512]{1,0:T(8,128)(2,1)S(1)} %get-tuple-element.73), channel_id=1, source_target_pairs={{0,2},{1,3},{2,0},{3,1},{4,6},{5,7},{6,4},{7,5},{8,10},{9,11},{10,... | collective-permute-start | bytes 393224 | tf_op jit(solution)/shard_map/ppermute | solution.py:474
  19.6 0.8 %collective-permute-start.8 = (bf16[128,512]{1,0:T(8,128)(2,1)S(1)}, bf16[128,512]{1,0:T(8,128)(2,1)S(1)}, u32[]{:S(2)}, u32[]{:S(2)}) collective-permute-start(bf16[128,512]{1,0:T(8,128)(2,1)S(1)} %get-tuple-element.74), channel_id=1, source_target_pairs={{0,4},{1,5},{2,6},{3,7},{4,0},{5,1},{6,2},{7,3},{8,12},{9,13},{10,... | collective-permute-start | bytes 393224 | tf_op jit(solution)/shard_map/ppermute | solution.py:474
  20.4 1.4 %collective-permute-start.9 = (bf16[128,512]{1,0:T(8,128)(2,1)S(1)}, bf16[128,512]{1,0:T(8,128)(2,1)S(1)}, u32[]{:S(2)}, u32[]{:S(2)}) collective-permute-start(bf16[128,512]{1,0:T(8,128)(2,1)S(1)} %get-tuple-element.75), channel_id=1, source_target_pairs={{0,6},{1,7},{2,4},{3,5},{4,2},{5,3},{6,0},{7,1},{8,14},{9,15},{10,... | collective-permute-start | bytes 393224 | tf_op jit(solution)/shard_map/ppermute | solution.py:474
  22.1 2.7 %collective-permute-start.10 = (bf16[512,128]{1,0:T(8,128)(2,1)S(1)}, bf16[512,128]{1,0:T(8,128)(2,1)S(1)}, u32[]{:S(2)}, u32[]{:S(2)}) collective-permute-start(bf16[512,128]{1,0:T(8,128)(2,1)S(1)} %shard_map.134.refs_7_.refs_6_), channel_id=1, source_target_pairs={{0,16},{8,24},{16,0},{24,8},{1,17},{9,25},{17,1},{25,9},{2,18},{10... | collective-permute-start | bytes 393224 | tf_op jit(solution)/shard_map/ppermute | solution.py:571
  24.8 2.0 %collective-permute-done.8.refs_2_ = bf16[128,512]{1,0:T(8,128)(2,1)S(1)} collective-permute-done((bf16[128,512]{1,0:T(8,128)(2,1)S(1)}, bf16[128,512]{1,0:T(8,128)(2,1)S(1)}, u32[]{:S(2)}, u32[]{:S(2)}) %collective-permute-start.8) | collective-permute-done | bytes 131104 | tf_op jit(solution)/shard_map/ppermute | solution.py:474
  26.8 1.1 %shard_map.135 = (bf16[512,128]{1,0:T(8,128)(2,1)S(1)}, bf16[256,512]{1,0:T(8,128)(2,1)S(1)}, bf16[256,512]{1,0:T(8,128)(2,1)S(1)}) custom-call(bf16[128,512]{1,0:T(8,128)(2,1)S(1)} %get-tuple-element.72.refs_0_, bf16[128,512]{1,0:T(8,128)(2,1)S(1)} %collective-permute-done.7.refs_1_, bf16[128,512]{1,0:T(8,128)(2,1)S(1)} %collective-permute-done.8.refs_2_, ...), custom_call_target="tpu_custom_call" | custom-call | flops 10000000 | bytes 30000 | tf_op jit(solution)/shard_map/pallas_call | solution.py:156
  27.9 2.7 %collective-permute-start.13 = (bf16[512,128]{1,0:T(8,128)(2,1)S(1)}, bf16[512,128]{1,0:T(8,128)(2,1)S(1)}, u32[]{:S(2)}, u32[]{:S(2)}) collective-permute-start(bf16[512,128]{1,0:T(8,128)(2,1)S(1)} %get-tuple-element.91.left_ref), channel_id=1, source_target_pairs={{0,16},{8,24},{16,0},{24,8},{1,17},{9,25},{17,1},{25,9},{2,18},{10... | collective-permute-start | bytes 393224 | tf_op jit(solution)/shard_map/ppermute | solution.py:571
  30.5 1.3 %shard_map.136 = (f32[1024,512]{1,0:T(8,128)S(1)}, f32[1024,512]{1,0:T(8,128)S(1)}, bf16[2048,512]{1,0:T(8,128)(2,1)S(1)}, bf16[512,128]{1,0:T(8,128)(2,1)S(1)}) custom-call(bf16[256,512]{1,0:T(8,128)(2,1)S(1)} %get-tuple-element.79.refs_0_, bf16[1024,512]{1,0:T(8,128)(2,1)S(1)} %copy-done.1, bf16[256,128]{1,0:T(8,128)(2,1)S(1)} %get-tuple-element.59.refs_2_, ...), custom_call_target="tpu_custom_call" | custom-call | flops 10000000 | bytes 30000 | tf_op jit(solution)/shard_map/pallas_call | solution.py:156
  31.8 1.7 %collective-permute-start.12 = (bf16[512,128]{1,0:T(8,128)(2,1)S(1)}, bf16[512,128]{1,0:T(8,128)(2,1)S(1)}, u32[]{:S(2)}, u32[]{:S(2)}) collective-permute-start(bf16[512,128]{1,0:T(8,128)(2,1)S(1)} %get-tuple-element.85.sum_ref), channel_id=1, source_target_pairs={{0,8},{8,0},{16,24},{24,16},{1,9},{9,1},{17,25},{25,17},{2,10},{10... | collective-permute-start | bytes 393224 | tf_op jit(solution)/shard_map/ppermute | solution.py:571
  33.4 0.7 %collective-permute-done.13.right_ref = bf16[512,128]{1,0:T(8,128)(2,1)S(1)} collective-permute-done((bf16[512,128]{1,0:T(8,128)(2,1)S(1)}, bf16[512,128]{1,0:T(8,128)(2,1)S(1)}, u32[]{:S(2)}, u32[]{:S(2)}) %collective-permute-start.13) | collective-permute-done | bytes 131104 | tf_op jit(solution)/shard_map/ppermute | solution.py:571
  34.2 1.9 %collective-permute-start.15 = (bf16[256,128]{1,0:T(8,128)(2,1)S(1)}, bf16[256,128]{1,0:T(8,128)(2,1)S(1)}, u32[]{:S(2)}, u32[]{:S(2)}) collective-permute-start(bf16[256,128]{1,0:T(8,128)(2,1)S(1)} %get-tuple-element.95), channel_id=1, source_target_pairs={{0,8},{8,0},{16,24},{24,16},{1,9},{9,1},{17,25},{25,17},{2,10},{10... | collective-permute-start | bytes 196616 | tf_op jit(solution)/shard_map/ppermute | solution.py:571
  36.2 0.6 %collective-permute-done.12.got_ref = bf16[512,128]{1,0:T(8,128)(2,1)S(1)} collective-permute-done((bf16[512,128]{1,0:T(8,128)(2,1)S(1)}, bf16[512,128]{1,0:T(8,128)(2,1)S(1)}, u32[]{:S(2)}, u32[]{:S(2)}) %collective-permute-start.12) | collective-permute-done | bytes 131104 | tf_op jit(solution)/shard_map/ppermute | solution.py:571
  36.8 0.9 %shard_map.137 = (f32[256,128]{1,0:T(8,128)}, f32[256,128]{1,0:T(8,128)}, f32[8,128]{1,0:T(8,128)S(1)}) custom-call(bf16[512,128]{1,0:T(8,128)(2,1)S(1)} %get-tuple-element.85.sum_ref, bf16[512,128]{1,0:T(8,128)(2,1)S(1)} %collective-permute-done.12.got_ref, bf16[128,128]{1,0:T(8,128)(2,1)S(1)} %get-tuple-element.86.take_up_ref, ...), custom_call_target="tpu_custom_call" | custom-call | flops 28000000000 | bytes 84000000 | tf_op jit(solution)/shard_map/pallas_call | solution.py:156
  38.0 1.6 %shard_map.138 = (bf16[1024,512]{1,0:T(8,128)(2,1)}, bf16[1024,512]{1,0:T(8,128)(2,1)}, f32[8,128]{1,0:T(8,128)S(1)}) custom-call(f32[1024,512]{1,0:T(8,128)S(1)} %get-tuple-element.82.mixed_ref, f32[1024,512]{1,0:T(8,128)S(1)} %get-tuple-element.83.grad_ref, bf16[2048,512]{1,0:T(8,128)(2,1)S(1)} %collective-permute-done.11.got_ref, ...), custom_call_target="tpu_custom_call" | custom-call | flops 10000000 | bytes 30000 | tf_op jit(solution)/shard_map/pallas_call | solution.py:156
  39.6 0.6 %collective-permute-done.16.far_ref = bf16[256,128]{1,0:T(8,128)(2,1)S(1)} collective-permute-done((bf16[256,128]{1,0:T(8,128)(2,1)S(1)}, bf16[256,128]{1,0:T(8,128)(2,1)S(1)}, u32[]{:S(2)}, u32[]{:S(2)}) %collective-permute-start.16) | collective-permute-done | bytes 65568 | tf_op jit(solution)/shard_map/ppermute | solution.py:601
  40.2 0.9 %shard_map.141 = (f32[256,128]{1,0:T(8,128)}, f32[256,128]{1,0:T(8,128)}) custom-call(f32[512,128]{1,0:T(8,128)S(1)} %shard_map.140.chip_ref, bf16[256,128]{1,0:T(8,128)(2,1)S(1)} %collective-permute-done.15.near_ref, bf16[256,128]{1,0:T(8,128)(2,1)S(1)} %collective-permute-done.16.far_ref, bf16[256,256]{1,0:T(8,128)(2,1)S(1)} %get-tuple-element.94.place_ref, ...), custom_call_target="tpu_custom_call" | custom-call | flops 10000000 | bytes 30000 | tf_op jit(solution)/shard_map/pallas_call | solution.py:156
  (41 shorter events, 5.1 us)
Async XLA Ops:
  0.6 1.6 %collective-permute-start = (bf16[256,128]{1,0:T(8,128)(2,1)}, bf16[256,128]{1,0:T(8,128)(2,1)S(1)}, u32[]{:S(2)}, u32[]{:S(2)}) collective-permute-start(bf16[256,128]{1,0:T(8,128)(2,1)} %bitcast.10), channel_id=1, source_target_pairs={{0,1},{1,0},{2,3},{3,2},{4,5},{5,4},{6,7},{7,6},{8,9},{9,8},{10,11... | collective-permute-start | bytes 196616 | tf_op jit(solution)/shard_map/ppermute | solution.py:14
  1.1 3.0 %copy-start.1 = (bf16[1024,512]{1,0:T(8,128)(2,1)S(1)}, bf16[1024,512]{1,0:T(8,128)(2,1)}, u32[]{:S(2)}) copy-start(bf16[1024,512]{1,0:T(8,128)(2,1)} %refs_1_.1) | copy-start | bytes 3145732
  1.2 3.0 %copy-start.2 = (bf16[16,16,128]{2,1,0:T(8,128)(2,1)S(1)}, bf16[16,16,128]{2,1,0:T(8,128)(2,1)}, u32[]{:S(2)}) copy-start(bf16[16,16,128]{2,1,0:T(8,128)(2,1)} %param.10) | copy-start | bytes 196612
  1.2 3.0 %copy-start.3 = (bf16[16,16,128]{2,1,0:T(8,128)(2,1)S(1)}, bf16[16,16,128]{2,1,0:T(8,128)(2,1)}, u32[]{:S(2)}) copy-start(bf16[16,16,128]{2,1,0:T(8,128)(2,1)} %param.13) | copy-start | bytes 196612
  1.2 1.5 %collective-permute-start.1 = (bf16[256,128]{1,0:T(8,128)(2,1)}, bf16[256,128]{1,0:T(8,128)(2,1)S(1)}, u32[]{:S(2)}, u32[]{:S(2)}) collective-permute-start(bf16[256,128]{1,0:T(8,128)(2,1)} %bitcast.12), channel_id=1, source_target_pairs={{0,1},{1,0},{2,3},{3,2},{4,5},{5,4},{6,7},{7,6},{8,9},{9,8},{10,11... | collective-permute-start | bytes 196616 | tf_op jit(solution)/shard_map/ppermute | solution.py:14
  1.3 2.9 %collective-permute-start.3 = (bf16[1024,512]{1,0:T(8,128)(2,1)}, bf16[1024,512]{1,0:T(8,128)(2,1)S(1)}, u32[]{:S(2)}, u32[]{:S(2)}) collective-permute-start(bf16[1024,512]{1,0:T(8,128)(2,1)} %refs_1_.1), channel_id=1, source_target_pairs={{0,1},{1,0},{2,3},{3,2},{4,5},{5,4},{6,7},{7,6},{8,9},{9,8},{10,11... | collective-permute-start | bytes 3145736 | tf_op jit(solution)/shard_map/ppermute | solution.py:14
  2.6 3.0 %collective-permute-start.2 = (bf16[1024,512]{1,0:T(8,128)(2,1)}, bf16[1024,512]{1,0:T(8,128)(2,1)S(1)}, u32[]{:S(2)}, u32[]{:S(2)}) collective-permute-start(bf16[1024,512]{1,0:T(8,128)(2,1)} %refs_4_.1), channel_id=1, source_target_pairs={{0,1},{1,0},{2,3},{3,2},{4,5},{5,4},{6,7},{7,6},{8,9},{9,8},{10,11... | collective-permute-start | bytes 3145736 | tf_op jit(solution)/shard_map/ppermute | solution.py:14
  4.2 6.6 %copy-start.4 = (bf16[2,128,128]{2,1,0:T(8,128)(2,1)S(1)}, bf16[2,128,128]{2,1,0:T(8,128)(2,1)}, u32[]{:S(2)}) copy-start(bf16[2,128,128]{2,1,0:T(8,128)(2,1)} %param.11) | copy-start | bytes 196612
  4.2 6.5 %copy-start.5 = (bf16[2,128,128]{2,1,0:T(8,128)(2,1)S(1)}, bf16[2,128,128]{2,1,0:T(8,128)(2,1)}, u32[]{:S(2)}) copy-start(bf16[2,128,128]{2,1,0:T(8,128)(2,1)} %param.12) | copy-start | bytes 196612
  4.2 6.5 %copy-start.6 = (s32[128]{0:T(128)S(1)}, s32[128]{0:T(128)}, u32[]{:S(2)}) copy-start(s32[128]{0:T(128)} %param.14) | copy-start | bytes 1540
  4.2 6.5 %copy-start.7 = (s32[128]{0:T(128)S(1)}, s32[128]{0:T(128)}, u32[]{:S(2)}) copy-start(s32[128]{0:T(128)} %param.15) | copy-start | bytes 1540
  6.3 6.8 %collective-permute-start.4 = (bf16[128,512]{1,0:T(8,128)(2,1)S(1)}, bf16[128,512]{1,0:T(8,128)(2,1)S(1)}, u32[]{:S(2)}, u32[]{:S(2)}) collective-permute-start(bf16[128,512]{1,0:T(8,128)(2,1)S(1)} %get-tuple-element.65), channel_id=1, source_target_pairs={{0,2},{1,3},{2,0},{3,1},{4,6},{5,7},{6,4},{7,5},{8,10},{9,11},{10,... | collective-permute-start | bytes 393224 | tf_op jit(solution)/shard_map/ppermute | solution.py:474
  9.2 8.1 %collective-permute-start.5 = (bf16[128,512]{1,0:T(8,128)(2,1)S(1)}, bf16[128,512]{1,0:T(8,128)(2,1)S(1)}, u32[]{:S(2)}, u32[]{:S(2)}) collective-permute-start(bf16[128,512]{1,0:T(8,128)(2,1)S(1)} %get-tuple-element.66), channel_id=1, source_target_pairs={{0,4},{1,5},{2,6},{3,7},{4,0},{5,1},{6,2},{7,3},{8,12},{9,13},{10,... | collective-permute-start | bytes 393224 | tf_op jit(solution)/shard_map/ppermute | solution.py:474
  10.7 6.5 %collective-permute-start.6 = (bf16[128,512]{1,0:T(8,128)(2,1)S(1)}, bf16[128,512]{1,0:T(8,128)(2,1)S(1)}, u32[]{:S(2)}, u32[]{:S(2)}) collective-permute-start(bf16[128,512]{1,0:T(8,128)(2,1)S(1)} %get-tuple-element.67), channel_id=1, source_target_pairs={{0,6},{1,7},{2,4},{3,5},{4,2},{5,3},{6,0},{7,1},{8,14},{9,15},{10,... | collective-permute-start | bytes 393224 | tf_op jit(solution)/shard_map/ppermute | solution.py:474
  18.3 6.5 %collective-permute-start.7 = (bf16[128,512]{1,0:T(8,128)(2,1)S(1)}, bf16[128,512]{1,0:T(8,128)(2,1)S(1)}, u32[]{:S(2)}, u32[]{:S(2)}) collective-permute-start(bf16[128,512]{1,0:T(8,128)(2,1)S(1)} %get-tuple-element.73), channel_id=1, source_target_pairs={{0,2},{1,3},{2,0},{3,1},{4,6},{5,7},{6,4},{7,5},{8,10},{9,11},{10,... | collective-permute-start | bytes 393224 | tf_op jit(solution)/shard_map/ppermute | solution.py:474
  19.6 7.2 %collective-permute-start.8 = (bf16[128,512]{1,0:T(8,128)(2,1)S(1)}, bf16[128,512]{1,0:T(8,128)(2,1)S(1)}, u32[]{:S(2)}, u32[]{:S(2)}) collective-permute-start(bf16[128,512]{1,0:T(8,128)(2,1)S(1)} %get-tuple-element.74), channel_id=1, source_target_pairs={{0,4},{1,5},{2,6},{3,7},{4,0},{5,1},{6,2},{7,3},{8,12},{9,13},{10,... | collective-permute-start | bytes 393224 | tf_op jit(solution)/shard_map/ppermute | solution.py:474
  20.4 6.4 %collective-permute-start.9 = (bf16[128,512]{1,0:T(8,128)(2,1)S(1)}, bf16[128,512]{1,0:T(8,128)(2,1)S(1)}, u32[]{:S(2)}, u32[]{:S(2)}) collective-permute-start(bf16[128,512]{1,0:T(8,128)(2,1)S(1)} %get-tuple-element.75), channel_id=1, source_target_pairs={{0,6},{1,7},{2,4},{3,5},{4,2},{5,3},{6,0},{7,1},{8,14},{9,15},{10,... | collective-permute-start | bytes 393224 | tf_op jit(solution)/shard_map/ppermute | solution.py:474
  22.1 8.4 %collective-permute-start.10 = (bf16[512,128]{1,0:T(8,128)(2,1)S(1)}, bf16[512,128]{1,0:T(8,128)(2,1)S(1)}, u32[]{:S(2)}, u32[]{:S(2)}) collective-permute-start(bf16[512,128]{1,0:T(8,128)(2,1)S(1)} %shard_map.134.refs_7_.refs_6_), channel_id=1, source_target_pairs={{0,16},{8,24},{16,0},{24,8},{1,17},{9,25},{17,1},{25,9},{2,18},{10... | collective-permute-start | bytes 393224 | tf_op jit(solution)/shard_map/ppermute | solution.py:571
  27.9 6.3 %collective-permute-start.13 = (bf16[512,128]{1,0:T(8,128)(2,1)S(1)}, bf16[512,128]{1,0:T(8,128)(2,1)S(1)}, u32[]{:S(2)}, u32[]{:S(2)}) collective-permute-start(bf16[512,128]{1,0:T(8,128)(2,1)S(1)} %get-tuple-element.91.left_ref), channel_id=1, source_target_pairs={{0,16},{8,24},{16,0},{24,8},{1,17},{9,25},{17,1},{25,9},{2,18},{10... | collective-permute-start | bytes 393224 | tf_op jit(solution)/shard_map/ppermute | solution.py:571
  31.8 5.0 %collective-permute-start.12 = (bf16[512,128]{1,0:T(8,128)(2,1)S(1)}, bf16[512,128]{1,0:T(8,128)(2,1)S(1)}, u32[]{:S(2)}, u32[]{:S(2)}) collective-permute-start(bf16[512,128]{1,0:T(8,128)(2,1)S(1)} %get-tuple-element.85.sum_ref), channel_id=1, source_target_pairs={{0,8},{8,0},{16,24},{24,16},{1,9},{9,1},{17,25},{25,17},{2,10},{10... | collective-permute-start | bytes 393224 | tf_op jit(solution)/shard_map/ppermute | solution.py:571
  33.4 4.5 %collective-permute-start.11 = (bf16[2048,512]{1,0:T(8,128)(2,1)S(1)}, bf16[2048,512]{1,0:T(8,128)(2,1)S(1)}, u32[]{:S(2)}, u32[]{:S(2)}) collective-permute-start(bf16[2048,512]{1,0:T(8,128)(2,1)S(1)} %get-tuple-element.84), channel_id=1, source_target_pairs={{0,1},{1,0},{2,3},{3,2},{4,5},{5,4},{6,7},{7,6},{8,9},{9,8},{10,11... | collective-permute-start | bytes 6291464 | tf_op jit(solution)/shard_map/ppermute | solution.py:14
  34.2 3.6 %collective-permute-start.14 = (bf16[256,128]{1,0:T(8,128)(2,1)S(1)}, bf16[256,128]{1,0:T(8,128)(2,1)S(1)}, u32[]{:S(2)}, u32[]{:S(2)}) collective-permute-start(bf16[256,128]{1,0:T(8,128)(2,1)S(1)} %get-tuple-element.93), channel_id=1, source_target_pairs={{0,1},{1,0},{2,3},{3,2},{4,5},{5,4},{6,7},{7,6},{8,9},{9,8},{10,11... | collective-permute-start | bytes 196616 | tf_op jit(solution)/shard_map/ppermute | solution.py:14
  34.2 5.3 %collective-permute-start.15 = (bf16[256,128]{1,0:T(8,128)(2,1)S(1)}, bf16[256,128]{1,0:T(8,128)(2,1)S(1)}, u32[]{:S(2)}, u32[]{:S(2)}) collective-permute-start(bf16[256,128]{1,0:T(8,128)(2,1)S(1)} %get-tuple-element.95), channel_id=1, source_target_pairs={{0,8},{8,0},{16,24},{24,16},{1,9},{9,1},{17,25},{25,17},{2,10},{10... | collective-permute-start | bytes 196616 | tf_op jit(solution)/shard_map/ppermute | solution.py:571
  36.1 4.0 %collective-permute-start.16 = (bf16[256,128]{1,0:T(8,128)(2,1)S(1)}, bf16[256,128]{1,0:T(8,128)(2,1)S(1)}, u32[]{:S(2)}, u32[]{:S(2)}) collective-permute-start(bf16[256,128]{1,0:T(8,128)(2,1)S(1)} %get-tuple-element.96), channel_id=1, source_target_pairs={{0,9},{1,8},{2,11},{3,10},{4,13},{5,12},{6,15},{7,14},{8,1},{9,0},... | collective-permute-start | bytes 196616 | tf_op jit(solution)/shard_map/ppermute | solution.py:601
  (1 other events, 2.7 us)
